TPU v7x, 128 devices: a whole 4x4x4 slice. The times are simulated.
128 devices in a mesh: dp: 2 (over y_hi), seq: 8 (over x, y_lo), expert: 8 (over z, core).
Axes of the slice: x: 4, y: 4 (y_hi: 2, y_lo: 2; y = y_hi * 2 + y_lo), z: 4, core: 2. Of those that a mesh axis runs over, the one named last changes fastest.
Arguments:
- queries: bfloat16 [4, 4096, 4096], P('dp', 'seq', 'expert'), may hold values from -10 to 10
- keys: bfloat16 [4, 4096, 4096], P('dp', 'seq', 'expert'), may hold values from -10 to 10
- values: bfloat16 [4, 4096, 4096], P('dp', 'seq', 'expert'), may hold values from -6 to 6
- residual: bfloat16 [4, 4096, 4096], P('dp', ('seq', 'expert')), may hold values from -4 to 4
- out_weight: bfloat16 [4096, 4096], P('expert'), may hold values from -0.09375 to 0.09375
- norm_gain: float32 [4096], replicated, may hold values from 0.5 to 1.5
- routes: int32 [4, 4096, 2], P('dp', ('seq', 'expert')), may hold values from 0 to 63, all different within a row; in each aligned block of 64 rows (0 to 63, 64 to 127, ..., all dimensions but the last counted through in order) at most 3 rows name the same one
- route_weights: float32 [4, 4096, 2], P('dp', ('seq', 'expert')), may hold values from 0.2 to 1
- sample_flags: int32 [4], P('dp'), may hold values from 0 to 1, as said below
- cond_gate: float32 [2, 4096], replicated, may hold values from 0.5 to 1.5
- up_weight: bfloat16 [64, 4096, 512], P(('seq', 'expert')), may hold values from -0.09375 to 0.09375
- down_weight: bfloat16 [64, 512, 4096], P(('seq', 'expert')), may hold values from -0.25 to 0.25
- cotangent: bfloat16 [4, 4096, 4096], P('dp', ('seq', 'expert')), may hold values from -2 to 2
Outputs:
- block_out: bfloat16 [4, 4096, 4096], P('dp', ('seq', 'expert'))
- up_grad: bfloat16 [64, 4096, 512], P(('seq', 'expert'), None, 'dp')
- down_grad: bfloat16 [64, 512, 4096], P(('seq', 'expert'), 'dp')
Inputs may be any that keep to these rules, and one draw needn't show every extreme that they name: `routes`: in each aligned block of 64 tokens of a sample no expert is named by more than 3 route entries, and in some blocks one is named by exactly 3; the two experts of a token differ. `sample_flags`: half of the 4 samples carry each flag.
All inputs are finite; a program needn't handle non-finite values.
Results may differ from a plain program's by a relative error of at most 0.025.
Values may be sent and summed in bfloat16 or wider, within the bound.
No kernel may reach another device: no remote copies, remote signals or barrier semaphores. Data moves between devices by JAX's collectives and lax.ppermute only.
A program may use at most 192 MiB of HBM per device.

v0:
```python
import jax
import jax.numpy as jnp
from jax import lax
from jax.sharding import PartitionSpec as P

D = 4096
HEADS = 32
FF = 512


def gelu_pair(pre):
    cdf_part = 0.5 * (1.0 + lax.erf(pre * 0.7071067811865476))
    density = jnp.exp(-0.5 * pre * pre) * 0.3989422804014327
    return (pre * cdf_part, cdf_part + pre * density)


def body(
    queries,
    keys,
    values,
    residual,
    out_weight,
    norm_gain,
    routes,
    route_weights,
    sample_flags,
    cond_gate,
    up_weight,
    down_weight,
    cotangent,
):
    head_dim = D // HEADS
    samples, tok_seq, local_width = queries.shape
    local_heads = local_width // head_dim
    scale = head_dim ** (-0.5)
    query_heads = queries.reshape(samples, tok_seq, local_heads, head_dim)

    def attend_block(carry, key_rows, value_rows):
        running, total, accum = carry
        key_heads = key_rows.reshape(samples, -1, local_heads, head_dim)
        value_heads = value_rows.reshape(samples, -1, local_heads, head_dim)
        scores = (
            jnp.einsum(
                "bqhd,bkhd->bhqk", query_heads, key_heads, preferred_element_type=jnp.float32
            )
            * scale
        )
        newmax = jnp.maximum(running, jnp.max(scores, axis=-1))
        factor = jnp.exp(running - newmax)
        expo = jnp.exp(scores - newmax[:, :, :, None])
        total = total * factor + jnp.sum(expo, axis=-1)
        accum = accum * factor[:, :, :, None] + jnp.einsum(
            "bhqk,bkhd->bhqd",
            expo.astype(jnp.bfloat16),
            value_heads,
            preferred_element_type=jnp.float32,
        )
        return (newmax, total, accum)

    start_state = (
        jnp.full((samples, local_heads, tok_seq), -1e30, jnp.float32),
        jnp.zeros((samples, local_heads, tok_seq), jnp.float32),
        jnp.zeros((samples, local_heads, tok_seq, head_dim), jnp.float32),
    )
    carry = start_state
    key_rows = lax.all_gather(keys, "seq", axis=1, tiled=True)
    value_rows = lax.all_gather(values, "seq", axis=1, tiled=True)
    count = key_rows.shape[1]
    pieces = count // 1024
    key_split = key_rows.reshape(samples, pieces, 1024, local_width).transpose(1, 0, 2, 3)
    value_split = value_rows.reshape(samples, pieces, 1024, local_width).transpose(1, 0, 2, 3)

    def advance(state, pair):
        return (attend_block(state, pair[0], pair[1]), None)

    carry, unused = lax.scan(advance, carry, (key_split, value_split))
    running, total, accum = carry
    attended = (
        (accum / total[:, :, :, None])
        .transpose(2, 0, 1, 3)
        .reshape(tok_seq * samples, local_width)
        .astype(jnp.bfloat16)
    )
    owner_count = lax.axis_size("expert")
    projected = lax.psum_scatter(
        jnp.dot(attended, out_weight, preferred_element_type=jnp.float32)
        .astype(jnp.bfloat16)
        .astype(jnp.float32)
        .astype(jnp.bfloat16),
        "expert",
        scatter_dimension=0,
        tiled=True,
    ).astype(jnp.float32)
    tok_moe = projected.shape[0] // samples
    projected = projected.reshape(tok_moe, samples, D).transpose(1, 0, 2)
    stream = residual.astype(jnp.float32) + projected
    normed = (
        stream * lax.rsqrt(jnp.mean(stream * stream, axis=-1, keepdims=True) + 1e-06) * norm_gain
    ).astype(jnp.bfloat16)
    gate_vec = jnp.where((sample_flags == 1)[:, None], cond_gate[1][None, :], cond_gate[0][None, :])
    seq_count = lax.axis_size("seq")
    experts_all = seq_count * owner_count
    capacity = max(2, 3 * tok_moe // experts_all)
    slots = capacity * samples
    grad_rows = (
        (
            route_weights[:, :, :, None]
            * gate_vec[:, None, None, :]
            * cotangent.astype(jnp.float32)[:, :, None, :]
        )
        .astype(jnp.bfloat16)
        .reshape(samples, 2 * tok_moe, D)
    )
    entry_rows = jnp.broadcast_to(normed[:, :, None, :], (samples, tok_moe, 2, D)).reshape(
        samples, 2 * tok_moe, D
    )
    expert_ids = routes.reshape(samples, 2 * tok_moe)
    onehot = (
        expert_ids[:, :, None] == jnp.arange(experts_all, dtype=jnp.int32)[None, None, :]
    ).astype(jnp.int32)
    slot_index = jnp.sum((jnp.cumsum(onehot, axis=1) - onehot) * onehot, axis=2)
    target = expert_ids * capacity + slot_index
    placing = (
        target[:, None, :] == jnp.arange(experts_all * capacity, dtype=jnp.int32)[None, :, None]
    ).astype(jnp.bfloat16)
    send_rows = (
        jnp.einsum("bpj,bjd->pbd", placing, entry_rows, preferred_element_type=jnp.float32)
        .astype(jnp.bfloat16)
        .reshape(experts_all, slots, D)
    )
    send_grad = (
        jnp.einsum("bpj,bjd->pbd", placing, grad_rows, preferred_element_type=jnp.float32)
        .astype(jnp.bfloat16)
        .reshape(experts_all, slots, D)
    )
    up_local = up_weight[0]
    down_local = down_weight[0]
    inputs = (
        lax.all_to_all(send_rows, ("seq", "expert"), split_axis=0, concat_axis=0, tiled=True),
        lax.all_to_all(send_grad, ("seq", "expert"), split_axis=0, concat_axis=0, tiled=True),
    )
    pre = jnp.einsum("scd,df->scf", inputs[0], up_local, preferred_element_type=jnp.float32)
    act, slope = gelu_pair(pre)
    hidden = act.astype(jnp.bfloat16)
    produced = jnp.einsum(
        "scf,fd->scd", hidden, down_local, preferred_element_type=jnp.float32
    ).astype(jnp.bfloat16)
    back_grad = jnp.einsum("scd,fd->scf", inputs[1], down_local, preferred_element_type=jnp.float32)
    pre_grad = (back_grad * slope).astype(jnp.bfloat16)
    produced, hidden, pre_grad = (produced, hidden, pre_grad)
    returned = lax.all_to_all(produced, ("seq", "expert"), split_axis=0, concat_axis=0, tiled=True)
    returned, hidden, pre_grad, recv_rows, recv_grad = (
        returned,
        hidden,
        pre_grad,
        inputs[0],
        inputs[1],
    )
    sources = recv_rows.shape[0]
    hidden_split = hidden.reshape(sources, capacity, samples, FF)
    pre_grad_split = pre_grad.reshape(sources, capacity, samples, FF)
    rows_split = recv_rows.reshape(sources, capacity, samples, D)
    grad_split = recv_grad.reshape(sources, capacity, samples, D)
    down_parts = (
        jnp.einsum("scbf,scbd->bfd", hidden_split, grad_split, preferred_element_type=jnp.float32)
        .astype(jnp.bfloat16)
        .astype(jnp.float32)
    )
    up_parts = (
        jnp.einsum("scbd,scbf->bdf", rows_split, pre_grad_split, preferred_element_type=jnp.float32)
        .astype(jnp.bfloat16)
        .astype(jnp.float32)
    )
    up_sums, down_sums = (
        lax.psum_scatter(
            up_parts.astype(jnp.bfloat16), "dp", scatter_dimension=2, tiled=True
        ).astype(jnp.float32),
        lax.psum_scatter(
            down_parts.astype(jnp.bfloat16), "dp", scatter_dimension=1, tiled=True
        ).astype(jnp.float32),
    )
    up_total = jnp.sum(up_sums, axis=0).astype(jnp.bfloat16)
    down_total = jnp.sum(down_sums, axis=0).astype(jnp.bfloat16)
    gathered = jnp.einsum(
        "bpj,pbd->bjd",
        placing,
        returned.reshape(experts_all * capacity, samples, D),
        preferred_element_type=jnp.float32,
    ).reshape(samples, tok_moe, 2, D)
    mixture = jnp.sum(route_weights[:, :, :, None] * gathered, axis=2)
    block_out = (stream + gate_vec[:, None, :] * mixture).astype(jnp.bfloat16)
    return (block_out, up_total[None], down_total[None])


def solution(mesh):
    placed = (
        P("dp", "seq", "expert"),
        P("dp", "seq", "expert"),
        P("dp", "seq", "expert"),
        P("dp", ("seq", "expert"), None),
        P("expert", None),
        P(),
        P("dp", ("seq", "expert"), None),
        P("dp", ("seq", "expert"), None),
        P("dp"),
        P(),
        P(("seq", "expert"), None, None),
        P(("seq", "expert"), None, None),
        P("dp", ("seq", "expert"), None),
    )
    return jax.shard_map(
        body,
        mesh=mesh,
        in_specs=placed,
        out_specs=(
            P("dp", ("seq", "expert"), None),
            P(("seq", "expert"), None, "dp"),
            P(("seq", "expert"), "dp", None),
        ),
        check_vma=False,
    )
```

profile of v0, /device:TPU:1, one launch (start us, length us, event | category | flops | bytes accessed | tf_op | source)
XLA Modules:
  0.0 987.6 jit_solution(14557465171403108188)
XLA Ops:
  10.9 170.3 %all-gather.3.cloned.1.call-done = bf16[2,4096,512]{2,1,0:T(8,128)(2,1)} async-done(((bf16[2,512,512]{2,1,0:T(8,128)(2,1)}), bf16[2,4096,512]{2,1,0:T(8,128)(2,1)}) %all-gather.3.cloned.1.call-update) | async-done | bytes 8388624 | tf_op jit(solution)/shard_map/all_gather | solution.py:66
  181.2 175.4 %all-gather.5.cloned.1.call-done = bf16[2,4096,512]{2,1,0:T(8,128)(2,1)} async-done(((bf16[2,512,512]{2,1,0:T(8,128)(2,1)}), bf16[2,4096,512]{2,1,0:T(8,128)(2,1)}) %all-gather.5.cloned.1.call-update) | async-done | bytes 8388624 | tf_op jit(solution)/shard_map/all_gather | solution.py:67
  356.6 147.4 %while.15 = (s32[]{:T(128)}, f32[2,4,512]{2,1,0:T(4,128)S(1)}, f32[2,4,512]{2,1,0:T(4,128)S(1)}, f32[2,4,512,128]{3,2,1,0:T(8,128)}, bf16[4,2,1024,512]{3,2,0,1:...) while((s32[]{:T(128)}, f32[2,4,512]{2,1,0:T(4,128)S(1)}, ...), condition=%wide.region_3.4_spmd.clone, body=%wide.region_0.3_spmd.clone.sunk | while | flops 2182631424 | bytes 76808296 | solution.py:76
  363.0 9.7 bitcast_reduce_fusion.2
  372.7 8.5 fusion.64
  384.2 8.8 fusion.66
  399.4 9.7 bitcast_reduce_fusion.2
  409.2 8.5 fusion.64
  420.7 9.4 fusion.66
  436.4 9.7 bitcast_reduce_fusion.2
  446.2 8.5 fusion.64
  457.7 9.4 fusion.66
  473.4 9.7 bitcast_reduce_fusion.2
  483.1 8.5 fusion.64
  494.7 9.4 fusion.66
  507.0 6.9 convolution_convert_fusion
  519.4 6.1 mul.150
  535.4 13.3 %all-to-all-start.2 = ((bf16[64,6,4096]{2,1,0:T(8,128)(2,1)}), bf16[64,6,4096]{2,1,0:T(8,128)(2,1)}, u32[]{:S(2)}, u32[]{:S(2)}) async-start(bf16[64,6,4096]{2,1,0:T(8,128)(2,1)} %reshape.166), calls=%async_computation.3 | async-start | bytes 8388608 | tf_op jit(solution)/shard_map/all_to_all | solution.py:140
  548.8 67.6 %reduce-scatter.4.cloned.1.call-done = bf16[128,4096]{1,0:T(8,128)(2,1)} async-done(((bf16[1024,4096]{1,0:T(8,128)(2,1)}), bf16[128,4096]{1,0:T(8,128)(2,1)}) %reduce-scatter.4.cloned.1.call-update) | async-done | bytes 1048592 | tf_op jit(solution)/shard_map/reduce_scatter | solution.py:85
  636.2 8.3 reshape.162
  644.6 9.6 all-to-all-start
  654.4 5.6 copy.63
  660.0 46.0 %all-to-all-done = bf16[64,6,4096]{2,1,0:T(8,128)(2,1)} async-done(((bf16[64,6,4096]{2,1,0:T(8,128)(2,1)}), bf16[64,6,4096]{2,1,0:T(8,128)(2,1)}, u32[]{:S(2)}, u32[]{:S(2)}) %all-to-all-start) | async-done | bytes 3145760 | tf_op jit(solution)/shard_map/all_to_all | solution.py:139
  715.3 5.7 bitcast_convert_fusion.1
  721.3 7.6 bitcast_convert_fusion
  734.9 67.3 %all_to_all.15 = bf16[64,6,4096]{2,1,0:T(8,128)(2,1)} all-to-all(bf16[64,6,4096]{2,1,0:T(8,128)(2,1)S(1)} %copy.58), channel_id=1, replica_groups=mesh['dp'=2,'seq'=8,'expert'=8] {'seq','expert'}, dimensions={0} | all-to-all | bytes 6291456 | tf_op jit(solution)/shard_map/all_to_all | solution.py:151
  802.1 8.2 reshape.163
  810.3 7.7 fusion.19
  818.0 6.1 reshape.164
  824.1 8.9 multiply_reduce_fusion
  835.4 35.1 %reduce-scatter.6.cloned.1.call-done = bf16[2,4096,256]{2,1,0:T(8,128)(2,1)} async-done(((bf16[2,4096,512]{2,1,0:T(8,128)(2,1)}), bf16[2,4096,256]{2,1,0:T(8,128)(2,1)}) %reduce-scatter.6.cloned.1.call-update) | async-done | bytes 4194320 | tf_op jit(solution)/shard_map/reduce_scatter | solution.py:175
  875.4 100.2 %reduce-scatter.8.cloned.1.call-done = bf16[2,256,4096]{2,1,0:T(8,128)(2,1)} async-done(((bf16[2,512,4096]{2,1,0:T(8,128)(2,1)}), bf16[2,256,4096]{2,1,0:T(8,128)(2,1)}) %reduce-scatter.8.cloned.1.call-update) | async-done | bytes 4194320 | tf_op jit(solution)/shard_map/reduce_scatter | solution.py:178
  (95 shorter events, 107.4 us)
Async XLA Ops:
  7.2 174.1 %all-gather.3.cloned.1.call-start = ((), (), s32[]{:S(2)}) async-start(), calls=%async_computation.6 | async-start | bytes 9437184 | tf_op jit(solution)/shard_map/all_gather | solution.py:66
  7.9 348.7 %all-gather.5.cloned.1.call-start = ((), (), s32[]{:S(2)}) async-start(), calls=%async_computation.7 | async-start | bytes 9437184 | tf_op jit(solution)/shard_map/all_gather | solution.py:67
  8.6 607.7 %reduce-scatter.4.cloned.1.call-start = ((), (), s32[]{:S(2)}) async-start(), calls=%async_computation.8 | async-start | bytes 9437184 | tf_op jit(solution)/shard_map/reduce_scatter | solution.py:85
  504.0 2.9 copy-start.7
  513.9 0.7 copy-start.5
  513.9 1.2 copy-start.6
  513.9 1.5 copy-start.2
  519.4 6.2 copy-start.10
  519.4 6.3 copy-start.3
  535.4 109.2 %all-to-all-start.2 = ((bf16[64,6,4096]{2,1,0:T(8,128)(2,1)}), bf16[64,6,4096]{2,1,0:T(8,128)(2,1)}, u32[]{:S(2)}, u32[]{:S(2)}) async-start(bf16[64,6,4096]{2,1,0:T(8,128)(2,1)} %reshape.166), calls=%async_computation.3 | async-start | bytes 8388608 | tf_op jit(solution)/shard_map/all_to_all | solution.py:140
  548.8 70.0 %copy-start = (bf16[2,64,4096]{2,1,0:T(8,128)(2,1)S(1)}, bf16[2,64,4096]{2,1,0:T(8,128)(2,1)}, u32[]{:S(2)}) copy-start(bf16[2,64,4096]{2,1,0:T(8,128)(2,1)} %param.18) | copy-start | bytes 3145732
  548.8 71.2 %copy-start.4 = (f32[4096]{0:T(1024)S(1)}, f32[4096]{0:T(1024)}, u32[]{:S(2)}) copy-start(f32[4096]{0:T(1024)} %param.20) | copy-start | bytes 49156
  644.6 61.4 %all-to-all-start = ((bf16[64,6,4096]{2,1,0:T(8,128)(2,1)}), bf16[64,6,4096]{2,1,0:T(8,128)(2,1)}, u32[]{:S(2)}, u32[]{:S(2)}) async-start(bf16[64,6,4096]{2,1,0:T(8,128)(2,1)} %reshape.162), calls=%async_computation.1 | async-start | bytes 8388608 | tf_op jit(solution)/shard_map/all_to_all | solution.py:139
  654.2 216.3 %reduce-scatter.6.cloned.1.call-start = ((), (), s32[]{:S(2)}) async-start(), calls=%async_computation.9 | async-start | bytes 12582912 | tf_op jit(solution)/shard_map/reduce_scatter | solution.py:175
  706.0 4.1 copy-start.8
  710.0 2.6 copy-start.1
  710.0 3.3 copy-start.9
  721.0 254.6 %reduce-scatter.8.cloned.1.call-start = ((), (), s32[]{:S(2)}) async-start(), calls=%async_computation.10 | async-start | bytes 12582912 | tf_op jit(solution)/shard_map/reduce_scatter | solution.py:178
Sparse Core Ops, SparseCore 0:
  9.6 171.5 all-gather.2
  182.9 173.6 all-gather.4
  514.0 102.2 reduce-scatter.3
  721.1 149.3 reduce-scatter.5
  872.9 102.6 reduce-scatter.7
where the time goes:
time: 997 us; the launch traced here: 988 us
  waiting for transfers between devices  596 us (60%)
  matrix products  118 us (12%)
  local copies, waits for them, and re-layouts  108 us (11%)
  blocking collectives  67.3 us (7%)
  other arithmetic  60.5 us (6%)
  starting transfers between devices  23.5 us (2%)
  between operations  14.5 us (1%)
    all_gather x1, waiting for transfers between devices, body(): value_rows = lax.all_gather(values, 'seq', axis=1, tiled=True)  175 us
    all_gather x1, waiting for transfers between devices, body(): key_rows = lax.all_gather(keys, 'seq', axis=1, tiled=True)  170 us
    reduce_scatter x1, waiting for transfers between devices, body(): lax.psum_scatter(down_parts.astype(jnp.bfloat16), 'dp', scatter_dimension...  100 us
    reduce_scatter x1, waiting for transfers between devices, body(): lax.psum_scatter(jnp.dot(attended, out_weight, preferred_element_type=jnp...  67.6 us
    all_to_all x1, blocking collectives, body(): lax.all_to_all(produced, ('seq', 'expert'), split_axis=0, concat_axis=0,...  67.3 us
    all_to_all x1, waiting for transfers between devices, body(): lax.all_to_all(send_rows, ('seq', 'expert'), split_axis=0, concat_axis=0,...  46 us
    dot_general x4, matrix products, attend_block(): jnp.einsum('bqhd,bkhd->bhqk', query_heads, key_heads, preferred_element_t...  38.9 us
    dynamic_slice x12, local copies, waits for them, and re-layouts, body(): carry, unused = lax.scan(advance, carry, (key_split, value_split))  37.4 us
  transfers between devices with their start and end apart: 7, of which 6 were waited for; matrix products, arithmetic and copies ran while one was open for 11% of the time, Pallas kernels for 0%

commit v1 on v0

v1 whole, which is shorter than its diff:
```python
import functools

import jax
import jax.numpy as jnp
from jax import lax
from jax.experimental import pallas as pl
from jax.experimental.pallas import tpu as pltpu
from jax.sharding import Mesh
from jax.sharding import PartitionSpec as P

BF = jnp.bfloat16
F32 = jnp.float32
D = 4096
FF = 512
HEAD = 128
LENGTH = 4096
HALF = FF // 2
EXPERTS = 64
ROWS = 6
TOK = 128
SLOTS = EXPERTS * ROWS
CB = 4
CW = D // CB
GROUP = 8
GR = GROUP * ROWS
EXP_SCALE = HEAD**-0.5 * 1.4426950408889634
QB = 256
KB = 512
SEQ = ("x", "yl")
BACK = ("x", "yl", "core")
ALL = ("x", "yl", "z", "core")
VMEM_LIMIT = 56 * 1024 * 1024


def params(limit=VMEM_LIMIT):
    return pltpu.CompilerParams(vmem_limit_bytes=limit)


def whole(*shape):
    return pl.BlockSpec(shape, lambda *_: (0,) * len(shape))


def dot_nt(a, b):
    return lax.dot_general(a, b, (((1,), (1,)), ((), ())), preferred_element_type=F32)


def dot_tn(a, b):
    return lax.dot_general(a, b, (((0,), (0,)), ((), ())), preferred_element_type=F32)


def dot_nn(a, b):
    return jnp.dot(a, b, preferred_element_type=F32)


def pack(queries, keys, values):
    def kernel(q_ref, k_ref, v_ref, o_ref):
        o_ref[0, 0] = q_ref[0]
        o_ref[0, 1] = k_ref[0]
        o_ref[0, 2] = v_ref[0]

    spec = pl.BlockSpec((1, 512, HEAD), lambda b, h: (b, 0, h))
    return pl.pallas_call(
        kernel,
        grid=(2, 4),
        in_specs=[spec] * 3,
        out_specs=pl.BlockSpec((1, 3, 512, HEAD), lambda b, h: (b * 4 + h, 0, 0, 0)),
        out_shape=jax.ShapeDtypeStruct((8, 3, 512, HEAD), BF),
        compiler_params=params(),
        name="pack_heads",
    )(queries, keys, values)


def lane_tiles(value):
    return [value[:, j : j + 128] for j in range(0, value.shape[1], 128)]


def attend(rows):
    pieces = [slice(i, i + KB) for i in range(0, LENGTH, KB)]

    def scores_of(q, k, s_ref):
        top = None
        for cut in pieces:
            s = dot_nt(q, k[cut])
            s_ref[:, cut] = s
            high = functools.reduce(jnp.maximum, lane_tiles(s))
            top = high if top is None else jnp.maximum(top, high)
        return jnp.max(top, axis=-1, keepdims=True)

    def step(q_next, k, s_next, s_now, top_now, v):
        top = None
        out = None
        for cut in pieces:
            s = dot_nt(q_next, k[cut])
            p = jnp.exp2((s_now[:, cut] - top_now) * EXP_SCALE).astype(BF)
            s_next[:, cut] = s
            high = functools.reduce(jnp.maximum, lane_tiles(s))
            top = high if top is None else jnp.maximum(top, high)
            wide = jnp.concatenate([v[cut], jnp.ones((KB, HEAD), BF)], axis=1)
            part = dot_nn(p, wide)
            out = part if out is None else out + part
        return jnp.max(top, axis=-1, keepdims=True), out[:, :HEAD] / out[:, HEAD:]

    def kernel(q_ref, qn_ref, k_ref, v_ref, o_ref, sa_ref, sb_ref, top_ref):
        k = k_ref[:, 0].reshape(LENGTH, HEAD)
        v = v_ref[:, 0].reshape(LENGTH, HEAD)

        @pl.when(pl.program_id(0) == 0)
        def _():
            top_ref[...] = jnp.broadcast_to(scores_of(q_ref[0, 0, :QB], k, sa_ref), (QB, 128))

        top_a = top_ref[:, :1]
        top_b, out_a = step(q_ref[0, 0, QB:], k, sb_ref, sa_ref, top_a, v)
        top_n, out_b = step(qn_ref[0, 0], k, sa_ref, sb_ref, top_b, v)
        top_ref[...] = jnp.broadcast_to(top_n, (QB, 128))
        for base, out in ((0, out_a), (4, out_b)):
            for t in range(QB // 64):
                j = base + t
                o_ref[0, j % 2, j // 2] = out[64 * t : 64 * t + 64].astype(BF)

    def following(i):
        j = jnp.minimum(2 * i + 2, LENGTH // QB - 1)
        return (j // 2, 0, j % 2, 0)

    return pl.pallas_call(
        kernel,
        grid=(8,),
        in_specs=[
            pl.BlockSpec((1, 1, 512, HEAD), lambda i: (i, 0, 0, 0)),
            pl.BlockSpec((1, 1, QB, HEAD), following),
            pl.BlockSpec((8, 1, 512, HEAD), lambda i: (0, 1, 0, 0)),
            pl.BlockSpec((8, 1, 512, HEAD), lambda i: (0, 2, 0, 0)),
        ],
        out_specs=pl.BlockSpec((1, 2, 4, 64, HEAD), lambda i: (i, 0, 0, 0, 0)),
        out_shape=jax.ShapeDtypeStruct((8, 2, 4, 64, HEAD), BF),
        scratch_shapes=[
            pltpu.VMEM((QB, LENGTH), F32),
            pltpu.VMEM((QB, LENGTH), F32),
            pltpu.VMEM((QB, 128), F32),
        ],
        compiler_params=params(),
        cost_estimate=pl.CostEstimate(
            flops=4 * LENGTH * LENGTH * 256, bytes_accessed=4 << 20, transcendentals=LENGTH * LENGTH
        ),
        name="attend",
    )(rows, rows, rows, rows)


def project(place, heads, weight_own, weight_other):
    def kernel(place_ref, a_ref, wo_ref, ws_ref, fa, fb, ua, ub, da, db, own):
        core = place_ref[1]

        def side(c):
            return jnp.concatenate(
                [
                    jnp.concatenate([a_ref[b, h, c, 0] for h in range(4)], axis=1)
                    for b in range(2)
                ],
                axis=0,
            )

        lhs_own = side(core)
        lhs_other = side(1 - core)
        total = dot_nn(lhs_own, wo_ref[...]) + dot_nn(lhs_other, ws_ref[...])
        for number, refs in enumerate(((fa, fb), (ua, ub), (da, db))):

            @pl.when(pl.program_id(0) == number)
            def _(refs=refs):
                refs[0][...] = total[:, : D // 2].astype(BF)
                refs[1][...] = total[:, D // 2 :].astype(BF)

        @pl.when(pl.program_id(0) == 3)
        def _():
            own[...] = total.astype(BF)

    def chunk_index(r, place_ref):
        offset = jnp.where(r == 0, 2, jnp.where(r == 1, 1, jnp.where(r == 2, 3, 0)))
        return (0, 0, 0, lax.rem(place_ref[0] + offset, 4), 0, 0)

    half = jax.ShapeDtypeStruct((TOK, D // 2), BF)
    return pl.pallas_call(
        kernel,
        grid_spec=pltpu.PrefetchScalarGridSpec(
            num_scalar_prefetch=1,
            grid=(4,),
            in_specs=[
                pl.BlockSpec((2, 4, 2, 1, 64, HEAD), chunk_index),
                whole(FF, D),
                whole(FF, D),
            ],
            out_specs=[whole(TOK, D // 2)] * 6 + [whole(TOK, D)],
        ),
        out_shape=[half] * 6 + [jax.ShapeDtypeStruct((TOK, D), BF)],
        compiler_params=params(),
        cost_estimate=pl.CostEstimate(
            flops=2 * 512 * 1024 * D, bytes_accessed=13 << 20, transcendentals=0
        ),
        name="project",
    )(place, heads, weight_own, weight_other)


def source_of(d):
    return lax.rem(d, CB * ROWS) // ROWS * GR + d // (CB * ROWS) * ROWS + lax.rem(d, ROWS)


def mixer():
    n = CB * GR
    d = lax.broadcasted_iota(jnp.int32, (n, n), 0)
    s = lax.broadcasted_iota(jnp.int32, (n, n), 1)
    return (s == source_of(d)).astype(BF)


def unmixer():
    n = CB * GR
    s = lax.broadcasted_iota(jnp.int32, (n, n), 0)
    d = lax.broadcasted_iota(jnp.int32, (n, n), 1)
    return (s == source_of(d)).astype(BF)


def mix_out(sc_ref, o_ref):
    mat = mixer()
    for g in range(EXPERTS // GROUP):
        stack = jnp.concatenate([sc_ref[c, g * GR : (g + 1) * GR, :] for c in range(CB)], axis=0)
        o_ref[g * CB * GR : (g + 1) * CB * GR, :] = dot_nn(mat, stack).astype(BF)


def mix_in(i_ref, sc_ref):
    mat = unmixer()
    for g in range(EXPERTS // GROUP):
        stack = dot_nn(mat, i_ref[g * CB * GR : (g + 1) * CB * GR, :]).astype(BF)
        for c in range(CB):
            sc_ref[c, g * GR : (g + 1) * GR, :] = stack[c * GR : (c + 1) * GR]


def placing(tgt_ref, k):
    slot = lax.broadcasted_iota(jnp.int32, (SLOTS, TOK), 0)
    return slot == tgt_ref[k : k + 1, :]


def send_grads(cotangent, gate, target, weight):
    def kernel(cot_ref, gate_ref, tgt_ref, w_ref, o_ref, sc_ref):
        first, second = placing(tgt_ref, 0), placing(tgt_ref, 1)
        both = (first | second).astype(BF)
        w = jnp.sum(
            jnp.where(first, w_ref[0:1, :], 0.0) + jnp.where(second, w_ref[1:2, :], 0.0),
            axis=1,
            keepdims=True,
        )
        odd = lax.rem(lax.broadcasted_iota(jnp.int32, (SLOTS, 1), 0), 2) == 1
        for c in range(CB):
            cut = slice(c * CW, (c + 1) * CW)
            rows = dot_nn(both, cot_ref[:, cut])
            gates = jnp.where(odd, gate_ref[1:2, cut], gate_ref[0:1, cut])
            sc_ref[c] = (w * gates * rows).astype(BF)
        mix_out(sc_ref, o_ref)

    return pl.pallas_call(
        kernel,
        grid=(1,),
        in_specs=[whole(TOK, D), whole(2, D), whole(2, TOK), whole(2, TOK)],
        out_specs=whole(CB * SLOTS, CW),
        out_shape=jax.ShapeDtypeStruct((CB * SLOTS, CW), BF),
        scratch_shapes=[pltpu.VMEM((CB, SLOTS, CW), BF)],
        compiler_params=params(),
        name="send_grads",
    )(cotangent, gate, target, weight)


def norm_send(own, up_a, up_b, down_a, down_b, residual, gain, target):
    def kernel(own_ref, ua, ub, da, db, res_ref, gain_ref, tgt_ref, s_ref, o_ref, sc_ref):
        square = jnp.zeros((TOK, 1), F32)
        for half, first, second in ((0, ua, da), (1, ub, db)):
            cut = slice(half * D // 2, (half + 1) * D // 2)
            s = own_ref[:, cut].astype(F32) + first[...].astype(F32) + second[...].astype(F32)
            s = res_ref[:, cut].astype(F32) + s
            s_ref[:, cut] = s
            square += jnp.sum(s * s, axis=1, keepdims=True)
        factor = lax.rsqrt(square * (1.0 / D) + 1e-06)
        both = (placing(tgt_ref, 0) | placing(tgt_ref, 1)).astype(BF)
        for c in range(CB):
            cut = slice(c * CW, (c + 1) * CW)
            normed = (s_ref[:, cut] * factor * gain_ref[:, cut]).astype(BF)
            sc_ref[c] = dot_nn(both, normed).astype(BF)
        mix_out(sc_ref, o_ref)

    return pl.pallas_call(
        kernel,
        grid=(1,),
        in_specs=[whole(TOK, D)]
        + [whole(TOK, D // 2)] * 4
        + [whole(TOK, D), whole(1, D), whole(2, TOK)],
        out_specs=[whole(TOK, D), whole(CB * SLOTS, CW)],
        out_shape=[
            jax.ShapeDtypeStruct((TOK, D), F32),
            jax.ShapeDtypeStruct((CB * SLOTS, CW), BF),
        ],
        scratch_shapes=[pltpu.VMEM((CB, SLOTS, CW), BF)],
        compiler_params=params(),
        name="norm_send",
    )(own, up_a, up_b, down_a, down_b, residual, gain, target)


def grads_in(chunks, down):
    def kernel(i_ref, d_ref, g_ref, b_ref):
        mix_in(i_ref, g_ref)
        back = None
        for c in range(CB):
            part = dot_nt(g_ref[c], d_ref[:, c * CW : (c + 1) * CW])
            back = part if back is None else back + part
        b_ref[...] = back

    return pl.pallas_call(
        kernel,
        grid=(1,),
        in_specs=[whole(CB * SLOTS, CW), whole(FF, D)],
        out_specs=[whole(CB, SLOTS, CW), whole(SLOTS, FF)],
        out_shape=[
            jax.ShapeDtypeStruct((CB, SLOTS, CW), BF),
            jax.ShapeDtypeStruct((SLOTS, FF), F32),
        ],
        compiler_params=params(),
        name="grads_in",
    )(chunks, down)


def gelu_pair(pre):
    cdf_part = 0.5 * (1.0 + lax.erf(pre * 0.7071067811865476))
    density = jnp.exp(-0.5 * pre * pre) * 0.3989422804014327
    return (pre * cdf_part, cdf_part + pre * density)


def experts(place, chunks, up, down, back):
    def kernel(place_ref, i_ref, up_ref, down_ref, b_ref, x_ref, ho_ref, hs_ref, pg_ref, o_ref, pre, hid, prod):
        i = pl.program_id(0)

        @pl.when(i == 0)
        def _():
            mix_in(i_ref, x_ref)
            pre[...] = dot_nn(x_ref[0], up_ref[...])

        @pl.when((i > 0) & (i < CB))
        def _():
            pre[...] += dot_nn(x_ref[i], up_ref[...])

        @pl.when(i == CB - 1)
        def _():
            act, slope = gelu_pair(pre[...])
            hid[...] = act.astype(BF)
            pg_ref[...] = (b_ref[...] * slope).astype(BF)
            low, high = act[:, :HALF].astype(BF), act[:, HALF:].astype(BF)
            mine = place_ref[2] == 0
            hs_ref[...] = jnp.where(mine, low, high)
            ho_ref[...] = jnp.where(mine, high, low)

        @pl.when(i >= CB)
        def _():
            prod[i - CB] = dot_nn(hid[...], down_ref[...]).astype(BF)

        @pl.when(i == 2 * CB - 1)
        def _():
            mix_out(prod, o_ref)

    return pl.pallas_call(
        kernel,
        grid_spec=pltpu.PrefetchScalarGridSpec(
            num_scalar_prefetch=1,
            grid=(2 * CB,),
            in_specs=[
                whole(CB * SLOTS, CW),
                pl.BlockSpec((CW, FF), lambda i, _: (jnp.minimum(i, CB - 1), 0)),
                pl.BlockSpec((FF, CW), lambda i, _: (0, jnp.maximum(i - CB, 0))),
                whole(SLOTS, FF),
            ],
            out_specs=[
                whole(CB, SLOTS, CW),
                whole(SLOTS, HALF),
                whole(SLOTS, HALF),
                whole(SLOTS, FF),
                whole(CB * SLOTS, CW),
            ],
            scratch_shapes=[
                pltpu.VMEM((SLOTS, FF), F32),
                pltpu.VMEM((SLOTS, FF), BF),
                pltpu.VMEM((CB, SLOTS, CW), BF),
            ],
        ),
        out_shape=[
            jax.ShapeDtypeStruct((CB, SLOTS, CW), BF),
            jax.ShapeDtypeStruct((SLOTS, HALF), BF),
            jax.ShapeDtypeStruct((SLOTS, HALF), BF),
            jax.ShapeDtypeStruct((SLOTS, FF), BF),
            jax.ShapeDtypeStruct((CB * SLOTS, CW), BF),
        ],
        compiler_params=params(),
        name="experts",
    )(place, chunks, up, down, back)


def up_half(half, rows, pre_grad):
    def kernel(half_ref, x_ref, p_ref, o_ref):
        o_ref[...] = dot_tn(x_ref[0], p_ref[...]).astype(BF)

    return pl.pallas_call(
        kernel,
        grid_spec=pltpu.PrefetchScalarGridSpec(
            num_scalar_prefetch=1,
            grid=(CB,),
            in_specs=[
                pl.BlockSpec((1, SLOTS, CW), lambda c, _: (c, 0, 0)),
                pl.BlockSpec((SLOTS, HALF), lambda c, half_ref: (0, half_ref[0])),
            ],
            out_specs=pl.BlockSpec((CW, HALF), lambda c, _: (c, 0)),
        ),
        out_shape=jax.ShapeDtypeStruct((D, HALF), BF),
        compiler_params=params(),
        cost_estimate=pl.CostEstimate(
            flops=2 * SLOTS * D * HALF, bytes_accessed=6 << 20, transcendentals=0
        ),
        name="up_half",
    )(half, rows, pre_grad)


def down_sum(hidden, grads, hidden_far, grads_far):
    def kernel(h_ref, g_ref, hf_ref, gf_ref, o_ref):
        total = dot_tn(h_ref[...], g_ref[0]) + dot_tn(hf_ref[...], gf_ref[0])
        o_ref[...] = total.astype(BF)

    rows = pl.BlockSpec((1, SLOTS, CW), lambda c: (c, 0, 0))
    return pl.pallas_call(
        kernel,
        grid=(CB,),
        in_specs=[whole(SLOTS, HALF), rows, whole(SLOTS, HALF), rows],
        out_specs=pl.BlockSpec((HALF, CW), lambda c: (0, c)),
        out_shape=jax.ShapeDtypeStruct((HALF, D), BF),
        compiler_params=params(),
        cost_estimate=pl.CostEstimate(
            flops=4 * SLOTS * D * HALF, bytes_accessed=9 << 20, transcendentals=0
        ),
        name="down_sum",
    )(hidden, grads, hidden_far, grads_far)


def combine(chunks, stream, gate, target, weight):
    def kernel(i_ref, s_ref, gate_ref, tgt_ref, w_ref, o_ref, sc_ref):
        mix_in(i_ref, sc_ref)
        first, second = placing(tgt_ref, 0).astype(BF), placing(tgt_ref, 1).astype(BF)
        late = lax.broadcasted_iota(jnp.int32, (TOK, 1), 0) >= TOK // 2
        for c in range(CB):
            cut = slice(c * CW, (c + 1) * CW)
            mix = w_ref[:, 0:1] * dot_tn(first, sc_ref[c]) + w_ref[:, 1:2] * dot_tn(second, sc_ref[c])
            gates = jnp.where(late, gate_ref[1:2, cut], gate_ref[0:1, cut])
            o_ref[:, cut] = (s_ref[:, cut] + gates * mix).astype(BF)

    return pl.pallas_call(
        kernel,
        grid=(1,),
        in_specs=[whole(CB * SLOTS, CW), whole(TOK, D), whole(2, D), whole(2, TOK), whole(TOK, 2)],
        out_specs=whole(TOK, D),
        out_shape=jax.ShapeDtypeStruct((TOK, D), BF),
        scratch_shapes=[pltpu.VMEM((CB, SLOTS, CW), BF)],
        compiler_params=params(),
        name="combine",
    )(chunks, stream, gate, target, weight)


def plus(a, b):
    return (a.astype(F32) + b.astype(F32)).astype(BF)


def body(
    queries,
    keys,
    values,
    residual,
    out_weight,
    norm_gain,
    routes,
    route_weights,
    sample_flags,
    cond_gate,
    up_weight,
    down_weight,
    cotangent,
):
    z, core, dp = lax.axis_index("z"), lax.axis_index("core"), lax.axis_index("dp")
    place = jnp.stack([z, core, dp]).astype(jnp.int32)
    swap = [(0, 1), (1, 0)]
    above = [(i, (i + 1) % 4) for i in range(4)]
    below = [(i, (i + 3) % 4) for i in range(4)]
    exchange = functools.partial(lax.all_to_all, split_axis=0, concat_axis=0, tiled=True)

    ids = routes.reshape(2, TOK)
    earlier = jnp.arange(TOK)[:, None] > jnp.arange(TOK)[None, :]
    same = (ids[:, :, None] == ids[:, None, :]) & earlier[None]
    slot = jnp.sum(same.astype(jnp.int32), axis=2)
    row = ids * ROWS + slot * 2 + jnp.arange(2, dtype=jnp.int32)[:, None]
    target = row.reshape(TOK, 2).T
    weight_col = route_weights.reshape(TOK, 2)
    gate = jnp.where((sample_flags == 1)[:, None], cond_gate[1][None, :], cond_gate[0][None, :])

    rows = exchange(pack(queries, keys, values), SEQ)
    weight_other = lax.ppermute(out_weight, "core", swap)

    grad_chunks = send_grads(cotangent.reshape(TOK, D), gate, target, weight_col.T)
    rows, grad_chunks = lax.optimization_barrier((rows, grad_chunks))
    grad_arrived = exchange(grad_chunks, ALL)

    heads = attend(rows).reshape(16, 256, HEAD)
    heads = exchange(heads, BACK).reshape(2, 4, 2, 4, 64, HEAD)
    fa, fb, ua, ub, da, db, own = project(place, heads, out_weight, weight_other)
    fa = lax.ppermute(fa, "z", above)
    fb = lax.ppermute(fb, "z", below)
    ub = lax.ppermute(ub, "z", above)
    da = lax.ppermute(da, "z", below)
    ua = lax.ppermute(plus(ua, fa), "z", above)
    db = lax.ppermute(plus(db, fb), "z", below)
    stream, chunks = norm_send(
        own, ua, ub, da, db, residual.reshape(TOK, D), norm_gain[None], target
    )
    arrived = exchange(chunks, ALL)

    grads, back = grads_in(grad_arrived, down_weight[0])
    grads_far = lax.ppermute(grads, "dp", swap)

    own_rows, hid_other, hid_own, pre_grad, products = experts(
        place, arrived, up_weight[0], down_weight[0], back
    )
    returned = exchange(products, ALL)
    hid_far = lax.ppermute(hid_other, "dp", swap)
    up_other = up_half((1 - dp)[None].astype(jnp.int32), own_rows, pre_grad)
    up_far = lax.ppermute(up_other, "dp", swap)
    up_own = up_half(dp[None].astype(jnp.int32), own_rows, pre_grad)
    down_total = down_sum(hid_own, grads, hid_far, grads_far)
    block_out = combine(returned, stream, gate, target, weight_col)
    up_total = plus(up_own, up_far)
    return (block_out.reshape(2, TOK // 2, D), up_total[None], down_total[None])


def solution(mesh):
    fine = Mesh(mesh.devices.reshape(2, 4, 2, 4, 2), ("dp", "x", "yl", "z", "core"))
    expert = ("z", "core")
    tokens = P("dp", ALL, None)
    placed = (
        P("dp", SEQ, expert),
        P("dp", SEQ, expert),
        P("dp", SEQ, expert),
        tokens,
        P(expert, None),
        P(),
        tokens,
        tokens,
        P("dp"),
        P(),
        P(ALL, None, None),
        P(ALL, None, None),
        tokens,
    )
    return jax.shard_map(
        body,
        mesh=fine,
        in_specs=placed,
        out_specs=(tokens, P(ALL, None, "dp"), P(ALL, "dp", None)),
        check_vma=False,
    )
```

time: 997 us -> 411 us (0.41)
  waiting for transfers between devices: 596 us -> 228 us
  matrix products: 118 us -> 0 us
  local copies, waits for them, and re-layouts: 108 us -> 8.1 us
  Pallas kernels: 0 us -> 99.4 us
  other arithmetic: 60.5 us -> 7.94 us
  blocking collectives: 67.3 us -> 21.1 us
  starting transfers between devices: 23.5 us -> 44.6 us
  between operations: 14.5 us -> 0.83 us
    all_gather x2 -> x0, waiting for transfers between devices: 346 us -> none  [the longest x1 175 us: body(): value_rows = lax.all_gather(values, 'seq', axis=1, tiled=True)]
    reduce_scatter x3 -> x0, waiting for transfers between devices: 203 us -> none  [the longest x1 100 us: body(): lax.psum_scatter(down_parts.astype(jnp.bfloat16), 'dp', scatter_dimension...]
    ppermute x0 -> x10, waiting for transfers between devices: none -> 162 us  [the longest x1 114 us: body(): hid_far = lax.ppermute(hid_other, 'dp', swap)]
    dot_general x17 -> x0, matrix products: 118 us -> none  [the longest x4 38.9 us: attend_block(): jnp.einsum('bqhd,bkhd->bhqk', query_heads, key_heads, preferred_element_t...]
    pallas_call x0 -> x11, Pallas kernels: none -> 99.4 us  [the longest x1 25.9 us: attend(): pl.pallas_call(kernel, grid=(8,), in_specs=[pl.BlockSpec((1, 1, 512, HEAD...]
    reduce_sum x9 -> x1, other arithmetic: 54.3 us -> 0.18 us  [body(): slot = jnp.sum(same.astype(jnp.int32), axis=2)]
    all_to_all x1, blocking collectives: 67.3 us -> 21.1 us  [body(): heads = exchange(heads, BACK).reshape(2, 4, 2, 4, 64, HEAD)]
    dynamic_slice x12 -> x0, local copies, waits for them, and re-layouts: 37.4 us -> none  [body(): carry, unused = lax.scan(advance, carry, (key_split, value_split))]
  transfers between devices with their start and end apart: 7 -> 14, of which waited for: 6 -> 6; matrix products, arithmetic and copies ran while one was open for 11% -> 2% of each run, Pallas kernels for 0% -> 21%
where the time goes in v1:
time: 411 us; the launch traced here: 410 us
  waiting for transfers between devices  228 us (55%)
  Pallas kernels  99.4 us (24%)
  starting transfers between devices  44.6 us (11%)
  blocking collectives  21.1 us (5%)
  local copies, waits for them, and re-layouts  8.1 us (2%)
  other arithmetic  7.94 us (2%)
    ppermute x1, waiting for transfers between devices, body(): hid_far = lax.ppermute(hid_other, 'dp', swap)  114 us
    all_to_all x1, waiting for transfers between devices, body(): rows = exchange(pack(queries, keys, values), SEQ)  35.8 us
    all_to_all x1, waiting for transfers between devices, body(): arrived = exchange(chunks, ALL)  30.7 us
    ppermute x1, waiting for transfers between devices, body(): fa = lax.ppermute(fa, 'z', above)  30.4 us
    pallas_call x1, Pallas kernels, attend(): pl.pallas_call(kernel, grid=(8,), in_specs=[pl.BlockSpec((1, 1, 512, HEAD...  25.9 us
    all_to_all x1, blocking collectives, body(): heads = exchange(heads, BACK).reshape(2, 4, 2, 4, 64, HEAD)  21.1 us
    pallas_call x1, Pallas kernels, experts(): pl.pallas_call(kernel, grid_spec=pltpu.PrefetchScalarGridSpec(num_scalar_...  15.5 us
    pallas_call x1, Pallas kernels, project(): pl.pallas_call(kernel, grid_spec=pltpu.PrefetchScalarGridSpec(num_scalar_...  11.9 us
  transfers between devices with their start and end apart: 14, of which 6 were waited for; matrix products, arithmetic and copies ran while one was open for 2% of the time, Pallas kernels for 21%

profile of v1, /device:TPU:1, one launch (start us, length us, event | category | flops | bytes accessed | tf_op | source)
XLA Modules:
  0.0 410.0 jit_solution(7768280121816650338)
XLA Ops:
  0.6 6.3 %pack_heads.1 = bf16[8,3,512,128]{3,2,1,0:T(8,128)(2,1)} custom-call(bf16[2,512,512]{2,1,0:T(8,128)(2,1)} %q_ref.1, bf16[2,512,512]{2,1,0:T(8,128)(2,1)} %k_ref.1, bf16[2,512,512]{2,1,0:T(8,128)(2,1)} %v_ref.1), custom_call_target="tpu_custom_call" | custom-call | tf_op jit(solution)/shard_map/pack_heads/pallas_call | solution.py:62
  7.0 6.0 %all-to-all-start = ((bf16[8,3,512,128]{3,2,1,0:T(8,128)(2,1)}), bf16[8,3,512,128]{3,2,1,0:T(8,128)(2,1)S(1)}, u32[]{:S(2)}, u32[]{:S(2)}) async-start(bf16[8,3,512,128]{3,2,1,0:T(8,128)(2,1)} %pack_heads.1), calls=%async_computation | async-start | bytes 6291456 | tf_op jit(solution)/shard_map/all_to_all | solution.py:500
  16.9 5.1 %send_grads.1 = bf16[1536,1024]{1,0:T(8,128)(2,1)} custom-call(bf16[128,4096]{1,0:T(8,128)(2,1)} %bitcast.42, f32[2,4096]{1,0:T(2,128)} %broadcast_select_fusion.gate_ref, s32[2,128]{1,0:T(2,128)} %add_bitcast_fusion.tgt_ref, f32[2,128]{1,0:T(2,128)} %copy.28.w_ref), custom_call_target="tpu_custom_call" | custom-call | tf_op jit(solution)/shard_map/send_grads/pallas_call | solution.py:256
  21.9 35.8 %all-to-all-done.q_ref.qn_ref.k_ref.v_ref = bf16[8,3,512,128]{3,2,1,0:T(8,128)(2,1)S(1)} async-done(((bf16[8,3,512,128]{3,2,1,0:T(8,128)(2,1)}), bf16[8,3,512,128]{3,2,1,0:T(8,128)(2,1)S(1)}, u32[]{:S(2)}, u32[]{:S(2)}) %all-to-all-start) | async-done | bytes 3145760 | tf_op jit(solution)/shard_map/all_to_all | solution.py:500
  57.8 1.7 copy-done.3
  59.5 25.9 %attend.1 = bf16[8,2,4,64,128]{4,3,2,1,0:T(8,128)(2,1)} custom-call(bf16[8,3,512,128]{3,2,1,0:T(8,128)(2,1)} %copy-done.3, bf16[8,3,512,128]{3,2,1,0:T(8,128)(2,1)} %copy-done.3, bf16[8,3,512,128]{3,2,1,0:T(8,128)(2,1)} %copy-done.3, bf16[8,3,512,128]{3,2,1,0:T(8,128)(2,1)} %copy-done.3), custom_call_target="tpu_custom_call" | custom-call | flops 17179869184 | bytes 4194304 | tf_op jit(solution)/shard_map/attend/pallas_call | solution.py:124
  85.4 21.1 %all_to_all.43 = bf16[16,256,128]{2,1,0:T(8,128)(2,1)} all-to-all(bf16[16,256,128]{2,1,0:T(8,128)(2,1)} %bitcast.41), channel_id=1, replica_groups=mesh['dp'=2,'x'=4,'yl'=2,'z'=4,'core'=2] {'x','yl','core'}, dimensions={0} | all-to-all | bytes 2097152 | tf_op jit(solution)/shard_map/all_to_all | solution.py:508
  106.5 7.8 %all-to-all-start.3 = ((bf16[64,24,1024]{2,1,0:T(8,128)(2,1)}), bf16[64,24,1024]{2,1,0:T(8,128)(2,1)S(1)}, u32[]{:S(2)}, u32[]{:S(2)}) async-start(bf16[64,24,1024]{2,1,0:T(8,128)(2,1)} %bitcast.33), calls=%async_computation.3 | async-start | bytes 6291456 | tf_op jit(solution)/shard_map/all_to_all | solution.py:505
  115.0 11.9 %project.1 = (bf16[128,2048]{1,0:T(8,128)(2,1)}, bf16[128,2048]{1,0:T(8,128)(2,1)}, bf16[128,2048]{1,0:T(8,128)(2,1)}, bf16[128,2048]{1,0:T(8,128)(2,1)}, bf16[1...) custom-call(s32[3]{0:T(128)} %pad_add_fusion.place_ref, ...), custom_call_target="tpu_custom_call" | custom-call | flops 4294967296 | bytes 13631488 | tf_op jit(solution)/shard_map/project/pallas_call | solution.py:180
  126.9 1.4 collective-permute-start.1
  128.2 1.3 collective-permute-start.5
  129.7 2.5 collective-permute-start.4
  132.2 30.4 %collective-permute-done.1 = bf16[128,2048]{1,0:T(8,128)(2,1)S(1)} collective-permute-done((bf16[128,2048]{1,0:T(8,128)(2,1)}, bf16[128,2048]{1,0:T(8,128)(2,1)S(1)}, u32[]{:S(2)}, u32[]{:S(2)}) %collective-permute-start.1) | collective-permute-done | bytes 524320 | tf_op jit(solution)/shard_map/ppermute | solution.py:510
  165.1 2.9 collective-permute-start.6
  168.0 5.9 %collective-permute-done.3.ub = bf16[128,2048]{1,0:T(8,128)(2,1)S(1)} collective-permute-done((bf16[128,2048]{1,0:T(8,128)(2,1)}, bf16[128,2048]{1,0:T(8,128)(2,1)S(1)}, u32[]{:S(2)}, u32[]{:S(2)}) %collective-permute-start.3) | collective-permute-done | bytes 524320 | tf_op jit(solution)/shard_map/ppermute | solution.py:512
  173.9 11.2 %collective-permute-done.2.ua = bf16[128,2048]{1,0:T(8,128)(2,1)S(1)} collective-permute-done((bf16[128,2048]{1,0:T(8,128)(2,1)S(1)}, bf16[128,2048]{1,0:T(8,128)(2,1)S(1)}, u32[]{:S(2)}, u32[]{:S(2)}) %collective-permute-start.2) | collective-permute-done | bytes 524320 | tf_op jit(solution)/shard_map/ppermute | solution.py:514
  186.1 6.3 %norm_send.1 = (f32[128,4096]{1,0:T(8,128)}, bf16[1536,1024]{1,0:T(8,128)(2,1)}) custom-call(bf16[128,4096]{1,0:T(8,128)(2,1)} %get-tuple-element.22.own_ref, bf16[128,2048]{1,0:T(8,128)(2,1)} %copy-done.7, bf16[128,2048]{1,0:T(8,128)(2,1)} %copy-done.5, bf16[128,2048]{1,0:T(8,128)(2,1)} %copy-done.6, bf16[128,2048]{1,0:T(8,128)(2,1)} %copy-done.8, ...), custom_call_target="tpu_custom_call" | custom-call | tf_op jit(solution)/shard_map/norm_send/pallas_call | solution.py:285
  192.4 1.7 copy-done
  194.1 8.3 %all-to-all-start.2 = ((bf16[64,24,1024]{2,1,0:T(8,128)(2,1)}), bf16[64,24,1024]{2,1,0:T(8,128)(2,1)}, u32[]{:S(2)}, u32[]{:S(2)}) async-start(bf16[64,24,1024]{2,1,0:T(8,128)(2,1)} %bitcast.37), calls=%async_computation.2 | async-start | bytes 6291456 | tf_op jit(solution)/shard_map/all_to_all | solution.py:519
  202.4 6.7 %grads_in.1 = (bf16[4,384,1024]{2,1,0:T(8,128)(2,1)}, f32[384,512]{1,0:T(8,128)}) custom-call(bf16[1536,1024]{1,0:T(8,128)(2,1)} %bitcast.32, bf16[512,4096]{1,0:T(8,128)(2,1)} %bitcast.30), custom_call_target="tpu_custom_call" | custom-call | tf_op jit(solution)/shard_map/grads_in/pallas_call | solution.py:311
  209.1 2.6 collective-permute-start.9
  211.7 30.7 %all-to-all-done.2 = bf16[64,24,1024]{2,1,0:T(8,128)(2,1)} async-done(((bf16[64,24,1024]{2,1,0:T(8,128)(2,1)}), bf16[64,24,1024]{2,1,0:T(8,128)(2,1)}, u32[]{:S(2)}, u32[]{:S(2)}) %all-to-all-start.2) | async-done | bytes 3145760 | tf_op jit(solution)/shard_map/all_to_all | solution.py:519
  242.3 15.5 %experts.1 = (bf16[4,384,1024]{2,1,0:T(8,128)(2,1)}, bf16[384,256]{1,0:T(8,128)(2,1)}, bf16[384,256]{1,0:T(8,128)(2,1)}, bf16[384,512]{1,0:T(8,128)(2,1)}, bf16[1536,1024]{1,0:T(8,128)(2,1)}) custom-call(s32[3]{0:T(128)} %pad_add_fusion.place_ref, bf16[1536,1024]{1,0:T(8,128)(2,1)} %bitcast.14.i_ref, bf16[4096,512]{1,0:T(8,128)(2,1)} %bitcast.35, ...), custom_call_target="tpu_custom_call" | custom-call | tf_op jit(solution)/shard_map/experts/pallas_call | solution.py:362
  257.8 4.9 %up_half.3 = bf16[4096,256]{1,0:T(8,128)(2,1)} custom-call(s32[1]{0:T(128)} %bitcast.22.half_ref, bf16[4,384,1024]{2,1,0:T(8,128)(2,1)} %get-tuple-element.34.x_ref, bf16[384,512]{1,0:T(8,128)(2,1)} %get-tuple-element.35.p_ref), custom_call_target="tpu_custom_call" | custom-call | flops 805306368 | bytes 6291456 | tf_op jit(solution)/shard_map/up_half/pallas_call | solution.py:402
  262.7 2.6 collective-permute-start.7
  265.3 7.2 %all-to-all-start.4 = ((bf16[64,24,1024]{2,1,0:T(8,128)(2,1)}), bf16[64,24,1024]{2,1,0:T(8,128)(2,1)S(1)}, u32[]{:S(2)}, u32[]{:S(2)}) async-start(bf16[64,24,1024]{2,1,0:T(8,128)(2,1)} %bitcast.36), calls=%async_computation.4 | async-start | bytes 6291456 | tf_op jit(solution)/shard_map/all_to_all | solution.py:527
  273.3 4.9 %up_half.2 = bf16[4096,256]{1,0:T(8,128)(2,1)} custom-call(s32[1]{0:T(128)} %bitcast.2.half_ref, bf16[4,384,1024]{2,1,0:T(8,128)(2,1)} %get-tuple-element.34.x_ref, bf16[384,512]{1,0:T(8,128)(2,1)} %get-tuple-element.35.p_ref), custom_call_target="tpu_custom_call" | custom-call | flops 805306368 | bytes 6291456 | tf_op jit(solution)/shard_map/up_half/pallas_call | solution.py:402
  278.2 114.1 %collective-permute-done.8.hf_ref = bf16[384,256]{1,0:T(8,128)(2,1)S(1)} collective-permute-done((bf16[384,256]{1,0:T(8,128)(2,1)S(1)}, bf16[384,256]{1,0:T(8,128)(2,1)S(1)}, u32[]{:S(2)}, u32[]{:S(2)}) %collective-permute-start.8) | collective-permute-done | bytes 196640 | tf_op jit(solution)/shard_map/ppermute | solution.py:528
  393.0 6.3 %down_sum.1 = bf16[256,4096]{1,0:T(8,128)(2,1)} custom-call(bf16[384,256]{1,0:T(8,128)(2,1)} %get-tuple-element.36.h_ref, bf16[4,384,1024]{2,1,0:T(8,128)(2,1)} %get-tuple-element.37.g_ref, bf16[384,256]{1,0:T(8,128)(2,1)} %copy-done.9, bf16[4,384,1024]{2,1,0:T(8,128)(2,1)} %collective-permute-done.9.gf_ref), custom_call_target="tpu_custom_call" | custom-call | flops 1610612736 | bytes 9437184 | tf_op jit(solution)/shard_map/down_sum/pallas_call | solution.py:428
  399.3 3.4 fusion
  402.7 1.6 copy-done.1
  404.4 5.7 %combine.1 = bf16[128,4096]{1,0:T(8,128)(2,1)} custom-call(bf16[1536,1024]{1,0:T(8,128)(2,1)} %bitcast.34, f32[128,4096]{1,0:T(8,128)} %get-tuple-element.33.s_ref, f32[2,4096]{1,0:T(2,128)} %broadcast_select_fusion.gate_ref, s32[2,128]{1,0:T(2,128)} %add_bitcast_fusion.tgt_ref, f32[128,2]{1,0:T(8,128)} %bitcast.45), custom_call_target="tpu_custom_call" | custom-call | tf_op jit(solution)/shard_map/combine/pallas_call | solution.py:453
  (60 shorter events, 9.6 us)
Async XLA Ops:
  6.9 7.0 %copy-start.11 = (s32[2,64,2]{1,2,0:T(2,128)S(1)}, s32[2,64,2]{1,2,0:T(2,128)}, u32[]{:S(2)}) copy-start(s32[2,64,2]{1,2,0:T(2,128)} %param.19) | copy-start | bytes 3076
  6.9 8.4 %copy-start.10 = (f32[2,4096]{1,0:T(2,128)S(1)}, f32[2,4096]{1,0:T(2,128)}, u32[]{:S(2)}) copy-start(f32[2,4096]{1,0:T(2,128)} %param.22) | copy-start | bytes 98308
  6.9 8.5 %copy-start.14 = (s32[2]{0:T(128)S(1)}, s32[2]{0:T(128)}, u32[]{:S(2)}) copy-start(s32[2]{0:T(128)} %param.21) | copy-start | bytes 28
  6.9 8.5 %copy-start.12 = (f32[2,64,2]{1,2,0:T(2,128)S(1)}, f32[2,64,2]{1,2,0:T(2,128)}, u32[]{:S(2)}) copy-start(f32[2,64,2]{1,2,0:T(2,128)} %param.20) | copy-start | bytes 3076
  7.0 50.8 %all-to-all-start = ((bf16[8,3,512,128]{3,2,1,0:T(8,128)(2,1)}), bf16[8,3,512,128]{3,2,1,0:T(8,128)(2,1)S(1)}, u32[]{:S(2)}, u32[]{:S(2)}) async-start(bf16[8,3,512,128]{3,2,1,0:T(8,128)(2,1)} %pack_heads.1), calls=%async_computation | async-start | bytes 6291456 | tf_op jit(solution)/shard_map/all_to_all | solution.py:500
  13.0 102.0 %collective-permute-start = (bf16[512,4096]{1,0:T(8,128)(2,1)}, bf16[512,4096]{1,0:T(8,128)(2,1)}, u32[]{:S(2)}, u32[]{:S(2)}) collective-permute-start(bf16[512,4096]{1,0:T(8,128)(2,1)} %wo_ref.1), channel_id=1, source_target_pairs={{0,1},{1,0},{2,3},{3,2},{4,5},{5,4},{6,7},{7,6},{8,9},{9,8},{10,11... | collective-permute-start | bytes 12582920 | tf_op jit(solution)/shard_map/ppermute | solution.py:501
  15.5 69.9 %copy-start.4 = (f32[2,64,2]{2,1,0:T(8,128)}, f32[2,64,2]{2,1,0:T(8,128)S(1)}, u32[]{:S(2)}) copy-start(f32[2,64,2]{2,1,0:T(8,128)S(1)} %copy.27) | copy-start | bytes 3076
  57.8 1.7 copy-start.3
  106.5 85.9 %all-to-all-start.3 = ((bf16[64,24,1024]{2,1,0:T(8,128)(2,1)}), bf16[64,24,1024]{2,1,0:T(8,128)(2,1)S(1)}, u32[]{:S(2)}, u32[]{:S(2)}) async-start(bf16[64,24,1024]{2,1,0:T(8,128)(2,1)} %bitcast.33), calls=%async_computation.3 | async-start | bytes 6291456 | tf_op jit(solution)/shard_map/all_to_all | solution.py:505
  126.9 35.8 %collective-permute-start.1 = (bf16[128,2048]{1,0:T(8,128)(2,1)}, bf16[128,2048]{1,0:T(8,128)(2,1)S(1)}, u32[]{:S(2)}, u32[]{:S(2)}) collective-permute-start(bf16[128,2048]{1,0:T(8,128)(2,1)} %get-tuple-element.24), channel_id=1, source_target_pairs={{0,2},{2,4},{4,6},{6,0},{1,3},{3,5},{5,7},{7,1},{8,10},{10,12},{12... | collective-permute-start | bytes 1572872 | tf_op jit(solution)/shard_map/ppermute | solution.py:510
  128.2 35.6 %collective-permute-start.5 = (bf16[128,2048]{1,0:T(8,128)(2,1)}, bf16[128,2048]{1,0:T(8,128)(2,1)S(1)}, u32[]{:S(2)}, u32[]{:S(2)}) collective-permute-start(bf16[128,2048]{1,0:T(8,128)(2,1)} %get-tuple-element.28), channel_id=1, source_target_pairs={{0,6},{2,0},{4,2},{6,4},{1,7},{3,1},{5,3},{7,5},{8,14},{10,8},{12,... | collective-permute-start | bytes 1572872 | tf_op jit(solution)/shard_map/ppermute | solution.py:511
  129.5 44.3 %collective-permute-start.3 = (bf16[128,2048]{1,0:T(8,128)(2,1)}, bf16[128,2048]{1,0:T(8,128)(2,1)S(1)}, u32[]{:S(2)}, u32[]{:S(2)}) collective-permute-start(bf16[128,2048]{1,0:T(8,128)(2,1)} %get-tuple-element.25), channel_id=1, source_target_pairs={{0,2},{2,4},{4,6},{6,0},{1,3},{3,5},{5,7},{7,1},{8,10},{10,12},{12... | collective-permute-start | bytes 1572872 | tf_op jit(solution)/shard_map/ppermute | solution.py:512
  129.7 44.1 %collective-permute-start.4 = (bf16[128,2048]{1,0:T(8,128)(2,1)}, bf16[128,2048]{1,0:T(8,128)(2,1)S(1)}, u32[]{:S(2)}, u32[]{:S(2)}) collective-permute-start(bf16[128,2048]{1,0:T(8,128)(2,1)} %get-tuple-element.26), channel_id=1, source_target_pairs={{0,6},{2,0},{4,2},{6,4},{1,7},{3,1},{5,3},{7,5},{8,14},{10,8},{12,... | collective-permute-start | bytes 1572872 | tf_op jit(solution)/shard_map/ppermute | solution.py:513
  163.8 21.3 %collective-permute-start.2 = (bf16[128,2048]{1,0:T(8,128)(2,1)S(1)}, bf16[128,2048]{1,0:T(8,128)(2,1)S(1)}, u32[]{:S(2)}, u32[]{:S(2)}) collective-permute-start(bf16[128,2048]{1,0:T(8,128)(2,1)S(1)} %add_convert_fusion.2), channel_id=1, source_target_pairs={{0,2},{2,4},{4,6},{6,0},{1,3},{3,5},{5,7},{7,1},{8,10},{10,12},{12... | collective-permute-start | bytes 1572872 | tf_op jit(solution)/shard_map/ppermute | solution.py:514
  165.1 20.0 %collective-permute-start.6 = (bf16[128,2048]{1,0:T(8,128)(2,1)S(1)}, bf16[128,2048]{1,0:T(8,128)(2,1)S(1)}, u32[]{:S(2)}, u32[]{:S(2)}) collective-permute-start(bf16[128,2048]{1,0:T(8,128)(2,1)S(1)} %add_convert_fusion.1), channel_id=1, source_target_pairs={{0,6},{2,0},{4,2},{6,4},{1,7},{3,1},{5,3},{7,5},{8,14},{10,8},{12,... | collective-permute-start | bytes 1572872 | tf_op jit(solution)/shard_map/ppermute | solution.py:515
  173.9 11.2 %copy-start.5 = (bf16[128,2048]{1,0:T(8,128)(2,1)}, bf16[128,2048]{1,0:T(8,128)(2,1)S(1)}, u32[]{:S(2)}) copy-start(bf16[128,2048]{1,0:T(8,128)(2,1)S(1)} %collective-permute-done.3.ub) | copy-start | bytes 1572868
  173.9 11.2 %copy-start.6 = (bf16[128,2048]{1,0:T(8,128)(2,1)}, bf16[128,2048]{1,0:T(8,128)(2,1)S(1)}, u32[]{:S(2)}) copy-start(bf16[128,2048]{1,0:T(8,128)(2,1)S(1)} %collective-permute-done.4.da) | copy-start | bytes 1572868
  185.1 0.8 copy-start.7
  185.1 1.0 copy-start.8
  192.4 1.7 copy-start
  194.1 48.2 %all-to-all-start.2 = ((bf16[64,24,1024]{2,1,0:T(8,128)(2,1)}), bf16[64,24,1024]{2,1,0:T(8,128)(2,1)}, u32[]{:S(2)}, u32[]{:S(2)}) async-start(bf16[64,24,1024]{2,1,0:T(8,128)(2,1)} %bitcast.37), calls=%async_computation.2 | async-start | bytes 6291456 | tf_op jit(solution)/shard_map/all_to_all | solution.py:519
  209.1 183.2 %collective-permute-start.9 = (bf16[4,384,1024]{2,1,0:T(8,128)(2,1)}, bf16[4,384,1024]{2,1,0:T(8,128)(2,1)}, u32[]{:S(2)}, u32[]{:S(2)}) collective-permute-start(bf16[4,384,1024]{2,1,0:T(8,128)(2,1)} %get-tuple-element.37.g_ref), channel_id=1, source_target_pairs={{0,64},{64,0},{1,65},{65,1},{2,66},{66,2},{3,67},{67,3},{4,68},{68... | collective-permute-start | bytes 9437192 | tf_op jit(solution)/shard_map/ppermute | solution.py:522
  262.7 136.6 %collective-permute-start.7 = (bf16[4096,256]{1,0:T(8,128)(2,1)}, bf16[4096,256]{1,0:T(8,128)(2,1)}, u32[]{:S(2)}, u32[]{:S(2)}) collective-permute-start(bf16[4096,256]{1,0:T(8,128)(2,1)} %up_half.3), channel_id=1, source_target_pairs={{0,64},{64,0},{1,65},{65,1},{2,66},{66,2},{3,67},{67,3},{4,68},{68... | collective-permute-start | bytes 6291464 | tf_op jit(solution)/shard_map/ppermute | solution.py:530
  265.3 7.2 %copy-start.13 = (bf16[384,256]{1,0:T(8,128)(2,1)S(1)}, bf16[384,256]{1,0:T(8,128)(2,1)}, u32[]{:S(2)}) copy-start(bf16[384,256]{1,0:T(8,128)(2,1)} %get-tuple-element.38) | copy-start | bytes 589828
  265.3 137.4 %all-to-all-start.4 = ((bf16[64,24,1024]{2,1,0:T(8,128)(2,1)}), bf16[64,24,1024]{2,1,0:T(8,128)(2,1)S(1)}, u32[]{:S(2)}, u32[]{:S(2)}) async-start(bf16[64,24,1024]{2,1,0:T(8,128)(2,1)} %bitcast.36), calls=%async_computation.4 | async-start | bytes 6291456 | tf_op jit(solution)/shard_map/all_to_all | solution.py:527
  272.5 119.7 %collective-permute-start.8 = (bf16[384,256]{1,0:T(8,128)(2,1)S(1)}, bf16[384,256]{1,0:T(8,128)(2,1)S(1)}, u32[]{:S(2)}, u32[]{:S(2)}) collective-permute-start(bf16[384,256]{1,0:T(8,128)(2,1)S(1)} %copy-done.13), channel_id=1, source_target_pairs={{0,64},{64,0},{1,65},{65,1},{2,66},{66,2},{3,67},{67,3},{4,68},{68... | collective-permute-start | bytes 589832 | tf_op jit(solution)/shard_map/ppermute | solution.py:528
  392.3 0.7 copy-start.9
  393.0 6.3 %copy-start.2 = (bf16[4096,256]{1,0:T(8,128)(2,1)S(1)}, bf16[4096,256]{1,0:T(8,128)(2,1)}, u32[]{:S(2)}) copy-start(bf16[4096,256]{1,0:T(8,128)(2,1)} %up_half.2) | copy-start | bytes 6291460
  402.7 1.6 copy-start.1

commit v2 on v1

--- a/solution.py
+++ b/solution.py
@@ -145,54 +145,44 @@
     )(rows, rows, rows, rows)
 
 
-def project(place, heads, weight_own, weight_other):
-    def kernel(place_ref, a_ref, wo_ref, ws_ref, fa, fb, ua, ub, da, db, own):
+def project(place, half, heads, weight_own, weight_other):
+    width = 512
+    blocks = D // 2 // width
+
+    def kernel(place_ref, a_ref, wo_ref, ws_ref, *refs):
+        lhs = refs[-1]
         core = place_ref[1]
 
-        def side(c):
-            return jnp.concatenate(
-                [
-                    jnp.concatenate([a_ref[b, h, c, 0] for h in range(4)], axis=1)
-                    for b in range(2)
-                ],
-                axis=0,
-            )
-
-        lhs_own = side(core)
-        lhs_other = side(1 - core)
-        total = dot_nn(lhs_own, wo_ref[...]) + dot_nn(lhs_other, ws_ref[...])
-        for number, refs in enumerate(((fa, fb), (ua, ub), (da, db))):
-
-            @pl.when(pl.program_id(0) == number)
-            def _(refs=refs):
-                refs[0][...] = total[:, : D // 2].astype(BF)
-                refs[1][...] = total[:, D // 2 :].astype(BF)
-
-        @pl.when(pl.program_id(0) == 3)
-        def _():
-            own[...] = total.astype(BF)
-
-    def chunk_index(r, place_ref):
-        offset = jnp.where(r == 0, 2, jnp.where(r == 1, 1, jnp.where(r == 2, 3, 0)))
-        return (0, 0, 0, lax.rem(place_ref[0] + offset, 4), 0, 0)
-
-    half = jax.ShapeDtypeStruct((TOK, D // 2), BF)
+        @pl.when(pl.program_id(0) == 0)
+        def _():
+            for side, c in enumerate((core, 1 - core)):
+                for number, offset in enumerate((2, 1, 3, 0)):
+                    z = lax.rem(place_ref[0] + offset, 4)
+                    for b in range(2):
+                        for h in range(4):
+                            lhs[
+                                number * TOK + b * 64 : number * TOK + (b + 1) * 64,
+                                side * FF + h * HEAD : side * FF + (h + 1) * HEAD,
+                            ] = a_ref[b, h, c, z]
+
+        total = dot_nn(lhs[:, :FF], wo_ref[...]) + dot_nn(lhs[:, FF:], ws_ref[...])
+        for number in range(4):
+            refs[number][...] = total[number * TOK : (number + 1) * TOK].astype(BF)
+
+    weights = pl.BlockSpec((FF, width), lambda n, _: (0, half * blocks + n))
     return pl.pallas_call(
         kernel,
         grid_spec=pltpu.PrefetchScalarGridSpec(
             num_scalar_prefetch=1,
-            grid=(4,),
-            in_specs=[
-                pl.BlockSpec((2, 4, 2, 1, 64, HEAD), chunk_index),
-                whole(FF, D),
-                whole(FF, D),
-            ],
-            out_specs=[whole(TOK, D // 2)] * 6 + [whole(TOK, D)],
-        ),
-        out_shape=[half] * 6 + [jax.ShapeDtypeStruct((TOK, D), BF)],
+            grid=(blocks,),
+            in_specs=[whole(2, 4, 2, 4, 64, HEAD), weights, weights],
+            out_specs=[pl.BlockSpec((TOK, width), lambda n, _: (0, n))] * 4,
+            scratch_shapes=[pltpu.VMEM((4 * TOK, 2 * FF), BF)],
+        ),
+        out_shape=[jax.ShapeDtypeStruct((TOK, D // 2), BF)] * 4,
         compiler_params=params(),
         cost_estimate=pl.CostEstimate(
-            flops=2 * 512 * 1024 * D, bytes_accessed=13 << 20, transcendentals=0
+            flops=512 * 1024 * D, bytes_accessed=7 << 20, transcendentals=0
         ),
         name="project",
     )(place, heads, weight_own, weight_other)
@@ -265,12 +255,12 @@
     )(cotangent, gate, target, weight)
 
 
-def norm_send(own, up_a, up_b, down_a, down_b, residual, gain, target):
-    def kernel(own_ref, ua, ub, da, db, res_ref, gain_ref, tgt_ref, s_ref, o_ref, sc_ref):
+def norm_send(own_a, own_b, up_a, up_b, down_a, down_b, residual, gain, target):
+    def kernel(oa, ob, ua, ub, da, db, res_ref, gain_ref, tgt_ref, s_ref, o_ref, sc_ref):
         square = jnp.zeros((TOK, 1), F32)
-        for half, first, second in ((0, ua, da), (1, ub, db)):
+        for half, own, first, second in ((0, oa, ua, da), (1, ob, ub, db)):
             cut = slice(half * D // 2, (half + 1) * D // 2)
-            s = own_ref[:, cut].astype(F32) + first[...].astype(F32) + second[...].astype(F32)
+            s = own[...].astype(F32) + first[...].astype(F32) + second[...].astype(F32)
             s = res_ref[:, cut].astype(F32) + s
             s_ref[:, cut] = s
             square += jnp.sum(s * s, axis=1, keepdims=True)
@@ -285,8 +275,7 @@
     return pl.pallas_call(
         kernel,
         grid=(1,),
-        in_specs=[whole(TOK, D)]
-        + [whole(TOK, D // 2)] * 4
+        in_specs=[whole(TOK, D // 2)] * 6
         + [whole(TOK, D), whole(1, D), whole(2, TOK)],
         out_specs=[whole(TOK, D), whole(CB * SLOTS, CW)],
         out_shape=[
@@ -296,7 +285,7 @@
         scratch_shapes=[pltpu.VMEM((CB, SLOTS, CW), BF)],
         compiler_params=params(),
         name="norm_send",
-    )(own, up_a, up_b, down_a, down_b, residual, gain, target)
+    )(own_a, own_b, up_a, up_b, down_a, down_b, residual, gain, target)
 
 
 def grads_in(chunks, down):
@@ -505,27 +494,29 @@
     grad_arrived = exchange(grad_chunks, ALL)
 
     heads = attend(rows).reshape(16, 256, HEAD)
+    heads, grad_arrived = lax.optimization_barrier((heads, grad_arrived))
     heads = exchange(heads, BACK).reshape(2, 4, 2, 4, 64, HEAD)
-    fa, fb, ua, ub, da, db, own = project(place, heads, out_weight, weight_other)
+    grads, back = grads_in(grad_arrived, down_weight[0])
+    grads_far = lax.ppermute(grads, "dp", swap)
+    heads, grads, back = lax.optimization_barrier((heads, grads, back))
+    fa, ua, da, own_a = project(place, 0, heads, out_weight, weight_other)
     fa = lax.ppermute(fa, "z", above)
+    fb, ub, db, own_b = project(place, 1, heads, out_weight, weight_other)
     fb = lax.ppermute(fb, "z", below)
     ub = lax.ppermute(ub, "z", above)
     da = lax.ppermute(da, "z", below)
     ua = lax.ppermute(plus(ua, fa), "z", above)
     db = lax.ppermute(plus(db, fb), "z", below)
     stream, chunks = norm_send(
-        own, ua, ub, da, db, residual.reshape(TOK, D), norm_gain[None], target
+        own_a, own_b, ua, ub, da, db, residual.reshape(TOK, D), norm_gain[None], target
     )
     arrived = exchange(chunks, ALL)
-
-    grads, back = grads_in(grad_arrived, down_weight[0])
-    grads_far = lax.ppermute(grads, "dp", swap)
 
     own_rows, hid_other, hid_own, pre_grad, products = experts(
         place, arrived, up_weight[0], down_weight[0], back
     )
+    hid_far = lax.ppermute(hid_other, "dp", swap)
     returned = exchange(products, ALL)
-    hid_far = lax.ppermute(hid_other, "dp", swap)
     up_other = up_half((1 - dp)[None].astype(jnp.int32), own_rows, pre_grad)
     up_far = lax.ppermute(up_other, "dp", swap)
     up_own = up_half(dp[None].astype(jnp.int32), own_rows, pre_grad)

time: 411 us -> 403 us (0.981)
  blocking collectives: 21.1 us -> 0 us
  waiting for transfers between devices: 228 us -> 235 us
  starting transfers between devices: 44.6 us -> 50 us
    ppermute x1, waiting for transfers between devices: 114 us -> 57.5 us  [body(): hid_far = lax.ppermute(hid_other, 'dp', swap)]
    ppermute x1, waiting for transfers between devices: 0.01 us -> 55.1 us  [body(): grads_far = lax.ppermute(grads, 'dp', swap)]
    ppermute x1, waiting for transfers between devices: 30.4 us -> 1.76 us  [body(): fa = lax.ppermute(fa, 'z', above)]
    all_to_all x1 -> x0, blocking collectives: 21.1 us -> none  [body(): heads = exchange(heads, BACK).reshape(2, 4, 2, 4, 64, HEAD)]
    all_to_all x1, waiting for transfers between devices: 0.01 us -> 14 us  [body(): grad_arrived = exchange(grad_chunks, ALL)]
    all_to_all x0 -> x1, waiting for transfers between devices: none -> 8.64 us  [body(): heads = exchange(heads, BACK).reshape(2, 4, 2, 4, 64, HEAD)]
    all_to_all x1, waiting for transfers between devices: 30.7 us -> 37.3 us  [body(): arrived = exchange(chunks, ALL)]
    ppermute x1, waiting for transfers between devices: 0.01 us -> 6.46 us  [body(): db = lax.ppermute(plus(db, fb), 'z', below)]
  transfers between devices with their start and end apart: 14 -> 15, of which waited for: 6 -> 12; matrix products, arithmetic and copies ran while one was open for 2% -> 2% of each run, Pallas kernels for 21% -> 19%
where the time goes in v2:
time: 403 us; the launch traced here: 401 us
  waiting for transfers between devices  235 us (58%)
  Pallas kernels  101 us (25%)
  starting transfers between devices  50 us (12%)
  local copies, waits for them, and re-layouts  7.82 us (2%)
  other arithmetic  6.78 us (2%)
    ppermute x1, waiting for transfers between devices, body(): hid_far = lax.ppermute(hid_other, 'dp', swap)  57.5 us
    ppermute x1, waiting for transfers between devices, body(): grads_far = lax.ppermute(grads, 'dp', swap)  55.1 us
    all_to_all x1, waiting for transfers between devices, body(): arrived = exchange(chunks, ALL)  37.3 us
    all_to_all x1, waiting for transfers between devices, body(): rows = exchange(pack(queries, keys, values), SEQ)  35.8 us
    pallas_call x1, Pallas kernels, attend(): pl.pallas_call(kernel, grid=(8,), in_specs=[pl.BlockSpec((1, 1, 512, HEAD...  26 us
    pallas_call x1, Pallas kernels, experts(): pl.pallas_call(kernel, grid_spec=pltpu.PrefetchScalarGridSpec(num_scalar_...  15.4 us
    all_to_all x1, waiting for transfers between devices, body(): grad_arrived = exchange(grad_chunks, ALL)  14 us
    pallas_call x2, Pallas kernels, project(): pl.pallas_call(kernel, grid_spec=pltpu.PrefetchScalarGridSpec(num_scalar_...  13.4 us
  transfers between devices with their start and end apart: 15, of which 12 were waited for; matrix products, arithmetic and copies ran while one was open for 2% of the time, Pallas kernels for 19%

profile of v2, /device:TPU:1, one launch (start us, length us, event | category | flops | bytes accessed | tf_op | source)
XLA Modules:
  0.0 401.4 jit_solution(5232599088281096202)
XLA Ops:
  0.6 6.3 %pack_heads.1 = bf16[8,3,512,128]{3,2,1,0:T(8,128)(2,1)} custom-call(bf16[2,512,512]{2,1,0:T(8,128)(2,1)} %q_ref.1, bf16[2,512,512]{2,1,0:T(8,128)(2,1)} %k_ref.1, bf16[2,512,512]{2,1,0:T(8,128)(2,1)} %v_ref.1), custom_call_target="tpu_custom_call" | custom-call | tf_op jit(solution)/shard_map/pack_heads/pallas_call | solution.py:62
  6.9 6.0 %all-to-all-start = ((bf16[8,3,512,128]{3,2,1,0:T(8,128)(2,1)}), bf16[8,3,512,128]{3,2,1,0:T(8,128)(2,1)S(1)}, u32[]{:S(2)}, u32[]{:S(2)}) async-start(bf16[8,3,512,128]{3,2,1,0:T(8,128)(2,1)} %pack_heads.1), calls=%async_computation | async-start | bytes 6291456 | tf_op jit(solution)/shard_map/all_to_all | solution.py:489
  16.8 5.1 %send_grads.1 = bf16[1536,1024]{1,0:T(8,128)(2,1)} custom-call(bf16[128,4096]{1,0:T(8,128)(2,1)} %bitcast.42, f32[2,4096]{1,0:T(2,128)} %broadcast_select_fusion.gate_ref, s32[2,128]{1,0:T(2,128)} %add_bitcast_fusion.tgt_ref, f32[2,128]{1,0:T(2,128)} %copy.28.w_ref), custom_call_target="tpu_custom_call" | custom-call | tf_op jit(solution)/shard_map/send_grads/pallas_call | solution.py:246
  22.0 35.8 %all-to-all-done.q_ref.qn_ref.k_ref.v_ref = bf16[8,3,512,128]{3,2,1,0:T(8,128)(2,1)S(1)} async-done(((bf16[8,3,512,128]{3,2,1,0:T(8,128)(2,1)}), bf16[8,3,512,128]{3,2,1,0:T(8,128)(2,1)S(1)}, u32[]{:S(2)}, u32[]{:S(2)}) %all-to-all-start) | async-done | bytes 3145760 | tf_op jit(solution)/shard_map/all_to_all | solution.py:489
  59.3 8.1 %all-to-all-start.1 = ((bf16[64,24,1024]{2,1,0:T(8,128)(2,1)}), bf16[64,24,1024]{2,1,0:T(8,128)(2,1)S(1)}, u32[]{:S(2)}, u32[]{:S(2)}) async-start(bf16[64,24,1024]{2,1,0:T(8,128)(2,1)} %bitcast.35), calls=%async_computation.1 | async-start | bytes 6291456 | tf_op jit(solution)/shard_map/all_to_all | solution.py:494
  67.5 26.0 %attend.1 = bf16[8,2,4,64,128]{4,3,2,1,0:T(8,128)(2,1)} custom-call(bf16[8,3,512,128]{3,2,1,0:T(8,128)(2,1)} %copy-done.4, bf16[8,3,512,128]{3,2,1,0:T(8,128)(2,1)} %copy-done.4, bf16[8,3,512,128]{3,2,1,0:T(8,128)(2,1)} %copy-done.4, bf16[8,3,512,128]{3,2,1,0:T(8,128)(2,1)} %copy-done.4), custom_call_target="tpu_custom_call" | custom-call | flops 17179869184 | bytes 4194304 | tf_op jit(solution)/shard_map/attend/pallas_call | solution.py:124
  93.4 14.0 %all-to-all-done.1 = bf16[64,24,1024]{2,1,0:T(8,128)(2,1)S(1)} async-done(((bf16[64,24,1024]{2,1,0:T(8,128)(2,1)}), bf16[64,24,1024]{2,1,0:T(8,128)(2,1)S(1)}, u32[]{:S(2)}, u32[]{:S(2)}) %all-to-all-start.1) | async-done | bytes 3145760 | tf_op jit(solution)/shard_map/all_to_all | solution.py:494
  107.5 4.3 %all-to-all-start.2 = ((bf16[16,256,128]{2,1,0:T(8,128)(2,1)}), bf16[16,256,128]{2,1,0:T(8,128)(2,1)}, u32[]{:S(2)}, u32[]{:S(2)}) async-start(bf16[16,256,128]{2,1,0:T(8,128)(2,1)} %bitcast.41), calls=%async_computation.2 | async-start | bytes 2097152 | tf_op jit(solution)/shard_map/all_to_all | solution.py:498
  112.3 6.7 %grads_in.1 = (bf16[4,384,1024]{2,1,0:T(8,128)(2,1)}, f32[384,512]{1,0:T(8,128)}) custom-call(bf16[1536,1024]{1,0:T(8,128)(2,1)} %bitcast.32, bf16[512,4096]{1,0:T(8,128)(2,1)} %bitcast.30), custom_call_target="tpu_custom_call" | custom-call | tf_op jit(solution)/shard_map/grads_in/pallas_call | solution.py:300
  119.0 8.6 %all-to-all-done.2 = bf16[16,256,128]{2,1,0:T(8,128)(2,1)} async-done(((bf16[16,256,128]{2,1,0:T(8,128)(2,1)}), bf16[16,256,128]{2,1,0:T(8,128)(2,1)}, u32[]{:S(2)}, u32[]{:S(2)}) %all-to-all-start.2) | async-done | bytes 1048608 | tf_op jit(solution)/shard_map/all_to_all | solution.py:498
  127.7 6.7 %project.2 = (bf16[128,2048]{1,0:T(8,128)(2,1)}, bf16[128,2048]{1,0:T(8,128)(2,1)}, bf16[128,2048]{1,0:T(8,128)(2,1)}, bf16[128,2048]{1,0:T(8,128)(2,1)}) custom-call(s32[3]{0:T(128)} %pad_add_fusion.place_ref, bf16[2,4,2,4,64,128]{5,4,3,2,1,0:T(8,128)(2,1)} %bitcast.12.a_ref, bf16[512,4096]{1,0:T(8,128)(2,1)} %wo_ref.3, ...), custom_call_target="tpu_custom_call" | custom-call | flops 2147483648 | bytes 7340032 | tf_op jit(solution)/shard_map/project/pallas_call | solution.py:173
  135.5 6.7 %project.3 = (bf16[128,2048]{1,0:T(8,128)(2,1)}, bf16[128,2048]{1,0:T(8,128)(2,1)}, bf16[128,2048]{1,0:T(8,128)(2,1)}, bf16[128,2048]{1,0:T(8,128)(2,1)}) custom-call(s32[3]{0:T(128)} %pad_add_fusion.place_ref, bf16[2,4,2,4,64,128]{5,4,3,2,1,0:T(8,128)(2,1)} %bitcast.12.a_ref, bf16[512,4096]{1,0:T(8,128)(2,1)} %wo_ref.3, ...), custom_call_target="tpu_custom_call" | custom-call | flops 2147483648 | bytes 7340032 | tf_op jit(solution)/shard_map/project/pallas_call | solution.py:173
  144.0 2.7 collective-permute-start.4
  148.6 6.2 %collective-permute-done.5 = bf16[128,2048]{1,0:T(8,128)(2,1)S(1)} collective-permute-done((bf16[128,2048]{1,0:T(8,128)(2,1)}, bf16[128,2048]{1,0:T(8,128)(2,1)S(1)}, u32[]{:S(2)}, u32[]{:S(2)}) %collective-permute-start.5) | collective-permute-done | bytes 524320 | tf_op jit(solution)/shard_map/ppermute | solution.py:505
  156.0 2.8 collective-permute-start.6
  159.6 6.5 %collective-permute-done.4.da = bf16[128,2048]{1,0:T(8,128)(2,1)S(1)} collective-permute-done((bf16[128,2048]{1,0:T(8,128)(2,1)S(1)}, bf16[128,2048]{1,0:T(8,128)(2,1)S(1)}, u32[]{:S(2)}, u32[]{:S(2)}) %collective-permute-start.4) | collective-permute-done | bytes 524320 | tf_op jit(solution)/shard_map/ppermute | solution.py:507
  166.1 4.8 %collective-permute-done.2.ua = bf16[128,2048]{1,0:T(8,128)(2,1)S(1)} collective-permute-done((bf16[128,2048]{1,0:T(8,128)(2,1)S(1)}, bf16[128,2048]{1,0:T(8,128)(2,1)S(1)}, u32[]{:S(2)}, u32[]{:S(2)}) %collective-permute-start.2) | collective-permute-done | bytes 524320 | tf_op jit(solution)/shard_map/ppermute | solution.py:508
  170.9 6.5 %collective-permute-done.6.db = bf16[128,2048]{1,0:T(8,128)(2,1)S(1)} collective-permute-done((bf16[128,2048]{1,0:T(8,128)(2,1)S(1)}, bf16[128,2048]{1,0:T(8,128)(2,1)S(1)}, u32[]{:S(2)}, u32[]{:S(2)}) %collective-permute-start.6) | collective-permute-done | bytes 524320 | tf_op jit(solution)/shard_map/ppermute | solution.py:509
  178.1 6.5 %norm_send.1 = (f32[128,4096]{1,0:T(8,128)}, bf16[1536,1024]{1,0:T(8,128)(2,1)}) custom-call(bf16[128,2048]{1,0:T(8,128)(2,1)} %get-tuple-element.34.oa, bf16[128,2048]{1,0:T(8,128)(2,1)} %get-tuple-element.35.ob, bf16[128,2048]{1,0:T(8,128)(2,1)} %copy-done.8, bf16[128,2048]{1,0:T(8,128)(2,1)} %copy-done.6, bf16[128,2048]{1,0:T(8,128)(2,1)} %copy-done.7, ...), custom_call_target="tpu_custom_call" | custom-call | tf_op jit(solution)/shard_map/norm_send/pallas_call | solution.py:275
  184.6 8.8 %all-to-all-start.3 = ((bf16[64,24,1024]{2,1,0:T(8,128)(2,1)}), bf16[64,24,1024]{2,1,0:T(8,128)(2,1)S(1)}, u32[]{:S(2)}, u32[]{:S(2)}) async-start(bf16[64,24,1024]{2,1,0:T(8,128)(2,1)} %bitcast.38), calls=%async_computation.3 | async-start | bytes 6291456 | tf_op jit(solution)/shard_map/all_to_all | solution.py:513
  193.4 2.7 collective-permute-start.9
  196.1 37.3 %all-to-all-done.3 = bf16[64,24,1024]{2,1,0:T(8,128)(2,1)S(1)} async-done(((bf16[64,24,1024]{2,1,0:T(8,128)(2,1)}), bf16[64,24,1024]{2,1,0:T(8,128)(2,1)S(1)}, u32[]{:S(2)}, u32[]{:S(2)}) %all-to-all-start.3) | async-done | bytes 3145760 | tf_op jit(solution)/shard_map/all_to_all | solution.py:513
  235.1 15.4 %experts.1 = (bf16[4,384,1024]{2,1,0:T(8,128)(2,1)}, bf16[384,256]{1,0:T(8,128)(2,1)}, bf16[384,256]{1,0:T(8,128)(2,1)}, bf16[384,512]{1,0:T(8,128)(2,1)}, bf16[1536,1024]{1,0:T(8,128)(2,1)}) custom-call(s32[3]{0:T(128)} %pad_add_fusion.place_ref, bf16[1536,1024]{1,0:T(8,128)(2,1)} %bitcast.34, bf16[4096,512]{1,0:T(8,128)(2,1)} %bitcast.36, ...), custom_call_target="tpu_custom_call" | custom-call | tf_op jit(solution)/shard_map/experts/pallas_call | solution.py:351
  250.5 4.9 %up_half.3 = bf16[4096,256]{1,0:T(8,128)(2,1)} custom-call(s32[1]{0:T(128)} %bitcast.22.half_ref, bf16[4,384,1024]{2,1,0:T(8,128)(2,1)} %get-tuple-element.46.x_ref, bf16[384,512]{1,0:T(8,128)(2,1)} %get-tuple-element.47.p_ref), custom_call_target="tpu_custom_call" | custom-call | flops 805306368 | bytes 6291456 | tf_op jit(solution)/shard_map/up_half/pallas_call | solution.py:391
  255.4 2.6 collective-permute-start.7
  258.0 7.3 %all-to-all-start.4 = ((bf16[64,24,1024]{2,1,0:T(8,128)(2,1)}), bf16[64,24,1024]{2,1,0:T(8,128)(2,1)S(1)}, u32[]{:S(2)}, u32[]{:S(2)}) async-start(bf16[64,24,1024]{2,1,0:T(8,128)(2,1)} %bitcast.37), calls=%async_computation.4 | async-start | bytes 6291456 | tf_op jit(solution)/shard_map/all_to_all | solution.py:519
  266.1 4.9 %up_half.2 = bf16[4096,256]{1,0:T(8,128)(2,1)} custom-call(s32[1]{0:T(128)} %bitcast.2.half_ref, bf16[4,384,1024]{2,1,0:T(8,128)(2,1)} %get-tuple-element.46.x_ref, bf16[384,512]{1,0:T(8,128)(2,1)} %get-tuple-element.47.p_ref), custom_call_target="tpu_custom_call" | custom-call | flops 805306368 | bytes 6291456 | tf_op jit(solution)/shard_map/up_half/pallas_call | solution.py:391
  271.0 55.1 %collective-permute-done.9.gf_ref = bf16[4,384,1024]{2,1,0:T(8,128)(2,1)} collective-permute-done((bf16[4,384,1024]{2,1,0:T(8,128)(2,1)}, bf16[4,384,1024]{2,1,0:T(8,128)(2,1)}, u32[]{:S(2)}, u32[]{:S(2)}) %collective-permute-start.9) | collective-permute-done | bytes 3145760 | tf_op jit(solution)/shard_map/ppermute | solution.py:500
  326.1 57.5 %collective-permute-done.8.hf_ref = bf16[384,256]{1,0:T(8,128)(2,1)S(1)} collective-permute-done((bf16[384,256]{1,0:T(8,128)(2,1)S(1)}, bf16[384,256]{1,0:T(8,128)(2,1)S(1)}, u32[]{:S(2)}, u32[]{:S(2)}) %collective-permute-start.8) | collective-permute-done | bytes 196640 | tf_op jit(solution)/shard_map/ppermute | solution.py:518
  384.3 6.3 %down_sum.1 = bf16[256,4096]{1,0:T(8,128)(2,1)} custom-call(bf16[384,256]{1,0:T(8,128)(2,1)} %get-tuple-element.48.h_ref, bf16[4,384,1024]{2,1,0:T(8,128)(2,1)} %get-tuple-element.49.g_ref, bf16[384,256]{1,0:T(8,128)(2,1)} %copy-done.11, bf16[4,384,1024]{2,1,0:T(8,128)(2,1)} %collective-permute-done.9.gf_ref), custom_call_target="tpu_custom_call" | custom-call | flops 1610612736 | bytes 9437184 | tf_op jit(solution)/shard_map/down_sum/pallas_call | solution.py:417
  390.6 3.4 fusion
  395.7 5.7 %combine.1 = bf16[128,4096]{1,0:T(8,128)(2,1)} custom-call(bf16[1536,1024]{1,0:T(8,128)(2,1)} %bitcast.33, f32[128,4096]{1,0:T(8,128)} %get-tuple-element.45.s_ref, f32[2,4096]{1,0:T(2,128)} %broadcast_select_fusion.gate_ref, s32[2,128]{1,0:T(2,128)} %add_bitcast_fusion.tgt_ref, f32[128,2]{1,0:T(8,128)} %bitcast.45), custom_call_target="tpu_custom_call" | custom-call | tf_op jit(solution)/shard_map/combine/pallas_call | solution.py:442
  (68 shorter events, 18.4 us)
Async XLA Ops:
  6.9 7.0 %copy-start.13 = (s32[2,64,2]{1,2,0:T(2,128)S(1)}, s32[2,64,2]{1,2,0:T(2,128)}, u32[]{:S(2)}) copy-start(s32[2,64,2]{1,2,0:T(2,128)} %param.19) | copy-start | bytes 3076
  6.9 7.8 %copy-start.14 = (f32[2,64,2]{1,2,0:T(2,128)S(1)}, f32[2,64,2]{1,2,0:T(2,128)}, u32[]{:S(2)}) copy-start(f32[2,64,2]{1,2,0:T(2,128)} %param.20) | copy-start | bytes 3076
  6.9 8.6 %copy-start.17 = (s32[2]{0:T(128)S(1)}, s32[2]{0:T(128)}, u32[]{:S(2)}) copy-start(s32[2]{0:T(128)} %param.21) | copy-start | bytes 28
  6.9 8.6 %copy-start.12 = (f32[2,4096]{1,0:T(2,128)S(1)}, f32[2,4096]{1,0:T(2,128)}, u32[]{:S(2)}) copy-start(f32[2,4096]{1,0:T(2,128)} %param.22) | copy-start | bytes 98308
  6.9 50.8 %all-to-all-start = ((bf16[8,3,512,128]{3,2,1,0:T(8,128)(2,1)}), bf16[8,3,512,128]{3,2,1,0:T(8,128)(2,1)S(1)}, u32[]{:S(2)}, u32[]{:S(2)}) async-start(bf16[8,3,512,128]{3,2,1,0:T(8,128)(2,1)} %pack_heads.1), calls=%async_computation | async-start | bytes 6291456 | tf_op jit(solution)/shard_map/all_to_all | solution.py:489
  12.9 114.7 %collective-permute-start = (bf16[512,4096]{1,0:T(8,128)(2,1)}, bf16[512,4096]{1,0:T(8,128)(2,1)}, u32[]{:S(2)}, u32[]{:S(2)}) collective-permute-start(bf16[512,4096]{1,0:T(8,128)(2,1)} %wo_ref.3), channel_id=1, source_target_pairs={{0,1},{1,0},{2,3},{3,2},{4,5},{5,4},{6,7},{7,6},{8,9},{9,8},{10,11... | collective-permute-start | bytes 12582920 | tf_op jit(solution)/shard_map/ppermute | solution.py:490
  14.9 44.5 %copy-start.5 = (f32[2,64,2]{2,1,0:T(8,128)}, f32[2,64,2]{2,1,0:T(8,128)S(1)}, u32[]{:S(2)}) copy-start(f32[2,64,2]{2,1,0:T(8,128)S(1)} %copy.27) | copy-start | bytes 3076
  57.7 1.6 copy-start.4
  59.3 48.1 %all-to-all-start.1 = ((bf16[64,24,1024]{2,1,0:T(8,128)(2,1)}), bf16[64,24,1024]{2,1,0:T(8,128)(2,1)S(1)}, u32[]{:S(2)}, u32[]{:S(2)}) async-start(bf16[64,24,1024]{2,1,0:T(8,128)(2,1)} %bitcast.35), calls=%async_computation.1 | async-start | bytes 6291456 | tf_op jit(solution)/shard_map/all_to_all | solution.py:494
  107.5 4.9 %copy-start = (bf16[64,24,1024]{2,1,0:T(8,128)(2,1)}, bf16[64,24,1024]{2,1,0:T(8,128)(2,1)S(1)}, u32[]{:S(2)}) copy-start(bf16[64,24,1024]{2,1,0:T(8,128)(2,1)S(1)} %all-to-all-done.1) | copy-start | bytes 9437188
  107.5 20.2 %all-to-all-start.2 = ((bf16[16,256,128]{2,1,0:T(8,128)(2,1)}), bf16[16,256,128]{2,1,0:T(8,128)(2,1)}, u32[]{:S(2)}, u32[]{:S(2)}) async-start(bf16[16,256,128]{2,1,0:T(8,128)(2,1)} %bitcast.41), calls=%async_computation.2 | async-start | bytes 2097152 | tf_op jit(solution)/shard_map/all_to_all | solution.py:498
  134.3 9.6 %copy-start.15 = (bf16[128,2048]{1,0:T(8,128)(2,1)S(1)}, bf16[128,2048]{1,0:T(8,128)(2,1)}, u32[]{:S(2)}) copy-start(bf16[128,2048]{1,0:T(8,128)(2,1)} %get-tuple-element.39) | copy-start | bytes 1572868
  134.3 14.1 %copy-start.9 = (bf16[128,2048]{1,0:T(8,128)(2,1)S(1)}, bf16[128,2048]{1,0:T(8,128)(2,1)}, u32[]{:S(2)}) copy-start(bf16[128,2048]{1,0:T(8,128)(2,1)} %get-tuple-element.36) | copy-start | bytes 1572868
  134.3 14.1 %collective-permute-start.1 = (bf16[128,2048]{1,0:T(8,128)(2,1)}, bf16[128,2048]{1,0:T(8,128)(2,1)S(1)}, u32[]{:S(2)}, u32[]{:S(2)}) collective-permute-start(bf16[128,2048]{1,0:T(8,128)(2,1)} %get-tuple-element.37), channel_id=1, source_target_pairs={{0,2},{2,4},{4,6},{6,0},{1,3},{3,5},{5,7},{7,1},{8,10},{10,12},{12... | collective-permute-start | bytes 1572872 | tf_op jit(solution)/shard_map/ppermute | solution.py:503
  142.3 12.6 %collective-permute-start.5 = (bf16[128,2048]{1,0:T(8,128)(2,1)}, bf16[128,2048]{1,0:T(8,128)(2,1)S(1)}, u32[]{:S(2)}, u32[]{:S(2)}) collective-permute-start(bf16[128,2048]{1,0:T(8,128)(2,1)} %get-tuple-element.41), channel_id=1, source_target_pairs={{0,6},{2,0},{4,2},{6,4},{1,7},{3,1},{5,3},{7,5},{8,14},{10,8},{12,... | collective-permute-start | bytes 1572872 | tf_op jit(solution)/shard_map/ppermute | solution.py:505
  144.0 15.7 %collective-permute-start.3 = (bf16[128,2048]{1,0:T(8,128)(2,1)}, bf16[128,2048]{1,0:T(8,128)(2,1)S(1)}, u32[]{:S(2)}, u32[]{:S(2)}) collective-permute-start(bf16[128,2048]{1,0:T(8,128)(2,1)} %get-tuple-element.38), channel_id=1, source_target_pairs={{0,2},{2,4},{4,6},{6,0},{1,3},{3,5},{5,7},{7,1},{8,10},{10,12},{12... | collective-permute-start | bytes 1572872 | tf_op jit(solution)/shard_map/ppermute | solution.py:506
  144.0 22.1 %collective-permute-start.4 = (bf16[128,2048]{1,0:T(8,128)(2,1)S(1)}, bf16[128,2048]{1,0:T(8,128)(2,1)S(1)}, u32[]{:S(2)}, u32[]{:S(2)}) collective-permute-start(bf16[128,2048]{1,0:T(8,128)(2,1)S(1)} %copy-done.15), channel_id=1, source_target_pairs={{0,6},{2,0},{4,2},{6,4},{1,7},{3,1},{5,3},{7,5},{8,14},{10,8},{12,... | collective-permute-start | bytes 1572872 | tf_op jit(solution)/shard_map/ppermute | solution.py:507
  148.5 22.3 %collective-permute-start.2 = (bf16[128,2048]{1,0:T(8,128)(2,1)S(1)}, bf16[128,2048]{1,0:T(8,128)(2,1)S(1)}, u32[]{:S(2)}, u32[]{:S(2)}) collective-permute-start(bf16[128,2048]{1,0:T(8,128)(2,1)S(1)} %add_convert_fusion.2), channel_id=1, source_target_pairs={{0,2},{2,4},{4,6},{6,0},{1,3},{3,5},{5,7},{7,1},{8,10},{10,12},{12... | collective-permute-start | bytes 1572872 | tf_op jit(solution)/shard_map/ppermute | solution.py:508
  156.0 21.3 %collective-permute-start.6 = (bf16[128,2048]{1,0:T(8,128)(2,1)S(1)}, bf16[128,2048]{1,0:T(8,128)(2,1)S(1)}, u32[]{:S(2)}, u32[]{:S(2)}) collective-permute-start(bf16[128,2048]{1,0:T(8,128)(2,1)S(1)} %add_convert_fusion.1), channel_id=1, source_target_pairs={{0,6},{2,0},{4,2},{6,4},{1,7},{3,1},{5,3},{7,5},{8,14},{10,8},{12,... | collective-permute-start | bytes 1572872 | tf_op jit(solution)/shard_map/ppermute | solution.py:509
  159.6 17.7 %copy-start.6 = (bf16[128,2048]{1,0:T(8,128)(2,1)}, bf16[128,2048]{1,0:T(8,128)(2,1)S(1)}, u32[]{:S(2)}) copy-start(bf16[128,2048]{1,0:T(8,128)(2,1)S(1)} %collective-permute-done.3.ub) | copy-start | bytes 1572868
  166.1 11.2 %copy-start.7 = (bf16[128,2048]{1,0:T(8,128)(2,1)}, bf16[128,2048]{1,0:T(8,128)(2,1)S(1)}, u32[]{:S(2)}) copy-start(bf16[128,2048]{1,0:T(8,128)(2,1)S(1)} %collective-permute-done.4.da) | copy-start | bytes 1572868
  170.9 6.5 %copy-start.8 = (bf16[128,2048]{1,0:T(8,128)(2,1)}, bf16[128,2048]{1,0:T(8,128)(2,1)S(1)}, u32[]{:S(2)}) copy-start(bf16[128,2048]{1,0:T(8,128)(2,1)S(1)} %collective-permute-done.2.ua) | copy-start | bytes 1572868
  177.3 0.8 copy-start.10
  184.6 48.8 %all-to-all-start.3 = ((bf16[64,24,1024]{2,1,0:T(8,128)(2,1)}), bf16[64,24,1024]{2,1,0:T(8,128)(2,1)S(1)}, u32[]{:S(2)}, u32[]{:S(2)}) async-start(bf16[64,24,1024]{2,1,0:T(8,128)(2,1)} %bitcast.38), calls=%async_computation.3 | async-start | bytes 6291456 | tf_op jit(solution)/shard_map/all_to_all | solution.py:513
  193.4 132.7 %collective-permute-start.9 = (bf16[4,384,1024]{2,1,0:T(8,128)(2,1)}, bf16[4,384,1024]{2,1,0:T(8,128)(2,1)}, u32[]{:S(2)}, u32[]{:S(2)}) collective-permute-start(bf16[4,384,1024]{2,1,0:T(8,128)(2,1)} %get-tuple-element.49.g_ref), channel_id=1, source_target_pairs={{0,64},{64,0},{1,65},{65,1},{2,66},{66,2},{3,67},{67,3},{4,68},{68... | collective-permute-start | bytes 9437192 | tf_op jit(solution)/shard_map/ppermute | solution.py:500
  233.4 1.6 copy-start.2
  255.4 135.3 %collective-permute-start.7 = (bf16[4096,256]{1,0:T(8,128)(2,1)}, bf16[4096,256]{1,0:T(8,128)(2,1)}, u32[]{:S(2)}, u32[]{:S(2)}) collective-permute-start(bf16[4096,256]{1,0:T(8,128)(2,1)} %up_half.3), channel_id=1, source_target_pairs={{0,64},{64,0},{1,65},{65,1},{2,66},{66,2},{3,67},{67,3},{4,68},{68... | collective-permute-start | bytes 6291464 | tf_op jit(solution)/shard_map/ppermute | solution.py:521
  258.0 7.3 %copy-start.16 = (bf16[384,256]{1,0:T(8,128)(2,1)S(1)}, bf16[384,256]{1,0:T(8,128)(2,1)}, u32[]{:S(2)}) copy-start(bf16[384,256]{1,0:T(8,128)(2,1)} %get-tuple-element.50) | copy-start | bytes 589828
  258.0 136.1 %all-to-all-start.4 = ((bf16[64,24,1024]{2,1,0:T(8,128)(2,1)}), bf16[64,24,1024]{2,1,0:T(8,128)(2,1)S(1)}, u32[]{:S(2)}, u32[]{:S(2)}) async-start(bf16[64,24,1024]{2,1,0:T(8,128)(2,1)} %bitcast.37), calls=%async_computation.4 | async-start | bytes 6291456 | tf_op jit(solution)/shard_map/all_to_all | solution.py:519
  265.3 118.4 %collective-permute-start.8 = (bf16[384,256]{1,0:T(8,128)(2,1)S(1)}, bf16[384,256]{1,0:T(8,128)(2,1)S(1)}, u32[]{:S(2)}, u32[]{:S(2)}) collective-permute-start(bf16[384,256]{1,0:T(8,128)(2,1)S(1)} %copy-done.16), channel_id=1, source_target_pairs={{0,64},{64,0},{1,65},{65,1},{2,66},{66,2},{3,67},{67,3},{4,68},{68... | collective-permute-start | bytes 589832 | tf_op jit(solution)/shard_map/ppermute | solution.py:518
  384.3 6.3 %copy-start.3 = (bf16[4096,256]{1,0:T(8,128)(2,1)S(1)}, bf16[4096,256]{1,0:T(8,128)(2,1)}, u32[]{:S(2)}) copy-start(bf16[4096,256]{1,0:T(8,128)(2,1)} %up_half.2) | copy-start | bytes 6291460
  394.1 1.6 copy-start.1
  (1 other events, 0.7 us)

commit v3 on v2

--- a/solution.py
+++ b/solution.py
@@ -23,6 +23,8 @@
 CW = D // CB
 GROUP = 8
 GR = GROUP * ROWS
+GRAD_WIDTHS = (CW, 2 * CW, CW)
+GRAD_CUTS = ((0, slice(0, CW)), (1, slice(0, CW)), (1, slice(CW, 2 * CW)), (2, slice(0, CW)))
 EXP_SCALE = HEAD**-0.5 * 1.4426950408889634
 QB = 256
 KB = 512
@@ -54,16 +56,16 @@
 
 def pack(queries, keys, values):
     def kernel(q_ref, k_ref, v_ref, o_ref):
-        o_ref[0, 0] = q_ref[0]
-        o_ref[0, 1] = k_ref[0]
-        o_ref[0, 2] = v_ref[0]
-
-    spec = pl.BlockSpec((1, 512, HEAD), lambda b, h: (b, 0, h))
-    return pl.pallas_call(
-        kernel,
-        grid=(2, 4),
+        for part, ref in enumerate((q_ref, k_ref, v_ref)):
+            for h in range(4):
+                o_ref[h, part] = ref[0, :, h * HEAD : (h + 1) * HEAD]
+
+    spec = pl.BlockSpec((1, 256, 4 * HEAD), lambda b, t: (b, t, 0))
+    return pl.pallas_call(
+        kernel,
+        grid=(2, 2),
         in_specs=[spec] * 3,
-        out_specs=pl.BlockSpec((1, 3, 512, HEAD), lambda b, h: (b * 4 + h, 0, 0, 0)),
+        out_specs=pl.BlockSpec((4, 3, 256, HEAD), lambda b, t: (b, 0, t, 0)),
         out_shape=jax.ShapeDtypeStruct((8, 3, 512, HEAD), BF),
         compiler_params=params(),
         name="pack_heads",
@@ -289,11 +291,14 @@
 
 
 def grads_in(chunks, down):
-    def kernel(i_ref, d_ref, g_ref, b_ref):
-        mix_in(i_ref, g_ref)
+    def kernel(i_ref, d_ref, *refs):
+        b_ref, sc_ref = refs[-2:]
+        mix_in(i_ref, sc_ref)
         back = None
         for c in range(CB):
-            part = dot_nt(g_ref[c], d_ref[:, c * CW : (c + 1) * CW])
+            number, cut = GRAD_CUTS[c]
+            refs[number][:, cut] = sc_ref[c]
+            part = dot_nt(sc_ref[c], d_ref[:, c * CW : (c + 1) * CW])
             back = part if back is None else back + part
         b_ref[...] = back
 
@@ -301,11 +306,10 @@
         kernel,
         grid=(1,),
         in_specs=[whole(CB * SLOTS, CW), whole(FF, D)],
-        out_specs=[whole(CB, SLOTS, CW), whole(SLOTS, FF)],
-        out_shape=[
-            jax.ShapeDtypeStruct((CB, SLOTS, CW), BF),
-            jax.ShapeDtypeStruct((SLOTS, FF), F32),
-        ],
+        out_specs=[whole(SLOTS, w) for w in GRAD_WIDTHS] + [whole(SLOTS, FF)],
+        out_shape=[jax.ShapeDtypeStruct((SLOTS, w), BF) for w in GRAD_WIDTHS]
+        + [jax.ShapeDtypeStruct((SLOTS, FF), F32)],
+        scratch_shapes=[pltpu.VMEM((CB, SLOTS, CW), BF)],
         compiler_params=params(),
         name="grads_in",
     )(chunks, down)
@@ -317,8 +321,8 @@
     return (pre * cdf_part, cdf_part + pre * density)
 
 
-def experts(place, chunks, up, down, back):
-    def kernel(place_ref, i_ref, up_ref, down_ref, b_ref, x_ref, ho_ref, hs_ref, pg_ref, o_ref, pre, hid, prod):
+def hidden_units(place, chunks, up, back):
+    def kernel(place_ref, i_ref, up_ref, b_ref, x_ref, hid_ref, ho_ref, hs_ref, pg_ref, pre):
         i = pl.program_id(0)
 
         @pl.when(i == 0)
@@ -326,62 +330,70 @@
             mix_in(i_ref, x_ref)
             pre[...] = dot_nn(x_ref[0], up_ref[...])
 
-        @pl.when((i > 0) & (i < CB))
+        @pl.when(i > 0)
         def _():
             pre[...] += dot_nn(x_ref[i], up_ref[...])
 
         @pl.when(i == CB - 1)
         def _():
             act, slope = gelu_pair(pre[...])
-            hid[...] = act.astype(BF)
+            hid_ref[...] = act.astype(BF)
             pg_ref[...] = (b_ref[...] * slope).astype(BF)
             low, high = act[:, :HALF].astype(BF), act[:, HALF:].astype(BF)
             mine = place_ref[2] == 0
             hs_ref[...] = jnp.where(mine, low, high)
             ho_ref[...] = jnp.where(mine, high, low)
 
-        @pl.when(i >= CB)
-        def _():
-            prod[i - CB] = dot_nn(hid[...], down_ref[...]).astype(BF)
-
-        @pl.when(i == 2 * CB - 1)
-        def _():
-            mix_out(prod, o_ref)
-
     return pl.pallas_call(
         kernel,
         grid_spec=pltpu.PrefetchScalarGridSpec(
             num_scalar_prefetch=1,
-            grid=(2 * CB,),
+            grid=(CB,),
             in_specs=[
                 whole(CB * SLOTS, CW),
-                pl.BlockSpec((CW, FF), lambda i, _: (jnp.minimum(i, CB - 1), 0)),
-                pl.BlockSpec((FF, CW), lambda i, _: (0, jnp.maximum(i - CB, 0))),
+                pl.BlockSpec((CW, FF), lambda i, _: (i, 0)),
                 whole(SLOTS, FF),
             ],
             out_specs=[
                 whole(CB, SLOTS, CW),
+                whole(SLOTS, FF),
                 whole(SLOTS, HALF),
                 whole(SLOTS, HALF),
                 whole(SLOTS, FF),
-                whole(CB * SLOTS, CW),
             ],
-            scratch_shapes=[
-                pltpu.VMEM((SLOTS, FF), F32),
-                pltpu.VMEM((SLOTS, FF), BF),
-                pltpu.VMEM((CB, SLOTS, CW), BF),
-            ],
+            scratch_shapes=[pltpu.VMEM((SLOTS, FF), F32)],
         ),
         out_shape=[
             jax.ShapeDtypeStruct((CB, SLOTS, CW), BF),
+            jax.ShapeDtypeStruct((SLOTS, FF), BF),
             jax.ShapeDtypeStruct((SLOTS, HALF), BF),
             jax.ShapeDtypeStruct((SLOTS, HALF), BF),
             jax.ShapeDtypeStruct((SLOTS, FF), BF),
-            jax.ShapeDtypeStruct((CB * SLOTS, CW), BF),
         ],
         compiler_params=params(),
-        name="experts",
-    )(place, chunks, up, down, back)
+        name="hidden_units",
+    )(place, chunks, up, back)
+
+
+def expert_out(hidden, down):
+    def kernel(h_ref, down_ref, o_ref, prod):
+        i = pl.program_id(0)
+        prod[i] = dot_nn(h_ref[...], down_ref[...]).astype(BF)
+
+        @pl.when(i == CB - 1)
+        def _():
+            mix_out(prod, o_ref)
+
+    return pl.pallas_call(
+        kernel,
+        grid=(CB,),
+        in_specs=[whole(SLOTS, FF), pl.BlockSpec((FF, CW), lambda i: (0, i))],
+        out_specs=whole(CB * SLOTS, CW),
+        out_shape=jax.ShapeDtypeStruct((CB * SLOTS, CW), BF),
+        scratch_shapes=[pltpu.VMEM((CB, SLOTS, CW), BF)],
+        compiler_params=params(),
+        name="expert_out",
+    )(hidden, down)
 
 
 def up_half(half, rows, pre_grad):
@@ -409,23 +421,26 @@
 
 
 def down_sum(hidden, grads, hidden_far, grads_far):
-    def kernel(h_ref, g_ref, hf_ref, gf_ref, o_ref):
-        total = dot_tn(h_ref[...], g_ref[0]) + dot_tn(hf_ref[...], gf_ref[0])
-        o_ref[...] = total.astype(BF)
-
-    rows = pl.BlockSpec((1, SLOTS, CW), lambda c: (c, 0, 0))
-    return pl.pallas_call(
-        kernel,
-        grid=(CB,),
-        in_specs=[whole(SLOTS, HALF), rows, whole(SLOTS, HALF), rows],
-        out_specs=pl.BlockSpec((HALF, CW), lambda c: (0, c)),
+    def kernel(h_ref, hf_ref, *refs):
+        o_ref = refs[-1]
+        for c in range(CB):
+            number, cut = GRAD_CUTS[c]
+            near, far = refs[number], refs[3 + number]
+            total = dot_tn(h_ref[...], near[:, cut]) + dot_tn(hf_ref[...], far[:, cut])
+            o_ref[:, c * CW : (c + 1) * CW] = total.astype(BF)
+
+    return pl.pallas_call(
+        kernel,
+        grid=(1,),
+        in_specs=[whole(SLOTS, HALF)] * 2 + [whole(SLOTS, w) for w in GRAD_WIDTHS] * 2,
+        out_specs=whole(HALF, D),
         out_shape=jax.ShapeDtypeStruct((HALF, D), BF),
         compiler_params=params(),
         cost_estimate=pl.CostEstimate(
             flops=4 * SLOTS * D * HALF, bytes_accessed=9 << 20, transcendentals=0
         ),
         name="down_sum",
-    )(hidden, grads, hidden_far, grads_far)
+    )(hidden, hidden_far, *grads, *grads_far)
 
 
 def combine(chunks, stream, gate, target, weight):
@@ -496,31 +511,33 @@
     heads = attend(rows).reshape(16, 256, HEAD)
     heads, grad_arrived = lax.optimization_barrier((heads, grad_arrived))
     heads = exchange(heads, BACK).reshape(2, 4, 2, 4, 64, HEAD)
-    grads, back = grads_in(grad_arrived, down_weight[0])
-    grads_far = lax.ppermute(grads, "dp", swap)
+    *grads, back = grads_in(grad_arrived, down_weight[0])
     heads, grads, back = lax.optimization_barrier((heads, grads, back))
+    far_0, far_1, far_2 = [lax.ppermute(g, "dp", swap) for g in grads]
     fa, ua, da, own_a = project(place, 0, heads, out_weight, weight_other)
     fa = lax.ppermute(fa, "z", above)
+    heads, far_0 = lax.optimization_barrier((heads, far_0))
     fb, ub, db, own_b = project(place, 1, heads, out_weight, weight_other)
     fb = lax.ppermute(fb, "z", below)
     ub = lax.ppermute(ub, "z", above)
     da = lax.ppermute(da, "z", below)
     ua = lax.ppermute(plus(ua, fa), "z", above)
     db = lax.ppermute(plus(db, fb), "z", below)
+    own_a, ua, far_1 = lax.optimization_barrier((own_a, ua, far_1))
     stream, chunks = norm_send(
         own_a, own_b, ua, ub, da, db, residual.reshape(TOK, D), norm_gain[None], target
     )
     arrived = exchange(chunks, ALL)
 
-    own_rows, hid_other, hid_own, pre_grad, products = experts(
-        place, arrived, up_weight[0], down_weight[0], back
-    )
+    own_rows, hidden, hid_other, hid_own, pre_grad = hidden_units(place, arrived, up_weight[0], back)
     hid_far = lax.ppermute(hid_other, "dp", swap)
-    returned = exchange(products, ALL)
+    returned = exchange(expert_out(hidden, down_weight[0]), ALL)
+    own_rows, pre_grad, far_2 = lax.optimization_barrier((own_rows, pre_grad, far_2))
     up_other = up_half((1 - dp)[None].astype(jnp.int32), own_rows, pre_grad)
+    up_other, hid_far = lax.optimization_barrier((up_other, hid_far))
     up_far = lax.ppermute(up_other, "dp", swap)
     up_own = up_half(dp[None].astype(jnp.int32), own_rows, pre_grad)
-    down_total = down_sum(hid_own, grads, hid_far, grads_far)
+    down_total = down_sum(hid_own, grads, hid_far, (far_0, far_1, far_2))
     block_out = combine(returned, stream, gate, target, weight_col)
     up_total = plus(up_own, up_far)
     return (block_out.reshape(2, TOK // 2, D), up_total[None], down_total[None])

time: 403 us -> 356 us (0.88)
  waiting for transfers between devices: 235 us -> 180 us
  starting transfers between devices: 50 us -> 57.4 us
    ppermute x1, waiting for transfers between devices: 57.5 us -> 0.01 us  [body(): hid_far = lax.ppermute(hid_other, 'dp', swap)]
    ppermute x1, waiting for transfers between devices: 0.01 us -> 43.7 us  [body(): up_far = lax.ppermute(up_other, 'dp', swap)]
    ppermute x1 -> x3, waiting for transfers between devices: 55.1 us -> 23.6 us  [body(): far_0, far_1, far_2 = [lax.ppermute(g, 'dp', swap) for g in grads]]
    ppermute x1, waiting for transfers between devices: 6.46 us -> 0.01 us  [body(): da = lax.ppermute(da, 'z', below)]
    ppermute x1, waiting for transfers between devices: 4.77 us -> 0.01 us  [body(): ua = lax.ppermute(plus(ua, fa), 'z', above)]
    pallas_call x3 -> x4, Pallas kernels: 28 us -> 27.6 us  [the longest x1 9.4 us: hidden_units(): pl.pallas_call(kernel, grid_spec=pltpu.PrefetchScalarGridSpec(num_scalar_...]
  transfers between devices with their start and end apart: 15 -> 17, of which waited for: 12 -> 11; matrix products, arithmetic and copies ran while one was open for 2% -> 2% of each run, Pallas kernels for 19% -> 24%
where the time goes in v3:
time: 356 us; the launch traced here: 354 us
  waiting for transfers between devices  180 us (51%)
  Pallas kernels  101 us (28%)
  starting transfers between devices  57.4 us (16%)
  local copies, waits for them, and re-layouts  8.43 us (2%)
  other arithmetic  6.83 us (2%)
    ppermute x1, waiting for transfers between devices, body(): up_far = lax.ppermute(up_other, 'dp', swap)  43.7 us
    all_to_all x1, waiting for transfers between devices, body(): arrived = exchange(chunks, ALL)  37.3 us
    all_to_all x1, waiting for transfers between devices, body(): rows = exchange(pack(queries, keys, values), SEQ)  36.9 us
    pallas_call x1, Pallas kernels, attend(): pl.pallas_call(kernel, grid=(8,), in_specs=[pl.BlockSpec((1, 1, 512, HEAD...  25.9 us
    ppermute x3, waiting for transfers between devices, body(): far_0, far_1, far_2 = [lax.ppermute(g, 'dp', swap) for g in grads]  23.6 us
    pallas_call x2, Pallas kernels, project(): pl.pallas_call(kernel, grid_spec=pltpu.PrefetchScalarGridSpec(num_scalar_...  13.6 us
    all_to_all x1, waiting for transfers between devices, body(): grad_arrived = exchange(grad_chunks, ALL)  13.5 us
    all_to_all x1, starting transfers between devices, body(): arrived = exchange(chunks, ALL)  12 us
  transfers between devices with their start and end apart: 17, of which 11 were waited for; matrix products, arithmetic and copies ran while one was open for 2% of the time, Pallas kernels for 24%

profile of v3, /device:TPU:1, one launch (start us, length us, event | category | flops | bytes accessed | tf_op | source)
XLA Modules:
  0.0 354.0 jit_solution(14534731866531896273)
XLA Ops:
  0.6 4.3 %pack_heads.1 = bf16[8,3,512,128]{3,2,1,0:T(8,128)(2,1)} custom-call(bf16[2,512,512]{2,1,0:T(8,128)(2,1)} %q_ref.1, bf16[2,512,512]{2,1,0:T(8,128)(2,1)} %k_ref.1, bf16[2,512,512]{2,1,0:T(8,128)(2,1)} %v_ref.1), custom_call_target="tpu_custom_call" | custom-call | tf_op jit(solution)/shard_map/pack_heads/pallas_call | solution.py:64
  5.0 6.0 %all-to-all-start = ((bf16[8,3,512,128]{3,2,1,0:T(8,128)(2,1)}), bf16[8,3,512,128]{3,2,1,0:T(8,128)(2,1)S(1)}, u32[]{:S(2)}, u32[]{:S(2)}) async-start(bf16[8,3,512,128]{3,2,1,0:T(8,128)(2,1)} %pack_heads.1), calls=%async_computation | async-start | bytes 6291456 | tf_op jit(solution)/shard_map/all_to_all | solution.py:504
  13.9 5.0 %send_grads.1 = bf16[1536,1024]{1,0:T(8,128)(2,1)} custom-call(bf16[128,4096]{1,0:T(8,128)(2,1)} %bitcast.42, f32[2,4096]{1,0:T(2,128)} %broadcast_select_fusion.gate_ref, s32[2,128]{1,0:T(2,128)} %add_bitcast_fusion.tgt_ref, f32[2,128]{1,0:T(2,128)} %copy.28.w_ref), custom_call_target="tpu_custom_call" | custom-call | tf_op jit(solution)/shard_map/send_grads/pallas_call | solution.py:248
  18.9 36.9 %all-to-all-done.q_ref.qn_ref.k_ref.v_ref = bf16[8,3,512,128]{3,2,1,0:T(8,128)(2,1)S(1)} async-done(((bf16[8,3,512,128]{3,2,1,0:T(8,128)(2,1)}), bf16[8,3,512,128]{3,2,1,0:T(8,128)(2,1)S(1)}, u32[]{:S(2)}, u32[]{:S(2)}) %all-to-all-start) | async-done | bytes 3145760 | tf_op jit(solution)/shard_map/all_to_all | solution.py:504
  57.5 8.1 %all-to-all-start.1 = ((bf16[64,24,1024]{2,1,0:T(8,128)(2,1)}), bf16[64,24,1024]{2,1,0:T(8,128)(2,1)S(1)}, u32[]{:S(2)}, u32[]{:S(2)}) async-start(bf16[64,24,1024]{2,1,0:T(8,128)(2,1)} %bitcast.36), calls=%async_computation.1 | async-start | bytes 6291456 | tf_op jit(solution)/shard_map/all_to_all | solution.py:509
  66.2 25.9 %attend.1 = bf16[8,2,4,64,128]{4,3,2,1,0:T(8,128)(2,1)} custom-call(bf16[8,3,512,128]{3,2,1,0:T(8,128)(2,1)} %copy-done.4, bf16[8,3,512,128]{3,2,1,0:T(8,128)(2,1)} %copy-done.4, bf16[8,3,512,128]{3,2,1,0:T(8,128)(2,1)} %copy-done.4, bf16[8,3,512,128]{3,2,1,0:T(8,128)(2,1)} %copy-done.4), custom_call_target="tpu_custom_call" | custom-call | flops 17179869184 | bytes 4194304 | tf_op jit(solution)/shard_map/attend/pallas_call | solution.py:126
  92.1 13.5 %all-to-all-done.1 = bf16[64,24,1024]{2,1,0:T(8,128)(2,1)S(1)} async-done(((bf16[64,24,1024]{2,1,0:T(8,128)(2,1)}), bf16[64,24,1024]{2,1,0:T(8,128)(2,1)S(1)}, u32[]{:S(2)}, u32[]{:S(2)}) %all-to-all-start.1) | async-done | bytes 3145760 | tf_op jit(solution)/shard_map/all_to_all | solution.py:509
  105.7 4.3 %all-to-all-start.2 = ((bf16[16,256,128]{2,1,0:T(8,128)(2,1)}), bf16[16,256,128]{2,1,0:T(8,128)(2,1)}, u32[]{:S(2)}, u32[]{:S(2)}) async-start(bf16[16,256,128]{2,1,0:T(8,128)(2,1)} %bitcast.41), calls=%async_computation.2 | async-start | bytes 2097152 | tf_op jit(solution)/shard_map/all_to_all | solution.py:513
  110.0 6.7 %grads_in.1 = (bf16[384,1024]{1,0:T(8,128)(2,1)}, bf16[384,2048]{1,0:T(8,128)(2,1)}, bf16[384,1024]{1,0:T(8,128)(2,1)}, f32[384,512]{1,0:T(8,128)}) custom-call(bf16[1536,1024]{1,0:T(8,128)(2,1)} %bitcast.32, bf16[512,4096]{1,0:T(8,128)(2,1)} %bitcast.30), custom_call_target="tpu_custom_call" | custom-call | tf_op jit(solution)/shard_map/grads_in/pallas_call | solution.py:305
  116.6 9.2 %all-to-all-done.2 = bf16[16,256,128]{2,1,0:T(8,128)(2,1)} async-done(((bf16[16,256,128]{2,1,0:T(8,128)(2,1)}), bf16[16,256,128]{2,1,0:T(8,128)(2,1)}, u32[]{:S(2)}, u32[]{:S(2)}) %all-to-all-start.2) | async-done | bytes 1048608 | tf_op jit(solution)/shard_map/all_to_all | solution.py:513
  129.1 6.8 %project.2 = (bf16[128,2048]{1,0:T(8,128)(2,1)}, bf16[128,2048]{1,0:T(8,128)(2,1)}, bf16[128,2048]{1,0:T(8,128)(2,1)}, bf16[128,2048]{1,0:T(8,128)(2,1)}) custom-call(s32[3]{0:T(128)} %pad_add_fusion.place_ref, bf16[2,4,2,4,64,128]{5,4,3,2,1,0:T(8,128)(2,1)} %bitcast.12.a_ref, bf16[512,4096]{1,0:T(8,128)(2,1)} %wo_ref.3, ...), custom_call_target="tpu_custom_call" | custom-call | flops 2147483648 | bytes 7340032 | tf_op jit(solution)/shard_map/project/pallas_call | solution.py:175
  137.5 8.3 %collective-permute-done.4.refs_3_ = bf16[384,1024]{1,0:T(8,128)(2,1)S(1)} collective-permute-done((bf16[384,1024]{1,0:T(8,128)(2,1)}, bf16[384,1024]{1,0:T(8,128)(2,1)S(1)}, u32[]{:S(2)}, u32[]{:S(2)}) %collective-permute-start.4) | collective-permute-done | bytes 786464 | tf_op jit(solution)/shard_map/ppermute | solution.py:516
  145.8 6.7 %project.3 = (bf16[128,2048]{1,0:T(8,128)(2,1)}, bf16[128,2048]{1,0:T(8,128)(2,1)}, bf16[128,2048]{1,0:T(8,128)(2,1)}, bf16[128,2048]{1,0:T(8,128)(2,1)}) custom-call(s32[3]{0:T(128)} %pad_add_fusion.place_ref, bf16[2,4,2,4,64,128]{5,4,3,2,1,0:T(8,128)(2,1)} %bitcast.12.a_ref, bf16[512,4096]{1,0:T(8,128)(2,1)} %wo_ref.3, ...), custom_call_target="tpu_custom_call" | custom-call | flops 2147483648 | bytes 7340032 | tf_op jit(solution)/shard_map/project/pallas_call | solution.py:175
  156.2 6.9 %collective-permute-done.7 = bf16[128,2048]{1,0:T(8,128)(2,1)S(1)} collective-permute-done((bf16[128,2048]{1,0:T(8,128)(2,1)}, bf16[128,2048]{1,0:T(8,128)(2,1)S(1)}, u32[]{:S(2)}, u32[]{:S(2)}) %collective-permute-start.7) | collective-permute-done | bytes 524320 | tf_op jit(solution)/shard_map/ppermute | solution.py:521
  164.2 3.1 collective-permute-start.8
  167.4 12.1 %collective-permute-done.3.refs_4_ = bf16[384,2048]{1,0:T(8,128)(2,1)S(1)} collective-permute-done((bf16[384,2048]{1,0:T(8,128)(2,1)S(1)}, bf16[384,2048]{1,0:T(8,128)(2,1)S(1)}, u32[]{:S(2)}, u32[]{:S(2)}) %collective-permute-start.3) | collective-permute-done | bytes 1572896 | tf_op jit(solution)/shard_map/ppermute | solution.py:516
  180.7 4.9 %collective-permute-done.8.db = bf16[128,2048]{1,0:T(8,128)(2,1)S(1)} collective-permute-done((bf16[128,2048]{1,0:T(8,128)(2,1)S(1)}, bf16[128,2048]{1,0:T(8,128)(2,1)S(1)}, u32[]{:S(2)}, u32[]{:S(2)}) %collective-permute-start.8) | collective-permute-done | bytes 524320 | tf_op jit(solution)/shard_map/ppermute | solution.py:525
  186.3 6.4 %norm_send.1 = (f32[128,4096]{1,0:T(8,128)}, bf16[1536,1024]{1,0:T(8,128)(2,1)}) custom-call(bf16[128,2048]{1,0:T(8,128)(2,1)} %get-tuple-element.54.oa, bf16[128,2048]{1,0:T(8,128)(2,1)} %get-tuple-element.57.ob, bf16[128,2048]{1,0:T(8,128)(2,1)} %copy-done.10, bf16[128,2048]{1,0:T(8,128)(2,1)} %copy-done.11, bf16[128,2048]{1,0:T(8,128)(2,1)} %copy-done.9, ...), custom_call_target="tpu_custom_call" | custom-call | tf_op jit(solution)/shard_map/norm_send/pallas_call | solution.py:277
  192.7 12.0 %all-to-all-start.3 = ((bf16[64,24,1024]{2,1,0:T(8,128)(2,1)}), bf16[64,24,1024]{2,1,0:T(8,128)(2,1)S(1)}, u32[]{:S(2)}, u32[]{:S(2)}) async-start(bf16[64,24,1024]{2,1,0:T(8,128)(2,1)} %bitcast.38), calls=%async_computation.3 | async-start | bytes 6291456 | tf_op jit(solution)/shard_map/all_to_all | solution.py:530
  204.7 2.7 collective-permute-start.9
  207.4 37.3 %all-to-all-done.3 = bf16[64,24,1024]{2,1,0:T(8,128)(2,1)S(1)} async-done(((bf16[64,24,1024]{2,1,0:T(8,128)(2,1)}), bf16[64,24,1024]{2,1,0:T(8,128)(2,1)S(1)}, u32[]{:S(2)}, u32[]{:S(2)}) %all-to-all-start.3) | async-done | bytes 3145760 | tf_op jit(solution)/shard_map/all_to_all | solution.py:530
  246.3 9.4 %hidden_units.1 = (bf16[4,384,1024]{2,1,0:T(8,128)(2,1)}, bf16[384,512]{1,0:T(8,128)(2,1)}, bf16[384,256]{1,0:T(8,128)(2,1)}, bf16[384,256]{1,0:T(8,128)(2,1)}, bf16[384,512]{1,0:T(8,128)(2,1)}) custom-call(s32[3]{0:T(128)} %pad_add_fusion.place_ref, bf16[1536,1024]{1,0:T(8,128)(2,1)} %bitcast.35, bf16[4096,512]{1,0:T(8,128)(2,1)} %bitcast.37, ...), custom_call_target="tpu_custom_call" | custom-call | tf_op jit(solution)/shard_map/hidden_units/pallas_call | solution.py:347
  258.4 3.2 collective-permute-done.9.refs_5_
  261.5 4.9 %up_half.3 = bf16[4096,256]{1,0:T(8,128)(2,1)} custom-call(s32[1]{0:T(128)} %bitcast.22.half_ref, bf16[4,384,1024]{2,1,0:T(8,128)(2,1)} %get-tuple-element.70.x_ref, bf16[384,512]{1,0:T(8,128)(2,1)} %get-tuple-element.71.p_ref), custom_call_target="tpu_custom_call" | custom-call | flops 805306368 | bytes 6291456 | tf_op jit(solution)/shard_map/up_half/pallas_call | solution.py:403
  266.8 7.1 %expert_out.1 = bf16[1536,1024]{1,0:T(8,128)(2,1)} custom-call(bf16[384,512]{1,0:T(8,128)(2,1)} %get-tuple-element.65.h_ref, bf16[512,4096]{1,0:T(8,128)(2,1)} %bitcast.31), custom_call_target="tpu_custom_call" | custom-call | tf_op jit(solution)/shard_map/expert_out/pallas_call | solution.py:387
  273.9 10.0 %all-to-all-start.4 = ((bf16[64,24,1024]{2,1,0:T(8,128)(2,1)}), bf16[64,24,1024]{2,1,0:T(8,128)(2,1)S(1)}, u32[]{:S(2)}, u32[]{:S(2)}) async-start(bf16[64,24,1024]{2,1,0:T(8,128)(2,1)} %bitcast.34), calls=%async_computation.4 | async-start | bytes 6291456 | tf_op jit(solution)/shard_map/all_to_all | solution.py:534
  283.9 4.9 %up_half.2 = bf16[4096,256]{1,0:T(8,128)(2,1)} custom-call(s32[1]{0:T(128)} %bitcast.2.half_ref, bf16[4,384,1024]{2,1,0:T(8,128)(2,1)} %get-tuple-element.70.x_ref, bf16[384,512]{1,0:T(8,128)(2,1)} %get-tuple-element.71.p_ref), custom_call_target="tpu_custom_call" | custom-call | flops 805306368 | bytes 6291456 | tf_op jit(solution)/shard_map/up_half/pallas_call | solution.py:403
  288.8 6.8 %down_sum.1 = bf16[256,4096]{1,0:T(8,128)(2,1)} custom-call(bf16[384,256]{1,0:T(8,128)(2,1)} %get-tuple-element.74.h_ref, bf16[384,256]{1,0:T(8,128)(2,1)} %copy-done.14, bf16[384,1024]{1,0:T(8,128)(2,1)} %get-tuple-element.55.refs_0_, bf16[384,2048]{1,0:T(8,128)(2,1)} %get-tuple-element.53.refs_1_, bf16[384,1024]{1,0:T(8,128)(2,1)} %get-tuple-element.69.refs_2_, ...), custom_call_target="tpu_custom_call" | custom-call | flops 1610612736 | bytes 9437184 | tf_op jit(solution)/shard_map/down_sum/pallas_call | solution.py:432
  295.6 43.7 %collective-permute-done.11 = bf16[4096,256]{1,0:T(8,128)(2,1)} collective-permute-done((bf16[4096,256]{1,0:T(8,128)(2,1)}, bf16[4096,256]{1,0:T(8,128)(2,1)}, u32[]{:S(2)}, u32[]{:S(2)}) %collective-permute-start.11) | collective-permute-done | bytes 2097184 | tf_op jit(solution)/shard_map/ppermute | solution.py:538
  339.3 3.4 fusion
  342.8 3.9 %all-to-all-done.4 = bf16[64,24,1024]{2,1,0:T(8,128)(2,1)S(1)} async-done(((bf16[64,24,1024]{2,1,0:T(8,128)(2,1)}), bf16[64,24,1024]{2,1,0:T(8,128)(2,1)S(1)}, u32[]{:S(2)}, u32[]{:S(2)}) %all-to-all-start.4) | async-done | bytes 3145760 | tf_op jit(solution)/shard_map/all_to_all | solution.py:534
  348.3 5.7 %combine.1 = bf16[128,4096]{1,0:T(8,128)(2,1)} custom-call(bf16[1536,1024]{1,0:T(8,128)(2,1)} %bitcast.33, f32[128,4096]{1,0:T(8,128)} %get-tuple-element.66.s_ref, f32[2,4096]{1,0:T(2,128)} %broadcast_select_fusion.gate_ref, s32[2,128]{1,0:T(2,128)} %add_bitcast_fusion.tgt_ref, f32[128,2]{1,0:T(8,128)} %bitcast.45), custom_call_target="tpu_custom_call" | custom-call | tf_op jit(solution)/shard_map/combine/pallas_call | solution.py:457
  (77 shorter events, 23.0 us)
Async XLA Ops:
  5.0 6.0 %copy-start.16 = (s32[2,64,2]{1,2,0:T(2,128)S(1)}, s32[2,64,2]{1,2,0:T(2,128)}, u32[]{:S(2)}) copy-start(s32[2,64,2]{1,2,0:T(2,128)} %param.19) | copy-start | bytes 3076
  5.0 6.3 %copy-start.17 = (f32[2,64,2]{1,2,0:T(2,128)S(1)}, f32[2,64,2]{1,2,0:T(2,128)}, u32[]{:S(2)}) copy-start(f32[2,64,2]{1,2,0:T(2,128)} %param.20) | copy-start | bytes 3076
  5.0 7.6 %copy-start.19 = (s32[2]{0:T(128)S(1)}, s32[2]{0:T(128)}, u32[]{:S(2)}) copy-start(s32[2]{0:T(128)} %param.21) | copy-start | bytes 28
  5.0 8.2 %copy-start.15 = (f32[2,4096]{1,0:T(2,128)S(1)}, f32[2,4096]{1,0:T(2,128)}, u32[]{:S(2)}) copy-start(f32[2,4096]{1,0:T(2,128)} %param.22) | copy-start | bytes 98308
  5.0 50.8 %all-to-all-start = ((bf16[8,3,512,128]{3,2,1,0:T(8,128)(2,1)}), bf16[8,3,512,128]{3,2,1,0:T(8,128)(2,1)S(1)}, u32[]{:S(2)}, u32[]{:S(2)}) async-start(bf16[8,3,512,128]{3,2,1,0:T(8,128)(2,1)} %pack_heads.1), calls=%async_computation | async-start | bytes 6291456 | tf_op jit(solution)/shard_map/all_to_all | solution.py:504
  11.4 46.1 %copy-start.8 = (f32[2,64,2]{2,1,0:T(8,128)}, f32[2,64,2]{2,1,0:T(8,128)S(1)}, u32[]{:S(2)}) copy-start(f32[2,64,2]{2,1,0:T(8,128)S(1)} %copy.27) | copy-start | bytes 3076
  57.5 48.1 %all-to-all-start.1 = ((bf16[64,24,1024]{2,1,0:T(8,128)(2,1)}), bf16[64,24,1024]{2,1,0:T(8,128)(2,1)S(1)}, u32[]{:S(2)}, u32[]{:S(2)}) async-start(bf16[64,24,1024]{2,1,0:T(8,128)(2,1)} %bitcast.36), calls=%async_computation.1 | async-start | bytes 6291456 | tf_op jit(solution)/shard_map/all_to_all | solution.py:509
  65.7 63.5 %collective-permute-start = (bf16[512,4096]{1,0:T(8,128)(2,1)}, bf16[512,4096]{1,0:T(8,128)(2,1)}, u32[]{:S(2)}, u32[]{:S(2)}) collective-permute-start(bf16[512,4096]{1,0:T(8,128)(2,1)} %wo_ref.3), channel_id=1, source_target_pairs={{0,1},{1,0},{2,3},{3,2},{4,5},{5,4},{6,7},{7,6},{8,9},{9,8},{10,11... | collective-permute-start | bytes 12582920 | tf_op jit(solution)/shard_map/ppermute | solution.py:505
  105.7 4.3 %copy-start = (bf16[64,24,1024]{2,1,0:T(8,128)(2,1)}, bf16[64,24,1024]{2,1,0:T(8,128)(2,1)S(1)}, u32[]{:S(2)}) copy-start(bf16[64,24,1024]{2,1,0:T(8,128)(2,1)S(1)} %all-to-all-done.1) | copy-start | bytes 9437188
  105.7 20.2 %all-to-all-start.2 = ((bf16[16,256,128]{2,1,0:T(8,128)(2,1)}), bf16[16,256,128]{2,1,0:T(8,128)(2,1)}, u32[]{:S(2)}, u32[]{:S(2)}) async-start(bf16[16,256,128]{2,1,0:T(8,128)(2,1)} %bitcast.41), calls=%async_computation.2 | async-start | bytes 2097152 | tf_op jit(solution)/shard_map/all_to_all | solution.py:513
  125.8 19.9 %collective-permute-start.4 = (bf16[384,1024]{1,0:T(8,128)(2,1)}, bf16[384,1024]{1,0:T(8,128)(2,1)S(1)}, u32[]{:S(2)}, u32[]{:S(2)}) collective-permute-start(bf16[384,1024]{1,0:T(8,128)(2,1)} %get-tuple-element.55.refs_0_), channel_id=1, source_target_pairs={{0,64},{64,0},{1,65},{65,1},{2,66},{66,2},{3,67},{67,3},{4,68},{68... | collective-permute-start | bytes 2359304 | tf_op jit(solution)/shard_map/ppermute | solution.py:516
  129.1 8.0 %copy-start.5 = (bf16[384,2048]{1,0:T(8,128)(2,1)S(1)}, bf16[384,2048]{1,0:T(8,128)(2,1)}, u32[]{:S(2)}) copy-start(bf16[384,2048]{1,0:T(8,128)(2,1)} %get-tuple-element.53.refs_1_) | copy-start | bytes 4718596
  135.9 18.5 %copy-start.18 = (bf16[128,2048]{1,0:T(8,128)(2,1)S(1)}, bf16[128,2048]{1,0:T(8,128)(2,1)}, u32[]{:S(2)}) copy-start(bf16[128,2048]{1,0:T(8,128)(2,1)} %get-tuple-element.60) | copy-start | bytes 1572868
  135.9 19.3 %copy-start.12 = (bf16[128,2048]{1,0:T(8,128)(2,1)S(1)}, bf16[128,2048]{1,0:T(8,128)(2,1)}, u32[]{:S(2)}) copy-start(bf16[128,2048]{1,0:T(8,128)(2,1)} %get-tuple-element.51) | copy-start | bytes 1572868
  135.9 19.3 %collective-permute-start.1 = (bf16[128,2048]{1,0:T(8,128)(2,1)}, bf16[128,2048]{1,0:T(8,128)(2,1)S(1)}, u32[]{:S(2)}, u32[]{:S(2)}) collective-permute-start(bf16[128,2048]{1,0:T(8,128)(2,1)} %get-tuple-element.52), channel_id=1, source_target_pairs={{0,2},{2,4},{4,6},{6,0},{1,3},{3,5},{5,7},{7,1},{8,10},{10,12},{12... | collective-permute-start | bytes 1572872 | tf_op jit(solution)/shard_map/ppermute | solution.py:518
  137.1 42.3 %collective-permute-start.3 = (bf16[384,2048]{1,0:T(8,128)(2,1)S(1)}, bf16[384,2048]{1,0:T(8,128)(2,1)S(1)}, u32[]{:S(2)}, u32[]{:S(2)}) collective-permute-start(bf16[384,2048]{1,0:T(8,128)(2,1)S(1)} %copy-done.5), channel_id=1, source_target_pairs={{0,64},{64,0},{1,65},{65,1},{2,66},{66,2},{3,67},{67,3},{4,68},{68... | collective-permute-start | bytes 4718600 | tf_op jit(solution)/shard_map/ppermute | solution.py:516
  145.7 6.8 %copy-start.7 = (bf16[384,1024]{1,0:T(8,128)(2,1)}, bf16[384,1024]{1,0:T(8,128)(2,1)S(1)}, u32[]{:S(2)}) copy-start(bf16[384,1024]{1,0:T(8,128)(2,1)S(1)} %collective-permute-done.4.refs_3_) | copy-start | bytes 2359300
  152.5 10.5 %collective-permute-start.7 = (bf16[128,2048]{1,0:T(8,128)(2,1)}, bf16[128,2048]{1,0:T(8,128)(2,1)S(1)}, u32[]{:S(2)}, u32[]{:S(2)}) collective-permute-start(bf16[128,2048]{1,0:T(8,128)(2,1)} %get-tuple-element.62), channel_id=1, source_target_pairs={{0,6},{2,0},{4,2},{6,4},{1,7},{3,1},{5,3},{7,5},{8,14},{10,8},{12,... | collective-permute-start | bytes 1572872 | tf_op jit(solution)/shard_map/ppermute | solution.py:521
  154.4 26.2 %collective-permute-start.6 = (bf16[128,2048]{1,0:T(8,128)(2,1)S(1)}, bf16[128,2048]{1,0:T(8,128)(2,1)S(1)}, u32[]{:S(2)}, u32[]{:S(2)}) collective-permute-start(bf16[128,2048]{1,0:T(8,128)(2,1)S(1)} %copy-done.18), channel_id=1, source_target_pairs={{0,6},{2,0},{4,2},{6,4},{1,7},{3,1},{5,3},{7,5},{8,14},{10,8},{12,... | collective-permute-start | bytes 1572872 | tf_op jit(solution)/shard_map/ppermute | solution.py:523
  155.4 11.9 %collective-permute-start.2 = (bf16[128,2048]{1,0:T(8,128)(2,1)S(1)}, bf16[128,2048]{1,0:T(8,128)(2,1)S(1)}, u32[]{:S(2)}, u32[]{:S(2)}) collective-permute-start(bf16[128,2048]{1,0:T(8,128)(2,1)S(1)} %add_convert_fusion.2), channel_id=1, source_target_pairs={{0,2},{2,4},{4,6},{6,0},{1,3},{3,5},{5,7},{7,1},{8,10},{10,12},{12... | collective-permute-start | bytes 1572872 | tf_op jit(solution)/shard_map/ppermute | solution.py:524
  156.1 24.5 %collective-permute-start.5 = (bf16[128,2048]{1,0:T(8,128)(2,1)}, bf16[128,2048]{1,0:T(8,128)(2,1)S(1)}, u32[]{:S(2)}, u32[]{:S(2)}) collective-permute-start(bf16[128,2048]{1,0:T(8,128)(2,1)} %get-tuple-element.59), channel_id=1, source_target_pairs={{0,2},{2,4},{4,6},{6,0},{1,3},{3,5},{5,7},{7,1},{8,10},{10,12},{12... | collective-permute-start | bytes 1572872 | tf_op jit(solution)/shard_map/ppermute | solution.py:522
  164.2 21.3 %collective-permute-start.8 = (bf16[128,2048]{1,0:T(8,128)(2,1)S(1)}, bf16[128,2048]{1,0:T(8,128)(2,1)S(1)}, u32[]{:S(2)}, u32[]{:S(2)}) collective-permute-start(bf16[128,2048]{1,0:T(8,128)(2,1)S(1)} %add_convert_fusion.1), channel_id=1, source_target_pairs={{0,6},{2,0},{4,2},{6,4},{1,7},{3,1},{5,3},{7,5},{8,14},{10,8},{12,... | collective-permute-start | bytes 1572872 | tf_op jit(solution)/shard_map/ppermute | solution.py:525
  167.4 18.2 %copy-start.10 = (bf16[128,2048]{1,0:T(8,128)(2,1)}, bf16[128,2048]{1,0:T(8,128)(2,1)S(1)}, u32[]{:S(2)}) copy-start(bf16[128,2048]{1,0:T(8,128)(2,1)S(1)} %collective-permute-done.2.ua) | copy-start | bytes 1572868
  180.6 4.9 %copy-start.9 = (bf16[128,2048]{1,0:T(8,128)(2,1)}, bf16[128,2048]{1,0:T(8,128)(2,1)S(1)}, u32[]{:S(2)}) copy-start(bf16[128,2048]{1,0:T(8,128)(2,1)S(1)} %collective-permute-done.6.da) | copy-start | bytes 1572868
  180.6 4.9 %copy-start.11 = (bf16[128,2048]{1,0:T(8,128)(2,1)}, bf16[128,2048]{1,0:T(8,128)(2,1)S(1)}, u32[]{:S(2)}) copy-start(bf16[128,2048]{1,0:T(8,128)(2,1)S(1)} %collective-permute-done.5.ub) | copy-start | bytes 1572868
  192.7 52.0 %all-to-all-start.3 = ((bf16[64,24,1024]{2,1,0:T(8,128)(2,1)}), bf16[64,24,1024]{2,1,0:T(8,128)(2,1)S(1)}, u32[]{:S(2)}, u32[]{:S(2)}) async-start(bf16[64,24,1024]{2,1,0:T(8,128)(2,1)} %bitcast.38), calls=%async_computation.3 | async-start | bytes 6291456 | tf_op jit(solution)/shard_map/all_to_all | solution.py:530
  204.7 56.9 %collective-permute-start.9 = (bf16[384,1024]{1,0:T(8,128)(2,1)}, bf16[384,1024]{1,0:T(8,128)(2,1)}, u32[]{:S(2)}, u32[]{:S(2)}) collective-permute-start(bf16[384,1024]{1,0:T(8,128)(2,1)} %get-tuple-element.69.refs_2_), channel_id=1, source_target_pairs={{0,64},{64,0},{1,65},{65,1},{2,66},{66,2},{3,67},{67,3},{4,68},{68... | collective-permute-start | bytes 2359304 | tf_op jit(solution)/shard_map/ppermute | solution.py:516
  255.7 10.7 %collective-permute-start.10 = (bf16[384,256]{1,0:T(8,128)(2,1)}, bf16[384,256]{1,0:T(8,128)(2,1)S(1)}, u32[]{:S(2)}, u32[]{:S(2)}) collective-permute-start(bf16[384,256]{1,0:T(8,128)(2,1)} %get-tuple-element.72), channel_id=1, source_target_pairs={{0,64},{64,0},{1,65},{65,1},{2,66},{66,2},{3,67},{67,3},{4,68},{68... | collective-permute-start | bytes 589832 | tf_op jit(solution)/shard_map/ppermute | solution.py:533
  266.4 7.4 %copy-start.14 = (bf16[384,256]{1,0:T(8,128)(2,1)}, bf16[384,256]{1,0:T(8,128)(2,1)S(1)}, u32[]{:S(2)}) copy-start(bf16[384,256]{1,0:T(8,128)(2,1)S(1)} %collective-permute-done.10.hf_ref) | copy-start | bytes 589828
  266.4 72.9 %collective-permute-start.11 = (bf16[4096,256]{1,0:T(8,128)(2,1)}, bf16[4096,256]{1,0:T(8,128)(2,1)}, u32[]{:S(2)}, u32[]{:S(2)}) collective-permute-start(bf16[4096,256]{1,0:T(8,128)(2,1)} %up_half.3), channel_id=1, source_target_pairs={{0,64},{64,0},{1,65},{65,1},{2,66},{66,2},{3,67},{67,3},{4,68},{68... | collective-permute-start | bytes 6291464 | tf_op jit(solution)/shard_map/ppermute | solution.py:538
  273.9 72.8 %all-to-all-start.4 = ((bf16[64,24,1024]{2,1,0:T(8,128)(2,1)}), bf16[64,24,1024]{2,1,0:T(8,128)(2,1)S(1)}, u32[]{:S(2)}, u32[]{:S(2)}) async-start(bf16[64,24,1024]{2,1,0:T(8,128)(2,1)} %bitcast.34), calls=%async_computation.4 | async-start | bytes 6291456 | tf_op jit(solution)/shard_map/all_to_all | solution.py:534
  288.8 50.5 %copy-start.3 = (bf16[4096,256]{1,0:T(8,128)(2,1)S(1)}, bf16[4096,256]{1,0:T(8,128)(2,1)}, u32[]{:S(2)}) copy-start(bf16[4096,256]{1,0:T(8,128)(2,1)} %up_half.2) | copy-start | bytes 6291460
  (5 other events, 7.0 us)

commit v4 on v3

--- a/solution.py
+++ b/solution.py
@@ -31,15 +31,29 @@
 SEQ = ("x", "yl")
 BACK = ("x", "yl", "core")
 ALL = ("x", "yl", "z", "core")
-VMEM_LIMIT = 56 * 1024 * 1024
+VMEM_LIMIT = 24 * 1024 * 1024
 
 
 def params(limit=VMEM_LIMIT):
     return pltpu.CompilerParams(vmem_limit_bytes=limit)
 
 
-def whole(*shape):
-    return pl.BlockSpec(shape, lambda *_: (0,) * len(shape))
+def cost(multiply_adds, transcendentals=0):
+    return pl.CostEstimate(
+        flops=2 * multiply_adds, bytes_accessed=1 << 20, transcendentals=transcendentals
+    )
+
+
+def resident(count):
+    return [pl.BlockSpec(memory_space=pltpu.VMEM)] * count
+
+
+def scalars():
+    return pl.BlockSpec(memory_space=pltpu.SMEM)
+
+
+def array(*shape, dtype=BF):
+    return jax.ShapeDtypeStruct(shape, dtype)
 
 
 def dot_nt(a, b):
@@ -149,43 +163,36 @@
 
 def project(place, half, heads, weight_own, weight_other):
     width = 512
-    blocks = D // 2 // width
 
     def kernel(place_ref, a_ref, wo_ref, ws_ref, *refs):
         lhs = refs[-1]
         core = place_ref[1]
-
-        @pl.when(pl.program_id(0) == 0)
-        def _():
-            for side, c in enumerate((core, 1 - core)):
-                for number, offset in enumerate((2, 1, 3, 0)):
-                    z = lax.rem(place_ref[0] + offset, 4)
-                    for b in range(2):
-                        for h in range(4):
-                            lhs[
-                                number * TOK + b * 64 : number * TOK + (b + 1) * 64,
-                                side * FF + h * HEAD : side * FF + (h + 1) * HEAD,
-                            ] = a_ref[b, h, c, z]
-
-        total = dot_nn(lhs[:, :FF], wo_ref[...]) + dot_nn(lhs[:, FF:], ws_ref[...])
-        for number in range(4):
-            refs[number][...] = total[number * TOK : (number + 1) * TOK].astype(BF)
-
-    weights = pl.BlockSpec((FF, width), lambda n, _: (0, half * blocks + n))
-    return pl.pallas_call(
-        kernel,
-        grid_spec=pltpu.PrefetchScalarGridSpec(
-            num_scalar_prefetch=1,
-            grid=(blocks,),
-            in_specs=[whole(2, 4, 2, 4, 64, HEAD), weights, weights],
-            out_specs=[pl.BlockSpec((TOK, width), lambda n, _: (0, n))] * 4,
-            scratch_shapes=[pltpu.VMEM((4 * TOK, 2 * FF), BF)],
-        ),
-        out_shape=[jax.ShapeDtypeStruct((TOK, D // 2), BF)] * 4,
-        compiler_params=params(),
-        cost_estimate=pl.CostEstimate(
-            flops=512 * 1024 * D, bytes_accessed=7 << 20, transcendentals=0
-        ),
+        for side, c in enumerate((core, 1 - core)):
+            for number, offset in enumerate((2, 1, 3, 0)):
+                z = lax.rem(place_ref[0] + offset, 4)
+                for b in range(2):
+                    for h in range(4):
+                        lhs[
+                            number * TOK + b * 64 : number * TOK + (b + 1) * 64,
+                            side * FF + h * HEAD : side * FF + (h + 1) * HEAD,
+                        ] = a_ref[b, h, c, z]
+
+        @pl.loop(0, D // 2 // width)
+        def _(n):
+            near = pl.ds(pl.multiple_of(n * width, width), width)
+            cut = pl.ds(pl.multiple_of(half * (D // 2) + n * width, width), width)
+            total = dot_nn(lhs[:, :FF], wo_ref[:, cut]) + dot_nn(lhs[:, FF:], ws_ref[:, cut])
+            for number in range(4):
+                refs[number][:, near] = total[number * TOK : (number + 1) * TOK].astype(BF)
+
+    return pl.pallas_call(
+        kernel,
+        in_specs=[scalars()] + resident(3),
+        out_specs=resident(4),
+        scratch_shapes=[pltpu.VMEM((4 * TOK, 2 * FF), BF)],
+        out_shape=[array(TOK, D // 2)] * 4,
+        compiler_params=params(),
+        cost_estimate=cost(512 * 1024 * D // 2),
         name="project",
     )(place, heads, weight_own, weight_other)
 
@@ -247,9 +254,8 @@
 
     return pl.pallas_call(
         kernel,
-        grid=(1,),
-        in_specs=[whole(TOK, D), whole(2, D), whole(2, TOK), whole(2, TOK)],
-        out_specs=whole(CB * SLOTS, CW),
+        in_specs=resident(4),
+        out_specs=resident(1)[0],
         out_shape=jax.ShapeDtypeStruct((CB * SLOTS, CW), BF),
         scratch_shapes=[pltpu.VMEM((CB, SLOTS, CW), BF)],
         compiler_params=params(),
@@ -276,10 +282,8 @@
 
     return pl.pallas_call(
         kernel,
-        grid=(1,),
-        in_specs=[whole(TOK, D // 2)] * 6
-        + [whole(TOK, D), whole(1, D), whole(2, TOK)],
-        out_specs=[whole(TOK, D), whole(CB * SLOTS, CW)],
+        in_specs=resident(9),
+        out_specs=resident(2),
         out_shape=[
             jax.ShapeDtypeStruct((TOK, D), F32),
             jax.ShapeDtypeStruct((CB * SLOTS, CW), BF),
@@ -304,9 +308,8 @@
 
     return pl.pallas_call(
         kernel,
-        grid=(1,),
-        in_specs=[whole(CB * SLOTS, CW), whole(FF, D)],
-        out_specs=[whole(SLOTS, w) for w in GRAD_WIDTHS] + [whole(SLOTS, FF)],
+        in_specs=resident(2),
+        out_specs=resident(4),
         out_shape=[jax.ShapeDtypeStruct((SLOTS, w), BF) for w in GRAD_WIDTHS]
         + [jax.ShapeDtypeStruct((SLOTS, FF), F32)],
         scratch_shapes=[pltpu.VMEM((CB, SLOTS, CW), BF)],
@@ -322,102 +325,64 @@
 
 
 def hidden_units(place, chunks, up, back):
-    def kernel(place_ref, i_ref, up_ref, b_ref, x_ref, hid_ref, ho_ref, hs_ref, pg_ref, pre):
-        i = pl.program_id(0)
-
-        @pl.when(i == 0)
-        def _():
-            mix_in(i_ref, x_ref)
-            pre[...] = dot_nn(x_ref[0], up_ref[...])
-
-        @pl.when(i > 0)
-        def _():
-            pre[...] += dot_nn(x_ref[i], up_ref[...])
-
-        @pl.when(i == CB - 1)
-        def _():
-            act, slope = gelu_pair(pre[...])
-            hid_ref[...] = act.astype(BF)
-            pg_ref[...] = (b_ref[...] * slope).astype(BF)
-            low, high = act[:, :HALF].astype(BF), act[:, HALF:].astype(BF)
-            mine = place_ref[2] == 0
-            hs_ref[...] = jnp.where(mine, low, high)
-            ho_ref[...] = jnp.where(mine, high, low)
-
-    return pl.pallas_call(
-        kernel,
-        grid_spec=pltpu.PrefetchScalarGridSpec(
-            num_scalar_prefetch=1,
-            grid=(CB,),
-            in_specs=[
-                whole(CB * SLOTS, CW),
-                pl.BlockSpec((CW, FF), lambda i, _: (i, 0)),
-                whole(SLOTS, FF),
-            ],
-            out_specs=[
-                whole(CB, SLOTS, CW),
-                whole(SLOTS, FF),
-                whole(SLOTS, HALF),
-                whole(SLOTS, HALF),
-                whole(SLOTS, FF),
-            ],
-            scratch_shapes=[pltpu.VMEM((SLOTS, FF), F32)],
-        ),
-        out_shape=[
-            jax.ShapeDtypeStruct((CB, SLOTS, CW), BF),
-            jax.ShapeDtypeStruct((SLOTS, FF), BF),
-            jax.ShapeDtypeStruct((SLOTS, HALF), BF),
-            jax.ShapeDtypeStruct((SLOTS, HALF), BF),
-            jax.ShapeDtypeStruct((SLOTS, FF), BF),
-        ],
-        compiler_params=params(),
+    def kernel(place_ref, i_ref, up_ref, b_ref, x_ref, hid_ref, ho_ref, hs_ref, po_ref, ps_ref):
+        mix_in(i_ref, x_ref)
+        pre = None
+        for c in range(CB):
+            part = dot_nn(x_ref[c], up_ref[c * CW : (c + 1) * CW, :])
+            pre = part if pre is None else pre + part
+        act, slope = gelu_pair(pre)
+        hidden, grad = act.astype(BF), (b_ref[...] * slope).astype(BF)
+        hid_ref[...] = hidden
+        mine = place_ref[2] == 0
+        for value, other, own in ((hidden, ho_ref, hs_ref), (grad, po_ref, ps_ref)):
+            low, high = value[:, :HALF], value[:, HALF:]
+            own[...] = jnp.where(mine, low, high)
+            other[...] = jnp.where(mine, high, low)
+
+    return pl.pallas_call(
+        kernel,
+        in_specs=[scalars()] + resident(3),
+        out_specs=resident(6),
+        out_shape=[array(CB, SLOTS, CW), array(SLOTS, FF)] + [array(SLOTS, HALF)] * 4,
+        compiler_params=params(),
+        cost_estimate=cost(SLOTS * D * FF, SLOTS * FF),
         name="hidden_units",
     )(place, chunks, up, back)
 
 
 def expert_out(hidden, down):
     def kernel(h_ref, down_ref, o_ref, prod):
-        i = pl.program_id(0)
-        prod[i] = dot_nn(h_ref[...], down_ref[...]).astype(BF)
-
-        @pl.when(i == CB - 1)
-        def _():
-            mix_out(prod, o_ref)
-
-    return pl.pallas_call(
-        kernel,
-        grid=(CB,),
-        in_specs=[whole(SLOTS, FF), pl.BlockSpec((FF, CW), lambda i: (0, i))],
-        out_specs=whole(CB * SLOTS, CW),
-        out_shape=jax.ShapeDtypeStruct((CB * SLOTS, CW), BF),
+        for c in range(CB):
+            prod[c] = dot_nn(h_ref[...], down_ref[:, c * CW : (c + 1) * CW]).astype(BF)
+        mix_out(prod, o_ref)
+
+    return pl.pallas_call(
+        kernel,
+        in_specs=resident(2),
+        out_specs=resident(1)[0],
+        out_shape=array(CB * SLOTS, CW),
         scratch_shapes=[pltpu.VMEM((CB, SLOTS, CW), BF)],
         compiler_params=params(),
+        cost_estimate=cost(SLOTS * D * FF),
         name="expert_out",
     )(hidden, down)
 
 
-def up_half(half, rows, pre_grad):
-    def kernel(half_ref, x_ref, p_ref, o_ref):
-        o_ref[...] = dot_tn(x_ref[0], p_ref[...]).astype(BF)
-
-    return pl.pallas_call(
-        kernel,
-        grid_spec=pltpu.PrefetchScalarGridSpec(
-            num_scalar_prefetch=1,
-            grid=(CB,),
-            in_specs=[
-                pl.BlockSpec((1, SLOTS, CW), lambda c, _: (c, 0, 0)),
-                pl.BlockSpec((SLOTS, HALF), lambda c, half_ref: (0, half_ref[0])),
-            ],
-            out_specs=pl.BlockSpec((CW, HALF), lambda c, _: (c, 0)),
-        ),
-        out_shape=jax.ShapeDtypeStruct((D, HALF), BF),
-        compiler_params=params(),
-        cost_estimate=pl.CostEstimate(
-            flops=2 * SLOTS * D * HALF, bytes_accessed=6 << 20, transcendentals=0
-        ),
+def up_half(rows, pre_grad):
+    def kernel(x_ref, p_ref, o_ref):
+        for c in range(CB):
+            o_ref[c * CW : (c + 1) * CW, :] = dot_tn(x_ref[c], p_ref[...]).astype(BF)
+
+    return pl.pallas_call(
+        kernel,
+        in_specs=resident(2),
+        out_specs=resident(1)[0],
+        out_shape=array(D, HALF),
+        compiler_params=params(),
+        cost_estimate=cost(SLOTS * D * HALF),
         name="up_half",
-    )(half, rows, pre_grad)
+    )(rows, pre_grad)
 
 
 def down_sum(hidden, grads, hidden_far, grads_far):
@@ -431,14 +396,11 @@
 
     return pl.pallas_call(
         kernel,
-        grid=(1,),
-        in_specs=[whole(SLOTS, HALF)] * 2 + [whole(SLOTS, w) for w in GRAD_WIDTHS] * 2,
-        out_specs=whole(HALF, D),
-        out_shape=jax.ShapeDtypeStruct((HALF, D), BF),
-        compiler_params=params(),
-        cost_estimate=pl.CostEstimate(
-            flops=4 * SLOTS * D * HALF, bytes_accessed=9 << 20, transcendentals=0
-        ),
+        in_specs=resident(8),
+        out_specs=resident(1)[0],
+        out_shape=array(HALF, D),
+        compiler_params=params(),
+        cost_estimate=cost(2 * SLOTS * D * HALF),
         name="down_sum",
     )(hidden, hidden_far, *grads, *grads_far)
 
@@ -456,9 +418,8 @@
 
     return pl.pallas_call(
         kernel,
-        grid=(1,),
-        in_specs=[whole(CB * SLOTS, CW), whole(TOK, D), whole(2, D), whole(2, TOK), whole(TOK, 2)],
-        out_specs=whole(TOK, D),
+        in_specs=resident(5),
+        out_specs=resident(1)[0],
         out_shape=jax.ShapeDtypeStruct((TOK, D), BF),
         scratch_shapes=[pltpu.VMEM((CB, SLOTS, CW), BF)],
         compiler_params=params(),
@@ -512,7 +473,7 @@
     heads, grad_arrived = lax.optimization_barrier((heads, grad_arrived))
     heads = exchange(heads, BACK).reshape(2, 4, 2, 4, 64, HEAD)
     *grads, back = grads_in(grad_arrived, down_weight[0])
-    heads, grads, back = lax.optimization_barrier((heads, grads, back))
+    heads, back = lax.optimization_barrier((heads, back))
     far_0, far_1, far_2 = [lax.ppermute(g, "dp", swap) for g in grads]
     fa, ua, da, own_a = project(place, 0, heads, out_weight, weight_other)
     fa = lax.ppermute(fa, "z", above)
@@ -529,16 +490,19 @@
     )
     arrived = exchange(chunks, ALL)
 
-    own_rows, hidden, hid_other, hid_own, pre_grad = hidden_units(place, arrived, up_weight[0], back)
+    own_rows, hidden, hid_other, hid_own, pre_other, pre_own = hidden_units(
+        place, arrived, up_weight[0], back
+    )
+    hid_other, far_2 = lax.optimization_barrier((hid_other, far_2))
     hid_far = lax.ppermute(hid_other, "dp", swap)
     returned = exchange(expert_out(hidden, down_weight[0]), ALL)
-    own_rows, pre_grad, far_2 = lax.optimization_barrier((own_rows, pre_grad, far_2))
-    up_other = up_half((1 - dp)[None].astype(jnp.int32), own_rows, pre_grad)
-    up_other, hid_far = lax.optimization_barrier((up_other, hid_far))
+    pre_other, hid_far = lax.optimization_barrier((pre_other, hid_far))
+    up_other = up_half(own_rows, pre_other)
     up_far = lax.ppermute(up_other, "dp", swap)
-    up_own = up_half(dp[None].astype(jnp.int32), own_rows, pre_grad)
+    up_own = up_half(own_rows, pre_own)
     down_total = down_sum(hid_own, grads, hid_far, (far_0, far_1, far_2))
     block_out = combine(returned, stream, gate, target, weight_col)
+    block_out, up_far = lax.optimization_barrier((block_out, up_far))
     up_total = plus(up_own, up_far)
     return (block_out.reshape(2, TOK // 2, D), up_total[None], down_total[None])
 

time: 356 us -> 361 us (1.014)
  Pallas kernels: 101 us -> 63 us
  local copies, waits for them, and re-layouts: 8.43 us -> 33 us
  waiting for transfers between devices: 180 us -> 202 us
    ppermute x1, waiting for transfers between devices: 0.01 us -> 41.2 us  [body(): hid_far = lax.ppermute(hid_other, 'dp', swap)]
    pallas_call x11, Pallas kernels: 70.4 us -> 37.2 us  [the longest x2 11.6 us: project(): pl.pallas_call(kernel, in_specs=[scalars()] + resident(3), out_specs=resi...]
    unnamed x42 -> x86, local copies, waits for them, and re-layouts: 7.26 us -> 32.4 us
    ppermute x1, waiting for transfers between devices: 43.7 us -> 34.7 us  [body(): up_far = lax.ppermute(up_other, 'dp', swap)]
    ppermute x3, waiting for transfers between devices: 23.6 us -> 17.6 us  [body(): far_0, far_1, far_2 = [lax.ppermute(g, 'dp', swap) for g in grads]]
    all_to_all x1, waiting for transfers between devices: 3.9 us -> 0.01 us  [body(): returned = exchange(expert_out(hidden, down_weight[0]), ALL)]
    all_to_all x1, waiting for transfers between devices: 9.21 us -> 5.39 us  [body(): heads = exchange(heads, BACK).reshape(2, 4, 2, 4, 64, HEAD)]
  transfers between devices with their start and end apart: 17 -> 17, of which waited for: 11 -> 10; matrix products, arithmetic and copies ran while one was open for 2% -> 0% of each run, Pallas kernels for 24% -> 16%
where the time goes in v4:
time: 361 us; the launch traced here: 359 us
  waiting for transfers between devices  202 us (56%)
  Pallas kernels  63 us (17%)
  starting transfers between devices  55.7 us (15%)
  local copies, waits for them, and re-layouts  33 us (9%)
  other arithmetic  4.09 us (1%)
    ppermute x1, waiting for transfers between devices, body(): hid_far = lax.ppermute(hid_other, 'dp', swap)  41.2 us
    all_to_all x1, waiting for transfers between devices, body(): arrived = exchange(chunks, ALL)  37.9 us
    all_to_all x1, waiting for transfers between devices, body(): rows = exchange(pack(queries, keys, values), SEQ)  37.6 us
    ppermute x1, waiting for transfers between devices, body(): up_far = lax.ppermute(up_other, 'dp', swap)  34.7 us
    unnamed x86, local copies, waits for them, and re-layouts  32.4 us
    pallas_call x1, Pallas kernels, attend(): pl.pallas_call(kernel, grid=(8,), in_specs=[pl.BlockSpec((1, 1, 512, HEAD...  23.4 us
    ppermute x3, waiting for transfers between devices, body(): far_0, far_1, far_2 = [lax.ppermute(g, 'dp', swap) for g in grads]  17.6 us
    all_to_all x1, waiting for transfers between devices, body(): grad_arrived = exchange(grad_chunks, ALL)  13.7 us
  transfers between devices with their start and end apart: 17, of which 10 were waited for; matrix products, arithmetic and copies ran while one was open for 0% of the time, Pallas kernels for 16%

profile of v4, /device:TPU:1, one launch (start us, length us, event | category | flops | bytes accessed | tf_op | source)
XLA Modules:
  0.0 359.1 jit_solution(6286938018509796343)
XLA Ops:
  4.3 2.4 pack_heads.1
  6.7 6.0 %all-to-all-start = ((bf16[8,3,512,128]{3,2,1,0:T(8,128)(2,1)}), bf16[8,3,512,128]{3,2,1,0:T(8,128)(2,1)S(1)}, u32[]{:S(2)}, u32[]{:S(2)}) async-start(bf16[8,3,512,128]{3,2,1,0:T(8,128)(2,1)} %pack_heads.1), calls=%async_computation | async-start | bytes 6291456 | tf_op jit(solution)/shard_map/all_to_all | solution.py:465
  19.9 37.6 %all-to-all-done.q_ref.qn_ref.k_ref.v_ref = bf16[8,3,512,128]{3,2,1,0:T(8,128)(2,1)S(1)} async-done(((bf16[8,3,512,128]{3,2,1,0:T(8,128)(2,1)}), bf16[8,3,512,128]{3,2,1,0:T(8,128)(2,1)S(1)}, u32[]{:S(2)}, u32[]{:S(2)}) %all-to-all-start) | async-done | bytes 3145760 | tf_op jit(solution)/shard_map/all_to_all | solution.py:465
  59.2 8.1 %all-to-all-start.1 = ((bf16[64,24,1024]{2,1,0:T(8,128)(2,1)}), bf16[64,24,1024]{2,1,0:T(8,128)(2,1)S(1)}, u32[]{:S(2)}, u32[]{:S(2)}) async-start(bf16[64,24,1024]{2,1,0:T(8,128)(2,1)} %bitcast.35), calls=%async_computation.1 | async-start | bytes 6291456 | tf_op jit(solution)/shard_map/all_to_all | solution.py:470
  69.3 23.4 %attend.1 = bf16[8,2,4,64,128]{4,3,2,1,0:T(8,128)(2,1)S(1)} custom-call(bf16[8,3,512,128]{3,2,1,0:T(8,128)(2,1)S(1)} %copy-done.11, bf16[8,3,512,128]{3,2,1,0:T(8,128)(2,1)S(1)} %copy-done.11, bf16[8,3,512,128]{3,2,1,0:T(8,128)(2,1)S(1)} %copy-done.11, bf16[8,3,512,128]{3,2,1,0:T(8,128)(2,1)S(1)} %copy-done.11), custom_call_target="tpu_custom_call" | custom-call | flops 17179869184 | bytes 4194304 | tf_op jit(solution)/shard_map/attend/pallas_call | solution.py:140
  93.7 13.7 %all-to-all-done.1 = bf16[64,24,1024]{2,1,0:T(8,128)(2,1)S(1)} async-done(((bf16[64,24,1024]{2,1,0:T(8,128)(2,1)}), bf16[64,24,1024]{2,1,0:T(8,128)(2,1)S(1)}, u32[]{:S(2)}, u32[]{:S(2)}) %all-to-all-start.1) | async-done | bytes 3145760 | tf_op jit(solution)/shard_map/all_to_all | solution.py:470
  107.4 4.3 %all-to-all-start.2 = ((bf16[16,256,128]{2,1,0:T(8,128)(2,1)}), bf16[16,256,128]{2,1,0:T(8,128)(2,1)}, u32[]{:S(2)}, u32[]{:S(2)}) async-start(bf16[16,256,128]{2,1,0:T(8,128)(2,1)} %bitcast.39), calls=%async_computation.2 | async-start | bytes 2097152 | tf_op jit(solution)/shard_map/all_to_all | solution.py:474
  113.8 2.6 grads_in.1
  119.5 2.6 collective-permute-start.4
  122.2 5.4 %all-to-all-done.2 = bf16[16,256,128]{2,1,0:T(8,128)(2,1)} async-done(((bf16[16,256,128]{2,1,0:T(8,128)(2,1)}), bf16[16,256,128]{2,1,0:T(8,128)(2,1)}, u32[]{:S(2)}, u32[]{:S(2)}) %all-to-all-start.2) | async-done | bytes 1048608 | tf_op jit(solution)/shard_map/all_to_all | solution.py:474
  129.7 5.7 %project.2 = (bf16[128,2048]{1,0:T(8,128)(2,1)S(1)}, bf16[128,2048]{1,0:T(8,128)(2,1)S(1)}, bf16[128,2048]{1,0:T(8,128)(2,1)S(1)}, bf16[128,2048]{1,0:T(8,128)(2,1)S(1)}) custom-call(s32[3]{0:T(128)S(1)} %pad_add_fusion.place_ref, bf16[2,4,2,4,64,128]{5,4,3,2,1,0:T(8,128)(2,1)} %bitcast.12.a_ref, bf16[512,4096]{1,0:T(8,128)(2,1)S(1)} %copy-done, ...), custom_call_target="tpu_custom_call" | custom-call | flops 2147483648 | bytes 1048576 | tf_op jit(solution)/shard_map/project/pallas_call | solution.py:188
  136.6 2.6 collective-permute-start.3
  139.3 5.6 %collective-permute-done.4.refs_3_ = bf16[384,1024]{1,0:T(8,128)(2,1)S(1)} collective-permute-done((bf16[384,1024]{1,0:T(8,128)(2,1)}, bf16[384,1024]{1,0:T(8,128)(2,1)S(1)}, u32[]{:S(2)}, u32[]{:S(2)}) %collective-permute-start.4) | collective-permute-done | bytes 786464 | tf_op jit(solution)/shard_map/ppermute | solution.py:477
  144.9 5.9 %project.3 = (bf16[128,2048]{1,0:T(8,128)(2,1)S(1)}, bf16[128,2048]{1,0:T(8,128)(2,1)S(1)}, bf16[128,2048]{1,0:T(8,128)(2,1)S(1)}, bf16[128,2048]{1,0:T(8,128)(2,1)S(1)}) custom-call(s32[3]{0:T(128)S(1)} %pad_add_fusion.place_ref, bf16[2,4,2,4,64,128]{5,4,3,2,1,0:T(8,128)(2,1)} %bitcast.12.a_ref, bf16[512,4096]{1,0:T(8,128)(2,1)S(1)} %copy-done, ...), custom_call_target="tpu_custom_call" | custom-call | flops 2147483648 | bytes 1048576 | tf_op jit(solution)/shard_map/project/pallas_call | solution.py:188
  152.9 2.7 collective-permute-start.6
  155.7 7.4 %collective-permute-done.7 = bf16[128,2048]{1,0:T(8,128)(2,1)S(1)} collective-permute-done((bf16[128,2048]{1,0:T(8,128)(2,1)S(1)}, bf16[128,2048]{1,0:T(8,128)(2,1)S(1)}, u32[]{:S(2)}, u32[]{:S(2)}) %collective-permute-start.7) | collective-permute-done | bytes 524320 | tf_op jit(solution)/shard_map/ppermute | solution.py:482
  163.2 3.4 collective-permute-start.8
  166.6 11.9 %collective-permute-done.3.refs_4_ = bf16[384,2048]{1,0:T(8,128)(2,1)S(1)} collective-permute-done((bf16[384,2048]{1,0:T(8,128)(2,1)S(1)}, bf16[384,2048]{1,0:T(8,128)(2,1)S(1)}, u32[]{:S(2)}, u32[]{:S(2)}) %collective-permute-start.3) | collective-permute-done | bytes 1572896 | tf_op jit(solution)/shard_map/ppermute | solution.py:477
  178.6 7.0 %collective-permute-done.8.db = bf16[128,2048]{1,0:T(8,128)(2,1)S(1)} collective-permute-done((bf16[128,2048]{1,0:T(8,128)(2,1)S(1)}, bf16[128,2048]{1,0:T(8,128)(2,1)S(1)}, u32[]{:S(2)}, u32[]{:S(2)}) %collective-permute-start.8) | collective-permute-done | bytes 524320 | tf_op jit(solution)/shard_map/ppermute | solution.py:486
  185.6 2.6 norm_send.1
  191.1 9.1 %all-to-all-start.3 = ((bf16[64,24,1024]{2,1,0:T(8,128)(2,1)}), bf16[64,24,1024]{2,1,0:T(8,128)(2,1)S(1)}, u32[]{:S(2)}, u32[]{:S(2)}) async-start(bf16[64,24,1024]{2,1,0:T(8,128)(2,1)} %bitcast.37), calls=%async_computation.3 | async-start | bytes 6291456 | tf_op jit(solution)/shard_map/all_to_all | solution.py:491
  202.3 37.9 %all-to-all-done.3 = bf16[64,24,1024]{2,1,0:T(8,128)(2,1)S(1)} async-done(((bf16[64,24,1024]{2,1,0:T(8,128)(2,1)}), bf16[64,24,1024]{2,1,0:T(8,128)(2,1)S(1)}, u32[]{:S(2)}, u32[]{:S(2)}) %all-to-all-start.3) | async-done | bytes 3145760 | tf_op jit(solution)/shard_map/all_to_all | solution.py:491
  243.5 3.5 hidden_units.1
  247.0 2.6 expert_out.1
  251.3 7.1 %all-to-all-start.4 = ((bf16[64,24,1024]{2,1,0:T(8,128)(2,1)}), bf16[64,24,1024]{2,1,0:T(8,128)(2,1)S(1)}, u32[]{:S(2)}, u32[]{:S(2)}) async-start(bf16[64,24,1024]{2,1,0:T(8,128)(2,1)} %bitcast.33), calls=%async_computation.4 | async-start | bytes 6291456 | tf_op jit(solution)/shard_map/all_to_all | solution.py:498
  258.5 2.4 collective-permute-start.10
  260.9 41.2 %collective-permute-done.10.hf_ref = bf16[384,256]{1,0:T(8,128)(2,1)S(1)} collective-permute-done((bf16[384,256]{1,0:T(8,128)(2,1)}, bf16[384,256]{1,0:T(8,128)(2,1)S(1)}, u32[]{:S(2)}, u32[]{:S(2)}) %collective-permute-start.10) | collective-permute-done | bytes 196640 | tf_op jit(solution)/shard_map/ppermute | solution.py:497
  304.8 2.7 up_half.2
  311.2 5.0 %down_sum.1 = bf16[256,4096]{1,0:T(8,128)(2,1)} custom-call(bf16[384,256]{1,0:T(8,128)(2,1)S(1)} %get-tuple-element.72.h_ref, bf16[384,256]{1,0:T(8,128)(2,1)S(1)} %collective-permute-done.10.hf_ref, bf16[384,1024]{1,0:T(8,128)(2,1)} %get-tuple-element.51.refs_0_, bf16[384,2048]{1,0:T(8,128)(2,1)S(1)} %copy-done.17, bf16[384,1024]{1,0:T(8,128)(2,1)S(1)} %copy-done.27, ...), custom_call_target="tpu_custom_call" | custom-call | flops 1610612736 | bytes 1048576 | tf_op jit(solution)/shard_map/down_sum/pallas_call | solution.py:397
  317.8 3.1 combine.1
  321.0 34.7 %collective-permute-done.11 = bf16[4096,256]{1,0:T(8,128)(2,1)} collective-permute-done((bf16[4096,256]{1,0:T(8,128)(2,1)}, bf16[4096,256]{1,0:T(8,128)(2,1)}, u32[]{:S(2)}, u32[]{:S(2)}) %collective-permute-start.11) | collective-permute-done | bytes 2097184 | tf_op jit(solution)/shard_map/ppermute | solution.py:501
  355.7 3.4 fusion
  (121 shorter events, 44.5 us)
Async XLA Ops:
  6.7 7.0 %copy-start.39 = (s32[2,64,2]{1,2,0:T(2,128)S(1)}, s32[2,64,2]{1,2,0:T(2,128)}, u32[]{:S(2)}) copy-start(s32[2,64,2]{1,2,0:T(2,128)} %param.19) | copy-start | bytes 3076
  6.7 7.8 %copy-start.40 = (f32[2,64,2]{1,2,0:T(2,128)S(1)}, f32[2,64,2]{1,2,0:T(2,128)}, u32[]{:S(2)}) copy-start(f32[2,64,2]{1,2,0:T(2,128)} %param.20) | copy-start | bytes 3076
  6.7 8.0 %copy-start.41 = (s32[2]{0:T(128)S(1)}, s32[2]{0:T(128)}, u32[]{:S(2)}) copy-start(s32[2]{0:T(128)} %param.21) | copy-start | bytes 28
  6.7 8.1 %copy-start.38 = (f32[2,4096]{1,0:T(2,128)S(1)}, f32[2,4096]{1,0:T(2,128)}, u32[]{:S(2)}) copy-start(f32[2,4096]{1,0:T(2,128)} %param.22) | copy-start | bytes 98308
  6.7 50.8 %all-to-all-start = ((bf16[8,3,512,128]{3,2,1,0:T(8,128)(2,1)}), bf16[8,3,512,128]{3,2,1,0:T(8,128)(2,1)S(1)}, u32[]{:S(2)}, u32[]{:S(2)}) async-start(bf16[8,3,512,128]{3,2,1,0:T(8,128)(2,1)} %pack_heads.1), calls=%async_computation | async-start | bytes 6291456 | tf_op jit(solution)/shard_map/all_to_all | solution.py:465
  12.7 114.8 %collective-permute-start = (bf16[512,4096]{1,0:T(8,128)(2,1)}, bf16[512,4096]{1,0:T(8,128)(2,1)}, u32[]{:S(2)}, u32[]{:S(2)}) collective-permute-start(bf16[512,4096]{1,0:T(8,128)(2,1)} %wo_ref.3), channel_id=1, source_target_pairs={{0,1},{1,0},{2,3},{3,2},{4,5},{5,4},{6,7},{7,6},{8,9},{9,8},{10,11... | collective-permute-start | bytes 12582920 | tf_op jit(solution)/shard_map/ppermute | solution.py:466
  59.2 48.1 %all-to-all-start.1 = ((bf16[64,24,1024]{2,1,0:T(8,128)(2,1)}), bf16[64,24,1024]{2,1,0:T(8,128)(2,1)S(1)}, u32[]{:S(2)}, u32[]{:S(2)}) async-start(bf16[64,24,1024]{2,1,0:T(8,128)(2,1)} %bitcast.35), calls=%async_computation.1 | async-start | bytes 6291456 | tf_op jit(solution)/shard_map/all_to_all | solution.py:470
  107.4 20.2 %all-to-all-start.2 = ((bf16[16,256,128]{2,1,0:T(8,128)(2,1)}), bf16[16,256,128]{2,1,0:T(8,128)(2,1)}, u32[]{:S(2)}, u32[]{:S(2)}) async-start(bf16[16,256,128]{2,1,0:T(8,128)(2,1)} %bitcast.39), calls=%async_computation.2 | async-start | bytes 2097152 | tf_op jit(solution)/shard_map/all_to_all | solution.py:474
  119.5 25.4 %collective-permute-start.4 = (bf16[384,1024]{1,0:T(8,128)(2,1)}, bf16[384,1024]{1,0:T(8,128)(2,1)S(1)}, u32[]{:S(2)}, u32[]{:S(2)}) collective-permute-start(bf16[384,1024]{1,0:T(8,128)(2,1)} %get-tuple-element.51.refs_0_), channel_id=1, source_target_pairs={{0,64},{64,0},{1,65},{65,1},{2,66},{66,2},{3,67},{67,3},{4,68},{68... | collective-permute-start | bytes 2359304 | tf_op jit(solution)/shard_map/ppermute | solution.py:477
  129.7 6.9 %copy-start.16 = (bf16[384,2048]{1,0:T(8,128)(2,1)S(1)}, bf16[384,2048]{1,0:T(8,128)(2,1)}, u32[]{:S(2)}) copy-start(bf16[384,2048]{1,0:T(8,128)(2,1)} %copy-done.15) | copy-start | bytes 4718596
  135.5 20.1 %collective-permute-start.1 = (bf16[128,2048]{1,0:T(8,128)(2,1)S(1)}, bf16[128,2048]{1,0:T(8,128)(2,1)S(1)}, u32[]{:S(2)}, u32[]{:S(2)}) collective-permute-start(bf16[128,2048]{1,0:T(8,128)(2,1)S(1)} %get-tuple-element.48), channel_id=1, source_target_pairs={{0,2},{2,4},{4,6},{6,0},{1,3},{3,5},{5,7},{7,1},{8,10},{10,12},{12... | collective-permute-start | bytes 1572872 | tf_op jit(solution)/shard_map/ppermute | solution.py:479
  136.6 41.9 %collective-permute-start.3 = (bf16[384,2048]{1,0:T(8,128)(2,1)S(1)}, bf16[384,2048]{1,0:T(8,128)(2,1)S(1)}, u32[]{:S(2)}, u32[]{:S(2)}) collective-permute-start(bf16[384,2048]{1,0:T(8,128)(2,1)S(1)} %copy-done.16), channel_id=1, source_target_pairs={{0,64},{64,0},{1,65},{65,1},{2,66},{66,2},{3,67},{67,3},{4,68},{68... | collective-permute-start | bytes 4718600 | tf_op jit(solution)/shard_map/ppermute | solution.py:477
  144.9 5.9 %copy-start.28 = (bf16[384,1024]{1,0:T(8,128)(2,1)}, bf16[384,1024]{1,0:T(8,128)(2,1)S(1)}, u32[]{:S(2)}) copy-start(bf16[384,1024]{1,0:T(8,128)(2,1)S(1)} %collective-permute-done.4.refs_3_) | copy-start | bytes 2359300
  150.8 34.8 %copy-start.20 = (bf16[2,64,4096]{2,1,0:T(8,128)(2,1)S(1)}, bf16[2,64,4096]{2,1,0:T(8,128)(2,1)}, u32[]{:S(2)}) copy-start(bf16[2,64,4096]{2,1,0:T(8,128)(2,1)} %param.16) | copy-start | bytes 3145732
  150.8 34.8 %copy-start.36 = (f32[4096]{0:T(1024)S(1)}, f32[4096]{0:T(1024)}, u32[]{:S(2)}) copy-start(f32[4096]{0:T(1024)} %param.18) | copy-start | bytes 49156
  150.8 12.3 %collective-permute-start.7 = (bf16[128,2048]{1,0:T(8,128)(2,1)S(1)}, bf16[128,2048]{1,0:T(8,128)(2,1)S(1)}, u32[]{:S(2)}, u32[]{:S(2)}) collective-permute-start(bf16[128,2048]{1,0:T(8,128)(2,1)S(1)} %get-tuple-element.58), channel_id=1, source_target_pairs={{0,6},{2,0},{4,2},{6,4},{1,7},{3,1},{5,3},{7,5},{8,14},{10,8},{12,... | collective-permute-start | bytes 1572872 | tf_op jit(solution)/shard_map/ppermute | solution.py:482
  152.8 25.7 %collective-permute-start.5 = (bf16[128,2048]{1,0:T(8,128)(2,1)S(1)}, bf16[128,2048]{1,0:T(8,128)(2,1)S(1)}, u32[]{:S(2)}, u32[]{:S(2)}) collective-permute-start(bf16[128,2048]{1,0:T(8,128)(2,1)S(1)} %get-tuple-element.55), channel_id=1, source_target_pairs={{0,2},{2,4},{4,6},{6,0},{1,3},{3,5},{5,7},{7,1},{8,10},{10,12},{12... | collective-permute-start | bytes 1572872 | tf_op jit(solution)/shard_map/ppermute | solution.py:483
  152.9 25.7 %collective-permute-start.6 = (bf16[128,2048]{1,0:T(8,128)(2,1)S(1)}, bf16[128,2048]{1,0:T(8,128)(2,1)S(1)}, u32[]{:S(2)}, u32[]{:S(2)}) collective-permute-start(bf16[128,2048]{1,0:T(8,128)(2,1)S(1)} %get-tuple-element.56), channel_id=1, source_target_pairs={{0,6},{2,0},{4,2},{6,4},{1,7},{3,1},{5,3},{7,5},{8,14},{10,8},{12,... | collective-permute-start | bytes 1572872 | tf_op jit(solution)/shard_map/ppermute | solution.py:484
  155.7 22.9 %collective-permute-start.2 = (bf16[128,2048]{1,0:T(8,128)(2,1)S(1)}, bf16[128,2048]{1,0:T(8,128)(2,1)S(1)}, u32[]{:S(2)}, u32[]{:S(2)}) collective-permute-start(bf16[128,2048]{1,0:T(8,128)(2,1)S(1)} %add_convert_fusion.2), channel_id=1, source_target_pairs={{0,2},{2,4},{4,6},{6,0},{1,3},{3,5},{5,7},{7,1},{8,10},{10,12},{12... | collective-permute-start | bytes 1572872 | tf_op jit(solution)/shard_map/ppermute | solution.py:485
  163.2 22.3 %collective-permute-start.8 = (bf16[128,2048]{1,0:T(8,128)(2,1)S(1)}, bf16[128,2048]{1,0:T(8,128)(2,1)S(1)}, u32[]{:S(2)}, u32[]{:S(2)}) collective-permute-start(bf16[128,2048]{1,0:T(8,128)(2,1)S(1)} %add_convert_fusion.1), channel_id=1, source_target_pairs={{0,6},{2,0},{4,2},{6,4},{1,7},{3,1},{5,3},{7,5},{8,14},{10,8},{12,... | collective-permute-start | bytes 1572872 | tf_op jit(solution)/shard_map/ppermute | solution.py:486
  178.6 9.6 %copy-start.18 = (bf16[384,2048]{1,0:T(8,128)(2,1)}, bf16[384,2048]{1,0:T(8,128)(2,1)S(1)}, u32[]{:S(2)}) copy-start(bf16[384,2048]{1,0:T(8,128)(2,1)S(1)} %collective-permute-done.3.refs_4_) | copy-start | bytes 4718596
  191.1 49.1 %all-to-all-start.3 = ((bf16[64,24,1024]{2,1,0:T(8,128)(2,1)}), bf16[64,24,1024]{2,1,0:T(8,128)(2,1)S(1)}, u32[]{:S(2)}, u32[]{:S(2)}) async-start(bf16[64,24,1024]{2,1,0:T(8,128)(2,1)} %bitcast.37), calls=%async_computation.3 | async-start | bytes 6291456 | tf_op jit(solution)/shard_map/all_to_all | solution.py:491
  200.2 58.3 %collective-permute-start.9 = (bf16[384,1024]{1,0:T(8,128)(2,1)}, bf16[384,1024]{1,0:T(8,128)(2,1)}, u32[]{:S(2)}, u32[]{:S(2)}) collective-permute-start(bf16[384,1024]{1,0:T(8,128)(2,1)} %copy-done.26), channel_id=1, source_target_pairs={{0,64},{64,0},{1,65},{65,1},{2,66},{66,2},{3,67},{67,3},{4,68},{68... | collective-permute-start | bytes 2359304 | tf_op jit(solution)/shard_map/ppermute | solution.py:477
  251.3 64.9 %all-to-all-start.4 = ((bf16[64,24,1024]{2,1,0:T(8,128)(2,1)}), bf16[64,24,1024]{2,1,0:T(8,128)(2,1)S(1)}, u32[]{:S(2)}, u32[]{:S(2)}) async-start(bf16[64,24,1024]{2,1,0:T(8,128)(2,1)} %bitcast.33), calls=%async_computation.4 | async-start | bytes 6291456 | tf_op jit(solution)/shard_map/all_to_all | solution.py:498
  258.5 43.6 %collective-permute-start.10 = (bf16[384,256]{1,0:T(8,128)(2,1)}, bf16[384,256]{1,0:T(8,128)(2,1)S(1)}, u32[]{:S(2)}, u32[]{:S(2)}) collective-permute-start(bf16[384,256]{1,0:T(8,128)(2,1)} %copy-done.37), channel_id=1, source_target_pairs={{0,64},{64,0},{1,65},{65,1},{2,66},{66,2},{3,67},{67,3},{4,68},{68... | collective-permute-start | bytes 589832 | tf_op jit(solution)/shard_map/ppermute | solution.py:497
  304.8 3.7 %copy-start.33 = (bf16[384,256]{1,0:T(8,128)(2,1)S(1)}, bf16[384,256]{1,0:T(8,128)(2,1)}, u32[]{:S(2)}) copy-start(bf16[384,256]{1,0:T(8,128)(2,1)} %copy-done.32) | copy-start | bytes 589828
  307.5 3.7 %copy-start.17 = (bf16[384,2048]{1,0:T(8,128)(2,1)S(1)}, bf16[384,2048]{1,0:T(8,128)(2,1)}, u32[]{:S(2)}) copy-start(bf16[384,2048]{1,0:T(8,128)(2,1)} %copy-done.15) | copy-start | bytes 4718596
  307.5 3.7 %copy-start.19 = (bf16[384,2048]{1,0:T(8,128)(2,1)S(1)}, bf16[384,2048]{1,0:T(8,128)(2,1)}, u32[]{:S(2)}) copy-start(bf16[384,2048]{1,0:T(8,128)(2,1)} %copy-done.18) | copy-start | bytes 4718596
  307.5 3.7 %copy-start.27 = (bf16[384,1024]{1,0:T(8,128)(2,1)S(1)}, bf16[384,1024]{1,0:T(8,128)(2,1)}, u32[]{:S(2)}) copy-start(bf16[384,1024]{1,0:T(8,128)(2,1)} %copy-done.26) | copy-start | bytes 2359300
  307.5 3.7 %copy-start.29 = (bf16[384,1024]{1,0:T(8,128)(2,1)S(1)}, bf16[384,1024]{1,0:T(8,128)(2,1)}, u32[]{:S(2)}) copy-start(bf16[384,1024]{1,0:T(8,128)(2,1)} %copy-done.28) | copy-start | bytes 2359300
  307.5 48.2 %collective-permute-start.11 = (bf16[4096,256]{1,0:T(8,128)(2,1)}, bf16[4096,256]{1,0:T(8,128)(2,1)}, u32[]{:S(2)}, u32[]{:S(2)}) collective-permute-start(bf16[4096,256]{1,0:T(8,128)(2,1)} %up_half.2), channel_id=1, source_target_pairs={{0,64},{64,0},{1,65},{65,1},{2,66},{66,2},{3,67},{67,3},{4,68},{68... | collective-permute-start | bytes 6291464 | tf_op jit(solution)/shard_map/ppermute | solution.py:501
  317.8 37.9 %copy-start.8 = (bf16[4096,256]{1,0:T(8,128)(2,1)S(1)}, bf16[4096,256]{1,0:T(8,128)(2,1)}, u32[]{:S(2)}) copy-start(bf16[4096,256]{1,0:T(8,128)(2,1)} %copy-done.7) | copy-start | bytes 6291460
  (27 other events, 46.4 us)

commit v5 on v4

--- a/solution.py
+++ b/solution.py
@@ -38,10 +38,14 @@
     return pltpu.CompilerParams(vmem_limit_bytes=limit)
 
 
-def cost(multiply_adds, transcendentals=0):
+def cost(multiply_adds, transcendentals=0, size=1 << 20):
     return pl.CostEstimate(
-        flops=2 * multiply_adds, bytes_accessed=1 << 20, transcendentals=transcendentals
+        flops=2 * multiply_adds, bytes_accessed=size, transcendentals=transcendentals
     )
+
+
+def whole(*shape):
+    return pl.BlockSpec(shape, lambda *_: (0,) * len(shape))
 
 
 def resident(count):
@@ -81,7 +85,7 @@
         in_specs=[spec] * 3,
         out_specs=pl.BlockSpec((4, 3, 256, HEAD), lambda b, t: (b, 0, t, 0)),
         out_shape=jax.ShapeDtypeStruct((8, 3, 512, HEAD), BF),
-        compiler_params=params(),
+        compiler_params=params(56 * 1024 * 1024),
         name="pack_heads",
     )(queries, keys, values)
 
@@ -161,14 +165,16 @@
     )(rows, rows, rows, rows)
 
 
-def project(place, half, heads, weight_own, weight_other):
+def project(place, offsets, splits, heads, weight_own, weight_other):
     width = 512
+    rows = len(offsets) * TOK
+    shapes = [array(TOK, D // n) for n in splits for _ in range(n)]
 
     def kernel(place_ref, a_ref, wo_ref, ws_ref, *refs):
         lhs = refs[-1]
         core = place_ref[1]
         for side, c in enumerate((core, 1 - core)):
-            for number, offset in enumerate((2, 1, 3, 0)):
+            for number, offset in enumerate(offsets):
                 z = lax.rem(place_ref[0] + offset, 4)
                 for b in range(2):
                     for h in range(4):
@@ -177,22 +183,30 @@
                             side * FF + h * HEAD : side * FF + (h + 1) * HEAD,
                         ] = a_ref[b, h, c, z]
 
-        @pl.loop(0, D // 2 // width)
-        def _(n):
-            near = pl.ds(pl.multiple_of(n * width, width), width)
-            cut = pl.ds(pl.multiple_of(half * (D // 2) + n * width, width), width)
-            total = dot_nn(lhs[:, :FF], wo_ref[:, cut]) + dot_nn(lhs[:, FF:], ws_ref[:, cut])
-            for number in range(4):
-                refs[number][:, near] = total[number * TOK : (number + 1) * TOK].astype(BF)
+        for half in range(2):
+
+            @pl.loop(0, D // 2 // width)
+            def _(n, half=half):
+                near = pl.ds(pl.multiple_of(n * width, width), width)
+                cut = pl.ds(pl.multiple_of(half * (D // 2) + n * width, width), width)
+                total = dot_nn(lhs[:, :FF], wo_ref[:, cut]) + dot_nn(lhs[:, FF:], ws_ref[:, cut])
+                first = 0
+                for number, pieces in enumerate(splits):
+                    part = total[number * TOK : (number + 1) * TOK].astype(BF)
+                    if pieces == 2:
+                        refs[first + half][:, near] = part
+                    else:
+                        refs[first][:, cut] = part
+                    first += pieces
 
     return pl.pallas_call(
         kernel,
         in_specs=[scalars()] + resident(3),
-        out_specs=resident(4),
-        scratch_shapes=[pltpu.VMEM((4 * TOK, 2 * FF), BF)],
-        out_shape=[array(TOK, D // 2)] * 4,
-        compiler_params=params(),
-        cost_estimate=cost(512 * 1024 * D // 2),
+        out_specs=resident(len(shapes)),
+        scratch_shapes=[pltpu.VMEM((rows, 2 * FF), BF)],
+        out_shape=shapes,
+        compiler_params=params(),
+        cost_estimate=cost(rows * 1024 * D),
         name="project",
     )(place, heads, weight_own, weight_other)
 
@@ -263,12 +277,12 @@
     )(cotangent, gate, target, weight)
 
 
-def norm_send(own_a, own_b, up_a, up_b, down_a, down_b, residual, gain, target):
-    def kernel(oa, ob, ua, ub, da, db, res_ref, gain_ref, tgt_ref, s_ref, o_ref, sc_ref):
+def norm_send(own, up_a, up_b, down_a, down_b, residual, gain, target):
+    def kernel(own_ref, ua, ub, da, db, res_ref, gain_ref, tgt_ref, s_ref, o_ref, sc_ref):
         square = jnp.zeros((TOK, 1), F32)
-        for half, own, first, second in ((0, oa, ua, da), (1, ob, ub, db)):
+        for half, first, second in ((0, ua, da), (1, ub, db)):
             cut = slice(half * D // 2, (half + 1) * D // 2)
-            s = own[...].astype(F32) + first[...].astype(F32) + second[...].astype(F32)
+            s = own_ref[:, cut].astype(F32) + first[...].astype(F32) + second[...].astype(F32)
             s = res_ref[:, cut].astype(F32) + s
             s_ref[:, cut] = s
             square += jnp.sum(s * s, axis=1, keepdims=True)
@@ -282,7 +296,7 @@
 
     return pl.pallas_call(
         kernel,
-        in_specs=resident(9),
+        in_specs=resident(8),
         out_specs=resident(2),
         out_shape=[
             jax.ShapeDtypeStruct((TOK, D), F32),
@@ -291,7 +305,7 @@
         scratch_shapes=[pltpu.VMEM((CB, SLOTS, CW), BF)],
         compiler_params=params(),
         name="norm_send",
-    )(own_a, own_b, up_a, up_b, down_a, down_b, residual, gain, target)
+    )(own, up_a, up_b, down_a, down_b, residual, gain, target)
 
 
 def grads_in(chunks, down):
@@ -346,7 +360,6 @@
         out_specs=resident(6),
         out_shape=[array(CB, SLOTS, CW), array(SLOTS, FF)] + [array(SLOTS, HALF)] * 4,
         compiler_params=params(),
-        cost_estimate=cost(SLOTS * D * FF, SLOTS * FF),
         name="hidden_units",
     )(place, chunks, up, back)
 
@@ -364,7 +377,6 @@
         out_shape=array(CB * SLOTS, CW),
         scratch_shapes=[pltpu.VMEM((CB, SLOTS, CW), BF)],
         compiler_params=params(),
-        cost_estimate=cost(SLOTS * D * FF),
         name="expert_out",
     )(hidden, down)
 
@@ -380,9 +392,26 @@
         out_specs=resident(1)[0],
         out_shape=array(D, HALF),
         compiler_params=params(),
-        cost_estimate=cost(SLOTS * D * HALF),
+        cost_estimate=cost(SLOTS * D * HALF, size=6 << 20),
         name="up_half",
     )(rows, pre_grad)
+
+
+def up_sum(rows, pre_grad, far):
+    def kernel(x_ref, p_ref, f_ref, o_ref):
+        for c in range(CB):
+            cut = slice(c * CW, (c + 1) * CW)
+            o_ref[cut, :] = (dot_tn(x_ref[c], p_ref[...]) + f_ref[cut, :].astype(F32)).astype(BF)
+
+    return pl.pallas_call(
+        kernel,
+        in_specs=resident(3),
+        out_specs=resident(1)[0],
+        out_shape=array(D, HALF),
+        compiler_params=params(),
+        cost_estimate=cost(SLOTS * D * HALF, size=6 << 20),
+        name="up_sum",
+    )(rows, pre_grad, far)
 
 
 def down_sum(hidden, grads, hidden_far, grads_far):
@@ -400,7 +429,7 @@
         out_specs=resident(1)[0],
         out_shape=array(HALF, D),
         compiler_params=params(),
-        cost_estimate=cost(2 * SLOTS * D * HALF),
+        cost_estimate=cost(2 * SLOTS * D * HALF, size=9 << 20),
         name="down_sum",
     )(hidden, hidden_far, *grads, *grads_far)
 
@@ -475,34 +504,33 @@
     *grads, back = grads_in(grad_arrived, down_weight[0])
     heads, back = lax.optimization_barrier((heads, back))
     far_0, far_1, far_2 = [lax.ppermute(g, "dp", swap) for g in grads]
-    fa, ua, da, own_a = project(place, 0, heads, out_weight, weight_other)
+    fa, fb = project(place, (2,), (2,), heads, out_weight, weight_other)
     fa = lax.ppermute(fa, "z", above)
+    fb = lax.ppermute(fb, "z", below)
     heads, far_0 = lax.optimization_barrier((heads, far_0))
-    fb, ub, db, own_b = project(place, 1, heads, out_weight, weight_other)
-    fb = lax.ppermute(fb, "z", below)
+    ua, ub, da, db, own = project(place, (1, 3, 0), (2, 2, 1), heads, out_weight, weight_other)
     ub = lax.ppermute(ub, "z", above)
     da = lax.ppermute(da, "z", below)
     ua = lax.ppermute(plus(ua, fa), "z", above)
     db = lax.ppermute(plus(db, fb), "z", below)
-    own_a, ua, far_1 = lax.optimization_barrier((own_a, ua, far_1))
+    own, ua, far_1 = lax.optimization_barrier((own, ua, far_1))
     stream, chunks = norm_send(
-        own_a, own_b, ua, ub, da, db, residual.reshape(TOK, D), norm_gain[None], target
+        own, ua, ub, da, db, residual.reshape(TOK, D), norm_gain[None], target
     )
     arrived = exchange(chunks, ALL)
 
     own_rows, hidden, hid_other, hid_own, pre_other, pre_own = hidden_units(
         place, arrived, up_weight[0], back
     )
-    hid_other, far_2 = lax.optimization_barrier((hid_other, far_2))
     hid_far = lax.ppermute(hid_other, "dp", swap)
+    hidden, far_2 = lax.optimization_barrier((hidden, far_2))
     returned = exchange(expert_out(hidden, down_weight[0]), ALL)
-    pre_other, hid_far = lax.optimization_barrier((pre_other, hid_far))
     up_other = up_half(own_rows, pre_other)
     up_far = lax.ppermute(up_other, "dp", swap)
+    block_out = combine(returned, stream, gate, target, weight_col)
     up_own = up_half(own_rows, pre_own)
+    block_out, hid_far = lax.optimization_barrier((block_out, hid_far))
     down_total = down_sum(hid_own, grads, hid_far, (far_0, far_1, far_2))
-    block_out = combine(returned, stream, gate, target, weight_col)
-    block_out, up_far = lax.optimization_barrier((block_out, up_far))
     up_total = plus(up_own, up_far)
     return (block_out.reshape(2, TOK // 2, D), up_total[None], down_total[None])
 

time: 361 us -> 338 us (0.936)
  waiting for transfers between devices: 202 us -> 178 us
  local copies, waits for them, and re-layouts: 33 us -> 29.3 us
    ppermute x1, waiting for transfers between devices: 41.2 us -> 1.25 us  [body(): hid_far = lax.ppermute(hid_other, 'dp', swap)]
    ppermute x1, waiting for transfers between devices: 34.7 us -> 50.5 us  [body(): up_far = lax.ppermute(up_other, 'dp', swap)]
    ppermute x3, waiting for transfers between devices: 17.6 us -> 27.4 us  [body(): far_0, far_1, far_2 = [lax.ppermute(g, 'dp', swap) for g in grads]]
    ppermute x1, waiting for transfers between devices: 7.35 us -> 0.01 us  [body(): fb = lax.ppermute(fb, 'z', below)]
    ppermute x1, waiting for transfers between devices: 6.98 us -> 1.17 us  [body(): db = lax.ppermute(plus(db, fb), 'z', below)]
    unnamed x86 -> x72, local copies, waits for them, and re-layouts: 32.4 us -> 28.7 us
  transfers between devices with their start and end apart: 17 -> 17, of which waited for: 10 -> 12; matrix products, arithmetic and copies ran while one was open for 0% -> 1% of each run, Pallas kernels for 16% -> 16%
where the time goes in v5:
time: 338 us; the launch traced here: 337 us
  waiting for transfers between devices  178 us (53%)
  Pallas kernels  66.1 us (20%)
  starting transfers between devices  58 us (17%)
  local copies, waits for them, and re-layouts  29.3 us (9%)
  other arithmetic  4.08 us (1%)
    ppermute x1, waiting for transfers between devices, body(): up_far = lax.ppermute(up_other, 'dp', swap)  50.5 us
    all_to_all x1, waiting for transfers between devices, body(): arrived = exchange(chunks, ALL)  37.9 us
    all_to_all x1, waiting for transfers between devices, body(): rows = exchange(pack(queries, keys, values), SEQ)  37.6 us
    unnamed x72, local copies, waits for them, and re-layouts  28.7 us
    ppermute x3, waiting for transfers between devices, body(): far_0, far_1, far_2 = [lax.ppermute(g, 'dp', swap) for g in grads]  27.4 us
    pallas_call x1, Pallas kernels, attend(): pl.pallas_call(kernel, grid=(8,), in_specs=[pl.BlockSpec((1, 1, 512, HEAD...  23.4 us
    all_to_all x1, waiting for transfers between devices, body(): grad_arrived = exchange(grad_chunks, ALL)  13.7 us
    pallas_call x2, Pallas kernels, project(): pl.pallas_call(kernel, in_specs=[scalars()] + resident(3), out_specs=resi...  12.6 us
  transfers between devices with their start and end apart: 17, of which 12 were waited for; matrix products, arithmetic and copies ran while one was open for 1% of the time, Pallas kernels for 16%

profile of v5, /device:TPU:1, one launch (start us, length us, event | category | flops | bytes accessed | tf_op | source)
XLA Modules:
  0.0 336.9 jit_solution(4155147124240582397)
XLA Ops:
  0.6 4.4 %pack_heads.1 = bf16[8,3,512,128]{3,2,1,0:T(8,128)(2,1)} custom-call(bf16[2,512,512]{2,1,0:T(8,128)(2,1)} %q_ref.1, bf16[2,512,512]{2,1,0:T(8,128)(2,1)} %k_ref.1, bf16[2,512,512]{2,1,0:T(8,128)(2,1)} %v_ref.1), custom_call_target="tpu_custom_call" | custom-call | tf_op jit(solution)/shard_map/pack_heads/pallas_call | solution.py:82
  5.1 6.0 %all-to-all-start = ((bf16[8,3,512,128]{3,2,1,0:T(8,128)(2,1)}), bf16[8,3,512,128]{3,2,1,0:T(8,128)(2,1)S(1)}, u32[]{:S(2)}, u32[]{:S(2)}) async-start(bf16[8,3,512,128]{3,2,1,0:T(8,128)(2,1)} %pack_heads.1), calls=%async_computation | async-start | bytes 6291456 | tf_op jit(solution)/shard_map/all_to_all | solution.py:494
  18.3 37.6 %all-to-all-done.q_ref.qn_ref.k_ref.v_ref = bf16[8,3,512,128]{3,2,1,0:T(8,128)(2,1)S(1)} async-done(((bf16[8,3,512,128]{3,2,1,0:T(8,128)(2,1)}), bf16[8,3,512,128]{3,2,1,0:T(8,128)(2,1)S(1)}, u32[]{:S(2)}, u32[]{:S(2)}) %all-to-all-start) | async-done | bytes 3145760 | tf_op jit(solution)/shard_map/all_to_all | solution.py:494
  57.6 8.1 %all-to-all-start.1 = ((bf16[64,24,1024]{2,1,0:T(8,128)(2,1)}), bf16[64,24,1024]{2,1,0:T(8,128)(2,1)S(1)}, u32[]{:S(2)}, u32[]{:S(2)}) async-start(bf16[64,24,1024]{2,1,0:T(8,128)(2,1)} %bitcast.35), calls=%async_computation.1 | async-start | bytes 6291456 | tf_op jit(solution)/shard_map/all_to_all | solution.py:499
  67.6 23.4 %attend.1 = bf16[8,2,4,64,128]{4,3,2,1,0:T(8,128)(2,1)S(1)} custom-call(bf16[8,3,512,128]{3,2,1,0:T(8,128)(2,1)S(1)} %copy-done.9, bf16[8,3,512,128]{3,2,1,0:T(8,128)(2,1)S(1)} %copy-done.9, bf16[8,3,512,128]{3,2,1,0:T(8,128)(2,1)S(1)} %copy-done.9, bf16[8,3,512,128]{3,2,1,0:T(8,128)(2,1)S(1)} %copy-done.9), custom_call_target="tpu_custom_call" | custom-call | flops 17179869184 | bytes 4194304 | tf_op jit(solution)/shard_map/attend/pallas_call | solution.py:144
  92.0 13.7 %all-to-all-done.1 = bf16[64,24,1024]{2,1,0:T(8,128)(2,1)S(1)} async-done(((bf16[64,24,1024]{2,1,0:T(8,128)(2,1)}), bf16[64,24,1024]{2,1,0:T(8,128)(2,1)S(1)}, u32[]{:S(2)}, u32[]{:S(2)}) %all-to-all-start.1) | async-done | bytes 3145760 | tf_op jit(solution)/shard_map/all_to_all | solution.py:499
  105.8 4.3 %all-to-all-start.2 = ((bf16[16,256,128]{2,1,0:T(8,128)(2,1)}), bf16[16,256,128]{2,1,0:T(8,128)(2,1)}, u32[]{:S(2)}, u32[]{:S(2)}) async-start(bf16[16,256,128]{2,1,0:T(8,128)(2,1)} %bitcast.39), calls=%async_computation.2 | async-start | bytes 2097152 | tf_op jit(solution)/shard_map/all_to_all | solution.py:503
  112.2 2.6 grads_in.1
  117.8 2.6 collective-permute-start
  120.5 5.4 %all-to-all-done.2 = bf16[16,256,128]{2,1,0:T(8,128)(2,1)} async-done(((bf16[16,256,128]{2,1,0:T(8,128)(2,1)}), bf16[16,256,128]{2,1,0:T(8,128)(2,1)}, u32[]{:S(2)}, u32[]{:S(2)}) %all-to-all-start.2) | async-done | bytes 1048608 | tf_op jit(solution)/shard_map/all_to_all | solution.py:503
  125.9 2.2 copy-done.6
  128.1 5.3 %project.3 = (bf16[128,2048]{1,0:T(8,128)(2,1)S(1)}, bf16[128,2048]{1,0:T(8,128)(2,1)S(1)}) custom-call(s32[3]{0:T(128)S(1)} %pad_add_fusion.place_ref, bf16[2,4,2,4,64,128]{5,4,3,2,1,0:T(8,128)(2,1)} %bitcast.12.a_ref, bf16[512,4096]{1,0:T(8,128)(2,1)S(1)} %copy-done.6, bf16[512,4096]{1,0:T(8,128)(2,1)} %collective-permute-done.1.ws_ref), custom_call_target="tpu_custom_call" | custom-call | flops 1073741824 | bytes 1048576 | tf_op jit(solution)/shard_map/project/pallas_call | solution.py:202
  134.6 2.6 collective-permute-start.4
  137.2 6.1 %collective-permute-done.refs_3_ = bf16[384,1024]{1,0:T(8,128)(2,1)S(1)} collective-permute-done((bf16[384,1024]{1,0:T(8,128)(2,1)}, bf16[384,1024]{1,0:T(8,128)(2,1)S(1)}, u32[]{:S(2)}, u32[]{:S(2)}) %collective-permute-start) | collective-permute-done | bytes 786464 | tf_op jit(solution)/shard_map/ppermute | solution.py:506
  145.2 7.3 %project.2 = (bf16[128,2048]{1,0:T(8,128)(2,1)S(1)}, bf16[128,2048]{1,0:T(8,128)(2,1)S(1)}, bf16[128,2048]{1,0:T(8,128)(2,1)S(1)}, bf16[128,2048]{1,0:T(8,128)(2,1)S(1)}, bf16[128,4096]{1,0:T(8,128)(2,1)S(1)}) custom-call(s32[3]{0:T(128)S(1)} %pad_add_fusion.place_ref, bf16[2,4,2,4,64,128]{5,4,3,2,1,0:T(8,128)(2,1)} %bitcast.12.a_ref, ...), custom_call_target="tpu_custom_call" | custom-call | flops 3221225472 | bytes 1048576 | tf_op jit(solution)/shard_map/project/pallas_call | solution.py:202
  152.7 2.7 collective-permute-start.6
  155.7 3.3 collective-permute-start.8
  159.0 18.0 %collective-permute-done.4.refs_4_ = bf16[384,2048]{1,0:T(8,128)(2,1)S(1)} collective-permute-done((bf16[384,2048]{1,0:T(8,128)(2,1)S(1)}, bf16[384,2048]{1,0:T(8,128)(2,1)S(1)}, u32[]{:S(2)}, u32[]{:S(2)}) %collective-permute-start.4) | collective-permute-done | bytes 1572896 | tf_op jit(solution)/shard_map/ppermute | solution.py:506
  178.4 2.6 norm_send.1
  183.9 8.6 %all-to-all-start.3 = ((bf16[64,24,1024]{2,1,0:T(8,128)(2,1)}), bf16[64,24,1024]{2,1,0:T(8,128)(2,1)S(1)}, u32[]{:S(2)}, u32[]{:S(2)}) async-start(bf16[64,24,1024]{2,1,0:T(8,128)(2,1)} %bitcast.37), calls=%async_computation.3 | async-start | bytes 6291456 | tf_op jit(solution)/shard_map/all_to_all | solution.py:520
  194.7 37.9 %all-to-all-done.3 = bf16[64,24,1024]{2,1,0:T(8,128)(2,1)S(1)} async-done(((bf16[64,24,1024]{2,1,0:T(8,128)(2,1)}), bf16[64,24,1024]{2,1,0:T(8,128)(2,1)S(1)}, u32[]{:S(2)}, u32[]{:S(2)}) %all-to-all-start.3) | async-done | bytes 3145760 | tf_op jit(solution)/shard_map/all_to_all | solution.py:520
  232.6 2.2 copy-done.7
  235.9 3.5 %hidden_units.1 = (bf16[4,384,1024]{2,1,0:T(8,128)(2,1)S(1)}, bf16[384,512]{1,0:T(8,128)(2,1)S(1)}, bf16[384,256]{1,0:T(8,128)(2,1)S(1)}, bf16[384,256]{1,0:T(8,...) custom-call(s32[3]{0:T(128)S(1)} %pad_add_fusion.place_ref, bf16[1536,1024]{1,0:T(8,128)(2,1)S(1)} %bitcast.33, ...), custom_call_target="tpu_custom_call" | custom-call | tf_op jit(solution)/shard_map/hidden_units/pallas_call | solution.py:357
  240.7 2.6 up_half.3
  245.5 3.4 %collective-permute-done.9.refs_5_ = bf16[384,1024]{1,0:T(8,128)(2,1)} collective-permute-done((bf16[384,1024]{1,0:T(8,128)(2,1)}, bf16[384,1024]{1,0:T(8,128)(2,1)}, u32[]{:S(2)}, u32[]{:S(2)}) %collective-permute-start.9) | collective-permute-done | bytes 786464 | tf_op jit(solution)/shard_map/ppermute | solution.py:506
  248.9 2.6 expert_out.1
  253.1 9.1 %all-to-all-start.4 = ((bf16[64,24,1024]{2,1,0:T(8,128)(2,1)}), bf16[64,24,1024]{2,1,0:T(8,128)(2,1)S(1)}, u32[]{:S(2)}, u32[]{:S(2)}) async-start(bf16[64,24,1024]{2,1,0:T(8,128)(2,1)} %bitcast.34), calls=%async_computation.4 | async-start | bytes 6291456 | tf_op jit(solution)/shard_map/all_to_all | solution.py:527
  268.6 50.5 %collective-permute-done.11 = bf16[4096,256]{1,0:T(8,128)(2,1)} collective-permute-done((bf16[4096,256]{1,0:T(8,128)(2,1)}, bf16[4096,256]{1,0:T(8,128)(2,1)}, u32[]{:S(2)}, u32[]{:S(2)}) %collective-permute-start.11) | collective-permute-done | bytes 2097184 | tf_op jit(solution)/shard_map/ppermute | solution.py:529
  319.1 3.4 %fusion = bf16[1,4096,256]{2,1,0:T(8,128)(2,1)} fusion(bf16[4096,256]{1,0:T(8,128)(2,1)} %collective-permute-done.11, bf16[4096,256]{1,0:T(8,128)(2,1)S(1)} %up_half.2), kind=kLoop, calls=%fused_computation.1 | loop fusion | flops 4194304 | bytes 6291456 | tf_op jit(solution)/shard_map/broadcast_in_dim | solution.py:535
  322.5 3.2 all-to-all-done.4
  327.4 3.1 combine.1
  331.8 5.1 %down_sum.1 = bf16[256,4096]{1,0:T(8,128)(2,1)} custom-call(bf16[384,256]{1,0:T(8,128)(2,1)S(1)} %get-tuple-element.66.h_ref, bf16[384,256]{1,0:T(8,128)(2,1)} %collective-permute-done.10.hf_ref, bf16[384,1024]{1,0:T(8,128)(2,1)} %get-tuple-element.43.refs_0_, bf16[384,2048]{1,0:T(8,128)(2,1)S(1)} %copy-done.15, bf16[384,1024]{1,0:T(8,128)(2,1)S(1)} %copy-done.22, ...), custom_call_target="tpu_custom_call" | custom-call | flops 1610612736 | bytes 9437184 | tf_op jit(solution)/shard_map/down_sum/pallas_call | solution.py:426
  (107 shorter events, 42.3 us)
Async XLA Ops:
  5.0 7.0 %copy-start.32 = (s32[2,64,2]{1,2,0:T(2,128)S(1)}, s32[2,64,2]{1,2,0:T(2,128)}, u32[]{:S(2)}) copy-start(s32[2,64,2]{1,2,0:T(2,128)} %param.19) | copy-start | bytes 3076
  5.1 7.3 %copy-start.33 = (f32[2,64,2]{1,2,0:T(2,128)S(1)}, f32[2,64,2]{1,2,0:T(2,128)}, u32[]{:S(2)}) copy-start(f32[2,64,2]{1,2,0:T(2,128)} %param.20) | copy-start | bytes 3076
  5.1 8.0 %copy-start.34 = (s32[2]{0:T(128)S(1)}, s32[2]{0:T(128)}, u32[]{:S(2)}) copy-start(s32[2]{0:T(128)} %param.21) | copy-start | bytes 28
  5.1 8.1 %copy-start.31 = (f32[2,4096]{1,0:T(2,128)S(1)}, f32[2,4096]{1,0:T(2,128)}, u32[]{:S(2)}) copy-start(f32[2,4096]{1,0:T(2,128)} %param.22) | copy-start | bytes 98308
  5.1 50.8 %all-to-all-start = ((bf16[8,3,512,128]{3,2,1,0:T(8,128)(2,1)}), bf16[8,3,512,128]{3,2,1,0:T(8,128)(2,1)S(1)}, u32[]{:S(2)}, u32[]{:S(2)}) async-start(bf16[8,3,512,128]{3,2,1,0:T(8,128)(2,1)} %pack_heads.1), calls=%async_computation | async-start | bytes 6291456 | tf_op jit(solution)/shard_map/all_to_all | solution.py:494
  11.1 114.9 %collective-permute-start.1 = (bf16[512,4096]{1,0:T(8,128)(2,1)}, bf16[512,4096]{1,0:T(8,128)(2,1)}, u32[]{:S(2)}, u32[]{:S(2)}) collective-permute-start(bf16[512,4096]{1,0:T(8,128)(2,1)} %wo_ref.3), channel_id=1, source_target_pairs={{0,1},{1,0},{2,3},{3,2},{4,5},{5,4},{6,7},{7,6},{8,9},{9,8},{10,11... | collective-permute-start | bytes 12582920 | tf_op jit(solution)/shard_map/ppermute | solution.py:495
  57.6 48.1 %all-to-all-start.1 = ((bf16[64,24,1024]{2,1,0:T(8,128)(2,1)}), bf16[64,24,1024]{2,1,0:T(8,128)(2,1)S(1)}, u32[]{:S(2)}, u32[]{:S(2)}) async-start(bf16[64,24,1024]{2,1,0:T(8,128)(2,1)} %bitcast.35), calls=%async_computation.1 | async-start | bytes 6291456 | tf_op jit(solution)/shard_map/all_to_all | solution.py:499
  105.8 20.2 %all-to-all-start.2 = ((bf16[16,256,128]{2,1,0:T(8,128)(2,1)}), bf16[16,256,128]{2,1,0:T(8,128)(2,1)}, u32[]{:S(2)}, u32[]{:S(2)}) async-start(bf16[16,256,128]{2,1,0:T(8,128)(2,1)} %bitcast.39), calls=%async_computation.2 | async-start | bytes 2097152 | tf_op jit(solution)/shard_map/all_to_all | solution.py:503
  117.8 25.4 %collective-permute-start = (bf16[384,1024]{1,0:T(8,128)(2,1)}, bf16[384,1024]{1,0:T(8,128)(2,1)S(1)}, u32[]{:S(2)}, u32[]{:S(2)}) collective-permute-start(bf16[384,1024]{1,0:T(8,128)(2,1)} %get-tuple-element.43.refs_0_), channel_id=1, source_target_pairs={{0,64},{64,0},{1,65},{65,1},{2,66},{66,2},{3,67},{67,3},{4,68},{68... | collective-permute-start | bytes 2359304 | tf_op jit(solution)/shard_map/ppermute | solution.py:506
  128.1 6.5 %copy-start.14 = (bf16[384,2048]{1,0:T(8,128)(2,1)S(1)}, bf16[384,2048]{1,0:T(8,128)(2,1)}, u32[]{:S(2)}) copy-start(bf16[384,2048]{1,0:T(8,128)(2,1)} %copy-done.13) | copy-start | bytes 4718596
  133.4 21.9 %collective-permute-start.2 = (bf16[128,2048]{1,0:T(8,128)(2,1)S(1)}, bf16[128,2048]{1,0:T(8,128)(2,1)S(1)}, u32[]{:S(2)}, u32[]{:S(2)}) collective-permute-start(bf16[128,2048]{1,0:T(8,128)(2,1)S(1)} %get-tuple-element.47), channel_id=1, source_target_pairs={{0,2},{2,4},{4,6},{6,0},{1,3},{3,5},{5,7},{7,1},{8,10},{10,12},{12... | collective-permute-start | bytes 1572872 | tf_op jit(solution)/shard_map/ppermute | solution.py:508
  134.6 42.4 %collective-permute-start.4 = (bf16[384,2048]{1,0:T(8,128)(2,1)S(1)}, bf16[384,2048]{1,0:T(8,128)(2,1)S(1)}, u32[]{:S(2)}, u32[]{:S(2)}) collective-permute-start(bf16[384,2048]{1,0:T(8,128)(2,1)S(1)} %copy-done.14), channel_id=1, source_target_pairs={{0,64},{64,0},{1,65},{65,1},{2,66},{66,2},{3,67},{67,3},{4,68},{68... | collective-permute-start | bytes 4718600 | tf_op jit(solution)/shard_map/ppermute | solution.py:506
  143.3 9.3 %copy-start.23 = (bf16[384,1024]{1,0:T(8,128)(2,1)}, bf16[384,1024]{1,0:T(8,128)(2,1)S(1)}, u32[]{:S(2)}) copy-start(bf16[384,1024]{1,0:T(8,128)(2,1)S(1)} %collective-permute-done.refs_3_) | copy-start | bytes 2359300
  143.3 12.3 %collective-permute-start.7 = (bf16[128,2048]{1,0:T(8,128)(2,1)S(1)}, bf16[128,2048]{1,0:T(8,128)(2,1)S(1)}, u32[]{:S(2)}, u32[]{:S(2)}) collective-permute-start(bf16[128,2048]{1,0:T(8,128)(2,1)S(1)} %get-tuple-element.54), channel_id=1, source_target_pairs={{0,6},{2,0},{4,2},{6,4},{1,7},{3,1},{5,3},{7,5},{8,14},{10,8},{12,... | collective-permute-start | bytes 1572872 | tf_op jit(solution)/shard_map/ppermute | solution.py:509
  152.6 25.8 %copy-start.18 = (bf16[2,64,4096]{2,1,0:T(8,128)(2,1)S(1)}, bf16[2,64,4096]{2,1,0:T(8,128)(2,1)}, u32[]{:S(2)}) copy-start(bf16[2,64,4096]{2,1,0:T(8,128)(2,1)} %param.16) | copy-start | bytes 3145732
  152.6 25.8 %copy-start.29 = (f32[4096]{0:T(1024)S(1)}, f32[4096]{0:T(1024)}, u32[]{:S(2)}) copy-start(f32[4096]{0:T(1024)} %param.18) | copy-start | bytes 49156
  152.6 24.6 %collective-permute-start.5 = (bf16[128,2048]{1,0:T(8,128)(2,1)S(1)}, bf16[128,2048]{1,0:T(8,128)(2,1)S(1)}, u32[]{:S(2)}, u32[]{:S(2)}) collective-permute-start(bf16[128,2048]{1,0:T(8,128)(2,1)S(1)} %get-tuple-element.51), channel_id=1, source_target_pairs={{0,2},{2,4},{4,6},{6,0},{1,3},{3,5},{5,7},{7,1},{8,10},{10,12},{12... | collective-permute-start | bytes 1572872 | tf_op jit(solution)/shard_map/ppermute | solution.py:512
  152.7 24.5 %collective-permute-start.6 = (bf16[128,2048]{1,0:T(8,128)(2,1)S(1)}, bf16[128,2048]{1,0:T(8,128)(2,1)S(1)}, u32[]{:S(2)}, u32[]{:S(2)}) collective-permute-start(bf16[128,2048]{1,0:T(8,128)(2,1)S(1)} %get-tuple-element.52), channel_id=1, source_target_pairs={{0,6},{2,0},{4,2},{6,4},{1,7},{3,1},{5,3},{7,5},{8,14},{10,8},{12,... | collective-permute-start | bytes 1572872 | tf_op jit(solution)/shard_map/ppermute | solution.py:513
  155.5 21.7 %collective-permute-start.3 = (bf16[128,2048]{1,0:T(8,128)(2,1)S(1)}, bf16[128,2048]{1,0:T(8,128)(2,1)S(1)}, u32[]{:S(2)}, u32[]{:S(2)}) collective-permute-start(bf16[128,2048]{1,0:T(8,128)(2,1)S(1)} %add_convert_fusion.2), channel_id=1, source_target_pairs={{0,2},{2,4},{4,6},{6,0},{1,3},{3,5},{5,7},{7,1},{8,10},{10,12},{12... | collective-permute-start | bytes 1572872 | tf_op jit(solution)/shard_map/ppermute | solution.py:514
  155.7 22.7 %collective-permute-start.8 = (bf16[128,2048]{1,0:T(8,128)(2,1)S(1)}, bf16[128,2048]{1,0:T(8,128)(2,1)S(1)}, u32[]{:S(2)}, u32[]{:S(2)}) collective-permute-start(bf16[128,2048]{1,0:T(8,128)(2,1)S(1)} %add_convert_fusion.1), channel_id=1, source_target_pairs={{0,6},{2,0},{4,2},{6,4},{1,7},{3,1},{5,3},{7,5},{8,14},{10,8},{12,... | collective-permute-start | bytes 1572872 | tf_op jit(solution)/shard_map/ppermute | solution.py:515
  177.0 4.0 %copy-start.16 = (bf16[384,2048]{1,0:T(8,128)(2,1)}, bf16[384,2048]{1,0:T(8,128)(2,1)S(1)}, u32[]{:S(2)}) copy-start(bf16[384,2048]{1,0:T(8,128)(2,1)S(1)} %collective-permute-done.4.refs_4_) | copy-start | bytes 4718596
  183.9 48.6 %all-to-all-start.3 = ((bf16[64,24,1024]{2,1,0:T(8,128)(2,1)}), bf16[64,24,1024]{2,1,0:T(8,128)(2,1)S(1)}, u32[]{:S(2)}, u32[]{:S(2)}) async-start(bf16[64,24,1024]{2,1,0:T(8,128)(2,1)} %bitcast.37), calls=%async_computation.3 | async-start | bytes 6291456 | tf_op jit(solution)/shard_map/all_to_all | solution.py:520
  192.6 56.3 %collective-permute-start.9 = (bf16[384,1024]{1,0:T(8,128)(2,1)}, bf16[384,1024]{1,0:T(8,128)(2,1)}, u32[]{:S(2)}, u32[]{:S(2)}) collective-permute-start(bf16[384,1024]{1,0:T(8,128)(2,1)} %copy-done.21), channel_id=1, source_target_pairs={{0,64},{64,0},{1,65},{65,1},{2,66},{66,2},{3,67},{67,3},{4,68},{68... | collective-permute-start | bytes 2359304 | tf_op jit(solution)/shard_map/ppermute | solution.py:506
  240.7 8.2 %copy-start.4 = (bf16[4,384,1024]{2,1,0:T(8,128)(2,1)}, bf16[4,384,1024]{2,1,0:T(8,128)(2,1)S(1)}, u32[]{:S(2)}) copy-start(bf16[4,384,1024]{2,1,0:T(8,128)(2,1)S(1)} %get-tuple-element.63.x_ref) | copy-start | bytes 9437188
  240.7 8.2 %copy-start.1 = (bf16[1,512,4096]{2,1,0:T(8,128)(2,1)S(1)}, bf16[1,512,4096]{2,1,0:T(8,128)(2,1)}, u32[]{:S(2)}) copy-start(bf16[1,512,4096]{2,1,0:T(8,128)(2,1)} %param.24) | copy-start | bytes 12582916
  243.4 75.7 %collective-permute-start.11 = (bf16[4096,256]{1,0:T(8,128)(2,1)}, bf16[4096,256]{1,0:T(8,128)(2,1)}, u32[]{:S(2)}, u32[]{:S(2)}) collective-permute-start(bf16[4096,256]{1,0:T(8,128)(2,1)} %up_half.3), channel_id=1, source_target_pairs={{0,64},{64,0},{1,65},{65,1},{2,66},{66,2},{3,67},{67,3},{4,68},{68... | collective-permute-start | bytes 6291464 | tf_op jit(solution)/shard_map/ppermute | solution.py:529
  253.1 72.7 %all-to-all-start.4 = ((bf16[64,24,1024]{2,1,0:T(8,128)(2,1)}), bf16[64,24,1024]{2,1,0:T(8,128)(2,1)S(1)}, u32[]{:S(2)}, u32[]{:S(2)}) async-start(bf16[64,24,1024]{2,1,0:T(8,128)(2,1)} %bitcast.34), calls=%async_computation.4 | async-start | bytes 6291456 | tf_op jit(solution)/shard_map/all_to_all | solution.py:527
  262.3 69.5 %collective-permute-start.10 = (bf16[384,256]{1,0:T(8,128)(2,1)}, bf16[384,256]{1,0:T(8,128)(2,1)}, u32[]{:S(2)}, u32[]{:S(2)}) collective-permute-start(bf16[384,256]{1,0:T(8,128)(2,1)} %copy-done.30), channel_id=1, source_target_pairs={{0,64},{64,0},{1,65},{65,1},{2,66},{66,2},{3,67},{67,3},{4,68},{68... | collective-permute-start | bytes 589832 | tf_op jit(solution)/shard_map/ppermute | solution.py:525
  327.4 4.4 %copy-start.15 = (bf16[384,2048]{1,0:T(8,128)(2,1)S(1)}, bf16[384,2048]{1,0:T(8,128)(2,1)}, u32[]{:S(2)}) copy-start(bf16[384,2048]{1,0:T(8,128)(2,1)} %copy-done.13) | copy-start | bytes 4718596
  327.4 4.4 %copy-start.17 = (bf16[384,2048]{1,0:T(8,128)(2,1)S(1)}, bf16[384,2048]{1,0:T(8,128)(2,1)}, u32[]{:S(2)}) copy-start(bf16[384,2048]{1,0:T(8,128)(2,1)} %copy-done.16) | copy-start | bytes 4718596
  327.4 4.4 %copy-start.22 = (bf16[384,1024]{1,0:T(8,128)(2,1)S(1)}, bf16[384,1024]{1,0:T(8,128)(2,1)}, u32[]{:S(2)}) copy-start(bf16[384,1024]{1,0:T(8,128)(2,1)} %copy-done.21) | copy-start | bytes 2359300
  327.4 4.4 %copy-start.24 = (bf16[384,1024]{1,0:T(8,128)(2,1)S(1)}, bf16[384,1024]{1,0:T(8,128)(2,1)}, u32[]{:S(2)}) copy-start(bf16[384,1024]{1,0:T(8,128)(2,1)} %copy-done.23) | copy-start | bytes 2359300
  (20 other events, 28.5 us)

commit v6 on v5

--- a/solution.py
+++ b/solution.py
@@ -52,6 +52,10 @@
     return [pl.BlockSpec(memory_space=pltpu.VMEM)] * count
 
 
+def in_hbm():
+    return pl.BlockSpec(memory_space=pltpu.HBM)
+
+
 def scalars():
     return pl.BlockSpec(memory_space=pltpu.SMEM)
 
@@ -236,6 +240,18 @@
         o_ref[g * CB * GR : (g + 1) * CB * GR, :] = dot_nn(mat, stack).astype(BF)
 
 
+def mix_to(sc_ref, buf_ref, o_ref, sem, first):
+    mat = mixer()
+    copies = []
+    for g in range(EXPERTS // GROUP):
+        cut = slice(g * CB * GR, (g + 1) * CB * GR)
+        stack = jnp.concatenate([sc_ref[c, g * GR : (g + 1) * GR, :] for c in range(CB)], axis=0)
+        buf_ref[cut, :] = dot_nn(mat, stack).astype(BF)
+        copies.append(pltpu.make_async_copy(buf_ref.at[cut], o_ref.at[cut], sem.at[first + g]))
+        copies[-1].start()
+    return copies
+
+
 def mix_in(i_ref, sc_ref):
     mat = unmixer()
     for g in range(EXPERTS // GROUP):
@@ -278,7 +294,7 @@
 
 
 def norm_send(own, up_a, up_b, down_a, down_b, residual, gain, target):
-    def kernel(own_ref, ua, ub, da, db, res_ref, gain_ref, tgt_ref, s_ref, o_ref, sc_ref):
+    def kernel(own_ref, ua, ub, da, db, res_ref, gain_ref, tgt_ref, so_ref, o_ref, sc_ref, s_ref, buf_ref, sem):
         square = jnp.zeros((TOK, 1), F32)
         for half, first, second in ((0, ua, da), (1, ub, db)):
             cut = slice(half * D // 2, (half + 1) * D // 2)
@@ -286,23 +302,31 @@
             s = res_ref[:, cut].astype(F32) + s
             s_ref[:, cut] = s
             square += jnp.sum(s * s, axis=1, keepdims=True)
+        kept = pltpu.make_async_copy(s_ref, so_ref, sem.at[0])
+        kept.start()
         factor = lax.rsqrt(square * (1.0 / D) + 1e-06)
         both = (placing(tgt_ref, 0) | placing(tgt_ref, 1)).astype(BF)
         for c in range(CB):
             cut = slice(c * CW, (c + 1) * CW)
             normed = (s_ref[:, cut] * factor * gain_ref[:, cut]).astype(BF)
             sc_ref[c] = dot_nn(both, normed).astype(BF)
-        mix_out(sc_ref, o_ref)
+        for copy in [kept] + mix_to(sc_ref, buf_ref, o_ref, sem, 1):
+            copy.wait()
 
     return pl.pallas_call(
         kernel,
         in_specs=resident(8),
-        out_specs=resident(2),
+        out_specs=[in_hbm(), in_hbm()],
         out_shape=[
             jax.ShapeDtypeStruct((TOK, D), F32),
             jax.ShapeDtypeStruct((CB * SLOTS, CW), BF),
         ],
-        scratch_shapes=[pltpu.VMEM((CB, SLOTS, CW), BF)],
+        scratch_shapes=[
+            pltpu.VMEM((CB, SLOTS, CW), BF),
+            pltpu.VMEM((TOK, D), F32),
+            pltpu.VMEM((CB * SLOTS, CW), BF),
+            pltpu.SemaphoreType.DMA((1 + EXPERTS // GROUP,)),
+        ],
         compiler_params=params(),
         name="norm_send",
     )(own, up_a, up_b, down_a, down_b, residual, gain, target)
@@ -339,11 +363,21 @@
 
 
 def hidden_units(place, chunks, up, back):
-    def kernel(place_ref, i_ref, up_ref, b_ref, x_ref, hid_ref, ho_ref, hs_ref, po_ref, ps_ref):
+    def kernel(
+        place_ref, i_ref, up_hbm, b_ref, x_ref, hid_ref, ho_ref, hs_ref, po_ref, ps_ref, up_ref, sem
+    ):
+        cuts = [slice(c * CW, (c + 1) * CW) for c in range(CB)]
+        copies = [
+            pltpu.make_async_copy(up_hbm.at[cut], up_ref.at[cut], sem.at[c])
+            for c, cut in enumerate(cuts)
+        ]
+        for copy in copies:
+            copy.start()
         mix_in(i_ref, x_ref)
         pre = None
         for c in range(CB):
-            part = dot_nn(x_ref[c], up_ref[c * CW : (c + 1) * CW, :])
+            copies[c].wait()
+            part = dot_nn(x_ref[c], up_ref[cuts[c], :])
             pre = part if pre is None else pre + part
         act, slope = gelu_pair(pre)
         hidden, grad = act.astype(BF), (b_ref[...] * slope).astype(BF)
@@ -356,8 +390,9 @@
 
     return pl.pallas_call(
         kernel,
-        in_specs=[scalars()] + resident(3),
+        in_specs=[scalars()] + resident(1) + [in_hbm()] + resident(1),
         out_specs=resident(6),
+        scratch_shapes=[pltpu.VMEM((D, FF), BF), pltpu.SemaphoreType.DMA((CB,))],
         out_shape=[array(CB, SLOTS, CW), array(SLOTS, FF)] + [array(SLOTS, HALF)] * 4,
         compiler_params=params(),
         name="hidden_units",
@@ -365,17 +400,22 @@
 
 
 def expert_out(hidden, down):
-    def kernel(h_ref, down_ref, o_ref, prod):
+    def kernel(h_ref, down_ref, o_ref, prod, buf_ref, sem):
         for c in range(CB):
             prod[c] = dot_nn(h_ref[...], down_ref[:, c * CW : (c + 1) * CW]).astype(BF)
-        mix_out(prod, o_ref)
+        for copy in mix_to(prod, buf_ref, o_ref, sem, 0):
+            copy.wait()
 
     return pl.pallas_call(
         kernel,
         in_specs=resident(2),
-        out_specs=resident(1)[0],
+        out_specs=in_hbm(),
         out_shape=array(CB * SLOTS, CW),
-        scratch_shapes=[pltpu.VMEM((CB, SLOTS, CW), BF)],
+        scratch_shapes=[
+            pltpu.VMEM((CB, SLOTS, CW), BF),
+            pltpu.VMEM((CB * SLOTS, CW), BF),
+            pltpu.SemaphoreType.DMA((EXPERTS // GROUP,)),
+        ],
         compiler_params=params(),
         name="expert_out",
     )(hidden, down)
@@ -523,13 +563,12 @@
         place, arrived, up_weight[0], back
     )
     hid_far = lax.ppermute(hid_other, "dp", swap)
-    hidden, far_2 = lax.optimization_barrier((hidden, far_2))
+    hidden, far_2, hid_far = lax.optimization_barrier((hidden, far_2, hid_far))
     returned = exchange(expert_out(hidden, down_weight[0]), ALL)
     up_other = up_half(own_rows, pre_other)
     up_far = lax.ppermute(up_other, "dp", swap)
     block_out = combine(returned, stream, gate, target, weight_col)
     up_own = up_half(own_rows, pre_own)
-    block_out, hid_far = lax.optimization_barrier((block_out, hid_far))
     down_total = down_sum(hid_own, grads, hid_far, (far_0, far_1, far_2))
     up_total = plus(up_own, up_far)
     return (block_out.reshape(2, TOK // 2, D), up_total[None], down_total[None])

time: 338 us -> 339 us (level)
  Pallas kernels: 66.1 us -> 72.1 us
  waiting for transfers between devices: 178 us -> 173 us
    ppermute x1, waiting for transfers between devices: 50.5 us -> 44.1 us  [body(): up_far = lax.ppermute(up_other, 'dp', swap)]
    pallas_call x3, Pallas kernels: 8.65 us -> 14.8 us  [the longest x1 5.32 us: norm_send(): pl.pallas_call(kernel, in_specs=resident(8), out_specs=[in_hbm(), in_hbm(...]
    unnamed x72 -> x74, local copies, waits for them, and re-layouts: 28.7 us -> 29 us
  transfers between devices with their start and end apart: 17 -> 17, of which waited for: 12 -> 12; matrix products, arithmetic and copies ran while one was open for 1% -> 1% of each run, Pallas kernels for 16% -> 18%
where the time goes in v6:
time: 339 us; the launch traced here: 336 us
  waiting for transfers between devices  173 us (51%)
  Pallas kernels  72.1 us (21%)
  starting transfers between devices  56.7 us (17%)
  local copies, waits for them, and re-layouts  29.6 us (9%)
  other arithmetic  4.09 us (1%)
    ppermute x1, waiting for transfers between devices, body(): up_far = lax.ppermute(up_other, 'dp', swap)  44.1 us
    all_to_all x1, waiting for transfers between devices, body(): arrived = exchange(chunks, ALL)  37.9 us
    all_to_all x1, waiting for transfers between devices, body(): rows = exchange(pack(queries, keys, values), SEQ)  37.6 us
    unnamed x74, local copies, waits for them, and re-layouts  29 us
    ppermute x3, waiting for transfers between devices, body(): far_0, far_1, far_2 = [lax.ppermute(g, 'dp', swap) for g in grads]  26.5 us
    pallas_call x1, Pallas kernels, attend(): pl.pallas_call(kernel, grid=(8,), in_specs=[pl.BlockSpec((1, 1, 512, HEAD...  23.4 us
    all_to_all x1, waiting for transfers between devices, body(): grad_arrived = exchange(grad_chunks, ALL)  13.7 us
    pallas_call x2, Pallas kernels, project(): pl.pallas_call(kernel, in_specs=[scalars()] + resident(3), out_specs=resi...  12.6 us
  transfers between devices with their start and end apart: 17, of which 12 were waited for; matrix products, arithmetic and copies ran while one was open for 1% of the time, Pallas kernels for 18%

profile of v6, /device:TPU:1, one launch (start us, length us, event | category | flops | bytes accessed | tf_op | source)
XLA Modules:
  0.0 336.4 jit_solution(5845933831948648848)
XLA Ops:
  0.6 4.4 %pack_heads.1 = bf16[8,3,512,128]{3,2,1,0:T(8,128)(2,1)} custom-call(bf16[2,512,512]{2,1,0:T(8,128)(2,1)} %q_ref.1, bf16[2,512,512]{2,1,0:T(8,128)(2,1)} %k_ref.1, bf16[2,512,512]{2,1,0:T(8,128)(2,1)} %v_ref.1), custom_call_target="tpu_custom_call" | custom-call | tf_op jit(solution)/shard_map/pack_heads/pallas_call | solution.py:86
  5.0 6.0 %all-to-all-start = ((bf16[8,3,512,128]{3,2,1,0:T(8,128)(2,1)}), bf16[8,3,512,128]{3,2,1,0:T(8,128)(2,1)S(1)}, u32[]{:S(2)}, u32[]{:S(2)}) async-start(bf16[8,3,512,128]{3,2,1,0:T(8,128)(2,1)} %pack_heads.1), calls=%async_computation | async-start | bytes 6291456 | tf_op jit(solution)/shard_map/all_to_all | solution.py:534
  18.3 37.6 %all-to-all-done.q_ref.qn_ref.k_ref.v_ref = bf16[8,3,512,128]{3,2,1,0:T(8,128)(2,1)S(1)} async-done(((bf16[8,3,512,128]{3,2,1,0:T(8,128)(2,1)}), bf16[8,3,512,128]{3,2,1,0:T(8,128)(2,1)S(1)}, u32[]{:S(2)}, u32[]{:S(2)}) %all-to-all-start) | async-done | bytes 3145760 | tf_op jit(solution)/shard_map/all_to_all | solution.py:534
  57.6 8.1 %all-to-all-start.1 = ((bf16[64,24,1024]{2,1,0:T(8,128)(2,1)}), bf16[64,24,1024]{2,1,0:T(8,128)(2,1)S(1)}, u32[]{:S(2)}, u32[]{:S(2)}) async-start(bf16[64,24,1024]{2,1,0:T(8,128)(2,1)} %bitcast.35), calls=%async_computation.1 | async-start | bytes 6291456 | tf_op jit(solution)/shard_map/all_to_all | solution.py:539
  67.6 23.4 %attend.1 = bf16[8,2,4,64,128]{4,3,2,1,0:T(8,128)(2,1)S(1)} custom-call(bf16[8,3,512,128]{3,2,1,0:T(8,128)(2,1)S(1)} %copy-done.9, bf16[8,3,512,128]{3,2,1,0:T(8,128)(2,1)S(1)} %copy-done.9, bf16[8,3,512,128]{3,2,1,0:T(8,128)(2,1)S(1)} %copy-done.9, bf16[8,3,512,128]{3,2,1,0:T(8,128)(2,1)S(1)} %copy-done.9), custom_call_target="tpu_custom_call" | custom-call | flops 17179869184 | bytes 4194304 | tf_op jit(solution)/shard_map/attend/pallas_call | solution.py:148
  92.0 13.7 %all-to-all-done.1 = bf16[64,24,1024]{2,1,0:T(8,128)(2,1)S(1)} async-done(((bf16[64,24,1024]{2,1,0:T(8,128)(2,1)}), bf16[64,24,1024]{2,1,0:T(8,128)(2,1)S(1)}, u32[]{:S(2)}, u32[]{:S(2)}) %all-to-all-start.1) | async-done | bytes 3145760 | tf_op jit(solution)/shard_map/all_to_all | solution.py:539
  105.7 4.3 %all-to-all-start.2 = ((bf16[16,256,128]{2,1,0:T(8,128)(2,1)}), bf16[16,256,128]{2,1,0:T(8,128)(2,1)}, u32[]{:S(2)}, u32[]{:S(2)}) async-start(bf16[16,256,128]{2,1,0:T(8,128)(2,1)} %bitcast.39), calls=%async_computation.2 | async-start | bytes 2097152 | tf_op jit(solution)/shard_map/all_to_all | solution.py:543
  112.2 2.6 grads_in.1
  117.7 2.6 collective-permute-start
  120.4 5.4 %all-to-all-done.2 = bf16[16,256,128]{2,1,0:T(8,128)(2,1)} async-done(((bf16[16,256,128]{2,1,0:T(8,128)(2,1)}), bf16[16,256,128]{2,1,0:T(8,128)(2,1)}, u32[]{:S(2)}, u32[]{:S(2)}) %all-to-all-start.2) | async-done | bytes 1048608 | tf_op jit(solution)/shard_map/all_to_all | solution.py:543
  125.9 2.2 copy-done.6
  128.1 5.3 %project.3 = (bf16[128,2048]{1,0:T(8,128)(2,1)S(1)}, bf16[128,2048]{1,0:T(8,128)(2,1)S(1)}) custom-call(s32[3]{0:T(128)S(1)} %pad_add_fusion.place_ref, bf16[2,4,2,4,64,128]{5,4,3,2,1,0:T(8,128)(2,1)} %bitcast.12.a_ref, bf16[512,4096]{1,0:T(8,128)(2,1)S(1)} %copy-done.6, bf16[512,4096]{1,0:T(8,128)(2,1)} %collective-permute-done.1.ws_ref), custom_call_target="tpu_custom_call" | custom-call | flops 1073741824 | bytes 1048576 | tf_op jit(solution)/shard_map/project/pallas_call | solution.py:206
  134.6 2.6 collective-permute-start.4
  137.2 6.1 %collective-permute-done.refs_3_ = bf16[384,1024]{1,0:T(8,128)(2,1)S(1)} collective-permute-done((bf16[384,1024]{1,0:T(8,128)(2,1)}, bf16[384,1024]{1,0:T(8,128)(2,1)S(1)}, u32[]{:S(2)}, u32[]{:S(2)}) %collective-permute-start) | collective-permute-done | bytes 786464 | tf_op jit(solution)/shard_map/ppermute | solution.py:546
  145.2 7.3 %project.2 = (bf16[128,2048]{1,0:T(8,128)(2,1)S(1)}, bf16[128,2048]{1,0:T(8,128)(2,1)S(1)}, bf16[128,2048]{1,0:T(8,128)(2,1)S(1)}, bf16[128,2048]{1,0:T(8,128)(2,1)S(1)}, bf16[128,4096]{1,0:T(8,128)(2,1)S(1)}) custom-call(s32[3]{0:T(128)S(1)} %pad_add_fusion.place_ref, bf16[2,4,2,4,64,128]{5,4,3,2,1,0:T(8,128)(2,1)} %bitcast.12.a_ref, ...), custom_call_target="tpu_custom_call" | custom-call | flops 3221225472 | bytes 1048576 | tf_op jit(solution)/shard_map/project/pallas_call | solution.py:206
  152.6 2.7 collective-permute-start.6
  155.7 3.3 collective-permute-start.8
  159.0 18.0 %collective-permute-done.4.refs_4_ = bf16[384,2048]{1,0:T(8,128)(2,1)S(1)} collective-permute-done((bf16[384,2048]{1,0:T(8,128)(2,1)S(1)}, bf16[384,2048]{1,0:T(8,128)(2,1)S(1)}, u32[]{:S(2)}, u32[]{:S(2)}) %collective-permute-start.4) | collective-permute-done | bytes 1572896 | tf_op jit(solution)/shard_map/ppermute | solution.py:546
  178.4 5.3 %norm_send.1 = (f32[128,4096]{1,0:T(8,128)S(1)}, bf16[1536,1024]{1,0:T(8,128)(2,1)S(1)}) custom-call(bf16[128,4096]{1,0:T(8,128)(2,1)S(1)} %get-tuple-element.48.own_ref, bf16[128,2048]{1,0:T(8,128)(2,1)S(1)} %collective-permute-done.3.ua, bf16[128,2048]{1,0:T(8,128)(2,1)S(1)} %collective-permute-done.5.ub, bf16[128,2048]{1,0:T(8,128)(2,1)S(1)} %collective-permute-done.6.da, ...), custom_call_target="tpu_custom_call" | custom-call | tf_op jit(solution)/shard_map/norm_send/pallas_call | solution.py:316
  186.7 8.6 %all-to-all-start.3 = ((bf16[64,24,1024]{2,1,0:T(8,128)(2,1)}), bf16[64,24,1024]{2,1,0:T(8,128)(2,1)S(1)}, u32[]{:S(2)}, u32[]{:S(2)}) async-start(bf16[64,24,1024]{2,1,0:T(8,128)(2,1)} %bitcast.37), calls=%async_computation.3 | async-start | bytes 6291456 | tf_op jit(solution)/shard_map/all_to_all | solution.py:560
  197.5 37.9 %all-to-all-done.3 = bf16[64,24,1024]{2,1,0:T(8,128)(2,1)S(1)} async-done(((bf16[64,24,1024]{2,1,0:T(8,128)(2,1)}), bf16[64,24,1024]{2,1,0:T(8,128)(2,1)S(1)}, u32[]{:S(2)}, u32[]{:S(2)}) %all-to-all-start.3) | async-done | bytes 3145760 | tf_op jit(solution)/shard_map/all_to_all | solution.py:560
  235.4 2.2 copy-done.7
  238.7 4.2 %hidden_units.1 = (bf16[4,384,1024]{2,1,0:T(8,128)(2,1)S(1)}, bf16[384,512]{1,0:T(8,128)(2,1)S(1)}, bf16[384,256]{1,0:T(8,128)(2,1)S(1)}, bf16[384,256]{1,0:T(8,...) custom-call(s32[3]{0:T(128)S(1)} %pad_add_fusion.place_ref, bf16[1536,1024]{1,0:T(8,128)(2,1)S(1)} %bitcast.34, ...), custom_call_target="tpu_custom_call" | custom-call | tf_op jit(solution)/shard_map/hidden_units/pallas_call | solution.py:391
  245.6 2.7 up_half.3
  249.2 2.5 collective-permute-done.9.refs_5_
  251.6 4.1 %collective-permute-done.10.hf_ref = bf16[384,256]{1,0:T(8,128)(2,1)S(1)} collective-permute-done((bf16[384,256]{1,0:T(8,128)(2,1)S(1)}, bf16[384,256]{1,0:T(8,128)(2,1)S(1)}, u32[]{:S(2)}, u32[]{:S(2)}) %collective-permute-start.10) | collective-permute-done | bytes 196640 | tf_op jit(solution)/shard_map/ppermute | solution.py:565
  255.8 5.3 %expert_out.1 = bf16[1536,1024]{1,0:T(8,128)(2,1)S(1)} custom-call(bf16[384,512]{1,0:T(8,128)(2,1)S(1)} %get-tuple-element.59.h_ref, bf16[512,4096]{1,0:T(8,128)(2,1)S(1)} %bitcast.30), custom_call_target="tpu_custom_call" | custom-call | tf_op jit(solution)/shard_map/expert_out/pallas_call | solution.py:409
  262.6 9.2 %all-to-all-start.4 = ((bf16[64,24,1024]{2,1,0:T(8,128)(2,1)}), bf16[64,24,1024]{2,1,0:T(8,128)(2,1)S(1)}, u32[]{:S(2)}, u32[]{:S(2)}) async-start(bf16[64,24,1024]{2,1,0:T(8,128)(2,1)} %bitcast.33), calls=%async_computation.4 | async-start | bytes 6291456 | tf_op jit(solution)/shard_map/all_to_all | solution.py:567
  277.0 5.0 %down_sum.1 = bf16[256,4096]{1,0:T(8,128)(2,1)} custom-call(bf16[384,256]{1,0:T(8,128)(2,1)S(1)} %get-tuple-element.64.h_ref, bf16[384,256]{1,0:T(8,128)(2,1)S(1)} %copy-done.28, bf16[384,1024]{1,0:T(8,128)(2,1)} %get-tuple-element.42.refs_0_, bf16[384,2048]{1,0:T(8,128)(2,1)S(1)} %copy-done.15, bf16[384,1024]{1,0:T(8,128)(2,1)S(1)} %copy-done.22, ...), custom_call_target="tpu_custom_call" | custom-call | flops 1610612736 | bytes 9437184 | tf_op jit(solution)/shard_map/down_sum/pallas_call | solution.py:466
  282.0 44.1 %collective-permute-done.11 = bf16[4096,256]{1,0:T(8,128)(2,1)} collective-permute-done((bf16[4096,256]{1,0:T(8,128)(2,1)}, bf16[4096,256]{1,0:T(8,128)(2,1)}, u32[]{:S(2)}, u32[]{:S(2)}) %collective-permute-start.11) | collective-permute-done | bytes 2097184 | tf_op jit(solution)/shard_map/ppermute | solution.py:569
  326.1 3.4 %fusion = bf16[1,4096,256]{2,1,0:T(8,128)(2,1)} fusion(bf16[4096,256]{1,0:T(8,128)(2,1)} %collective-permute-done.11, bf16[4096,256]{1,0:T(8,128)(2,1)S(1)} %up_half.2), kind=kLoop, calls=%fused_computation.1 | loop fusion | flops 4194304 | bytes 6291456 | tf_op jit(solution)/shard_map/broadcast_in_dim | solution.py:574
  333.3 3.1 combine.1
  (109 shorter events, 42.3 us)
Async XLA Ops:
  5.0 7.0 %copy-start.33 = (s32[2,64,2]{1,2,0:T(2,128)S(1)}, s32[2,64,2]{1,2,0:T(2,128)}, u32[]{:S(2)}) copy-start(s32[2,64,2]{1,2,0:T(2,128)} %param.19) | copy-start | bytes 3076
  5.0 7.9 %copy-start.34 = (f32[2,64,2]{1,2,0:T(2,128)S(1)}, f32[2,64,2]{1,2,0:T(2,128)}, u32[]{:S(2)}) copy-start(f32[2,64,2]{1,2,0:T(2,128)} %param.20) | copy-start | bytes 3076
  5.0 8.0 %copy-start.35 = (s32[2]{0:T(128)S(1)}, s32[2]{0:T(128)}, u32[]{:S(2)}) copy-start(s32[2]{0:T(128)} %param.21) | copy-start | bytes 28
  5.0 8.1 %copy-start.32 = (f32[2,4096]{1,0:T(2,128)S(1)}, f32[2,4096]{1,0:T(2,128)}, u32[]{:S(2)}) copy-start(f32[2,4096]{1,0:T(2,128)} %param.22) | copy-start | bytes 98308
  5.0 50.8 %all-to-all-start = ((bf16[8,3,512,128]{3,2,1,0:T(8,128)(2,1)}), bf16[8,3,512,128]{3,2,1,0:T(8,128)(2,1)S(1)}, u32[]{:S(2)}, u32[]{:S(2)}) async-start(bf16[8,3,512,128]{3,2,1,0:T(8,128)(2,1)} %pack_heads.1), calls=%async_computation | async-start | bytes 6291456 | tf_op jit(solution)/shard_map/all_to_all | solution.py:534
  11.0 114.9 %collective-permute-start.1 = (bf16[512,4096]{1,0:T(8,128)(2,1)}, bf16[512,4096]{1,0:T(8,128)(2,1)}, u32[]{:S(2)}, u32[]{:S(2)}) collective-permute-start(bf16[512,4096]{1,0:T(8,128)(2,1)} %wo_ref.3), channel_id=1, source_target_pairs={{0,1},{1,0},{2,3},{3,2},{4,5},{5,4},{6,7},{7,6},{8,9},{9,8},{10,11... | collective-permute-start | bytes 12582920 | tf_op jit(solution)/shard_map/ppermute | solution.py:535
  57.6 48.1 %all-to-all-start.1 = ((bf16[64,24,1024]{2,1,0:T(8,128)(2,1)}), bf16[64,24,1024]{2,1,0:T(8,128)(2,1)S(1)}, u32[]{:S(2)}, u32[]{:S(2)}) async-start(bf16[64,24,1024]{2,1,0:T(8,128)(2,1)} %bitcast.35), calls=%async_computation.1 | async-start | bytes 6291456 | tf_op jit(solution)/shard_map/all_to_all | solution.py:539
  105.7 20.2 %all-to-all-start.2 = ((bf16[16,256,128]{2,1,0:T(8,128)(2,1)}), bf16[16,256,128]{2,1,0:T(8,128)(2,1)}, u32[]{:S(2)}, u32[]{:S(2)}) async-start(bf16[16,256,128]{2,1,0:T(8,128)(2,1)} %bitcast.39), calls=%async_computation.2 | async-start | bytes 2097152 | tf_op jit(solution)/shard_map/all_to_all | solution.py:543
  117.7 25.5 %collective-permute-start = (bf16[384,1024]{1,0:T(8,128)(2,1)}, bf16[384,1024]{1,0:T(8,128)(2,1)S(1)}, u32[]{:S(2)}, u32[]{:S(2)}) collective-permute-start(bf16[384,1024]{1,0:T(8,128)(2,1)} %get-tuple-element.42.refs_0_), channel_id=1, source_target_pairs={{0,64},{64,0},{1,65},{65,1},{2,66},{66,2},{3,67},{67,3},{4,68},{68... | collective-permute-start | bytes 2359304 | tf_op jit(solution)/shard_map/ppermute | solution.py:546
  125.9 2.2 copy-start.6
  128.1 6.5 %copy-start.14 = (bf16[384,2048]{1,0:T(8,128)(2,1)S(1)}, bf16[384,2048]{1,0:T(8,128)(2,1)}, u32[]{:S(2)}) copy-start(bf16[384,2048]{1,0:T(8,128)(2,1)} %copy-done.13) | copy-start | bytes 4718596
  133.4 21.9 %collective-permute-start.2 = (bf16[128,2048]{1,0:T(8,128)(2,1)S(1)}, bf16[128,2048]{1,0:T(8,128)(2,1)S(1)}, u32[]{:S(2)}, u32[]{:S(2)}) collective-permute-start(bf16[128,2048]{1,0:T(8,128)(2,1)S(1)} %get-tuple-element.46), channel_id=1, source_target_pairs={{0,2},{2,4},{4,6},{6,0},{1,3},{3,5},{5,7},{7,1},{8,10},{10,12},{12... | collective-permute-start | bytes 1572872 | tf_op jit(solution)/shard_map/ppermute | solution.py:548
  134.6 42.4 %collective-permute-start.4 = (bf16[384,2048]{1,0:T(8,128)(2,1)S(1)}, bf16[384,2048]{1,0:T(8,128)(2,1)S(1)}, u32[]{:S(2)}, u32[]{:S(2)}) collective-permute-start(bf16[384,2048]{1,0:T(8,128)(2,1)S(1)} %copy-done.14), channel_id=1, source_target_pairs={{0,64},{64,0},{1,65},{65,1},{2,66},{66,2},{3,67},{67,3},{4,68},{68... | collective-permute-start | bytes 4718600 | tf_op jit(solution)/shard_map/ppermute | solution.py:546
  143.2 9.3 %copy-start.23 = (bf16[384,1024]{1,0:T(8,128)(2,1)}, bf16[384,1024]{1,0:T(8,128)(2,1)S(1)}, u32[]{:S(2)}) copy-start(bf16[384,1024]{1,0:T(8,128)(2,1)S(1)} %collective-permute-done.refs_3_) | copy-start | bytes 2359300
  143.2 12.3 %collective-permute-start.7 = (bf16[128,2048]{1,0:T(8,128)(2,1)S(1)}, bf16[128,2048]{1,0:T(8,128)(2,1)S(1)}, u32[]{:S(2)}, u32[]{:S(2)}) collective-permute-start(bf16[128,2048]{1,0:T(8,128)(2,1)S(1)} %get-tuple-element.53), channel_id=1, source_target_pairs={{0,6},{2,0},{4,2},{6,4},{1,7},{3,1},{5,3},{7,5},{8,14},{10,8},{12,... | collective-permute-start | bytes 1572872 | tf_op jit(solution)/shard_map/ppermute | solution.py:549
  152.5 25.8 %copy-start.18 = (bf16[2,64,4096]{2,1,0:T(8,128)(2,1)S(1)}, bf16[2,64,4096]{2,1,0:T(8,128)(2,1)}, u32[]{:S(2)}) copy-start(bf16[2,64,4096]{2,1,0:T(8,128)(2,1)} %param.16) | copy-start | bytes 3145732
  152.6 25.8 %copy-start.31 = (f32[4096]{0:T(1024)S(1)}, f32[4096]{0:T(1024)}, u32[]{:S(2)}) copy-start(f32[4096]{0:T(1024)} %param.18) | copy-start | bytes 49156
  152.6 24.6 %collective-permute-start.5 = (bf16[128,2048]{1,0:T(8,128)(2,1)S(1)}, bf16[128,2048]{1,0:T(8,128)(2,1)S(1)}, u32[]{:S(2)}, u32[]{:S(2)}) collective-permute-start(bf16[128,2048]{1,0:T(8,128)(2,1)S(1)} %get-tuple-element.50), channel_id=1, source_target_pairs={{0,2},{2,4},{4,6},{6,0},{1,3},{3,5},{5,7},{7,1},{8,10},{10,12},{12... | collective-permute-start | bytes 1572872 | tf_op jit(solution)/shard_map/ppermute | solution.py:552
  152.6 24.6 %collective-permute-start.6 = (bf16[128,2048]{1,0:T(8,128)(2,1)S(1)}, bf16[128,2048]{1,0:T(8,128)(2,1)S(1)}, u32[]{:S(2)}, u32[]{:S(2)}) collective-permute-start(bf16[128,2048]{1,0:T(8,128)(2,1)S(1)} %get-tuple-element.51), channel_id=1, source_target_pairs={{0,6},{2,0},{4,2},{6,4},{1,7},{3,1},{5,3},{7,5},{8,14},{10,8},{12,... | collective-permute-start | bytes 1572872 | tf_op jit(solution)/shard_map/ppermute | solution.py:553
  155.4 21.7 %collective-permute-start.3 = (bf16[128,2048]{1,0:T(8,128)(2,1)S(1)}, bf16[128,2048]{1,0:T(8,128)(2,1)S(1)}, u32[]{:S(2)}, u32[]{:S(2)}) collective-permute-start(bf16[128,2048]{1,0:T(8,128)(2,1)S(1)} %add_convert_fusion.2), channel_id=1, source_target_pairs={{0,2},{2,4},{4,6},{6,0},{1,3},{3,5},{5,7},{7,1},{8,10},{10,12},{12... | collective-permute-start | bytes 1572872 | tf_op jit(solution)/shard_map/ppermute | solution.py:554
  155.7 22.7 %collective-permute-start.8 = (bf16[128,2048]{1,0:T(8,128)(2,1)S(1)}, bf16[128,2048]{1,0:T(8,128)(2,1)S(1)}, u32[]{:S(2)}, u32[]{:S(2)}) collective-permute-start(bf16[128,2048]{1,0:T(8,128)(2,1)S(1)} %add_convert_fusion.1), channel_id=1, source_target_pairs={{0,6},{2,0},{4,2},{6,4},{1,7},{3,1},{5,3},{7,5},{8,14},{10,8},{12,... | collective-permute-start | bytes 1572872 | tf_op jit(solution)/shard_map/ppermute | solution.py:555
  176.9 6.7 %copy-start.16 = (bf16[384,2048]{1,0:T(8,128)(2,1)}, bf16[384,2048]{1,0:T(8,128)(2,1)S(1)}, u32[]{:S(2)}) copy-start(bf16[384,2048]{1,0:T(8,128)(2,1)S(1)} %collective-permute-done.4.refs_4_) | copy-start | bytes 4718596
  186.7 48.7 %all-to-all-start.3 = ((bf16[64,24,1024]{2,1,0:T(8,128)(2,1)}), bf16[64,24,1024]{2,1,0:T(8,128)(2,1)S(1)}, u32[]{:S(2)}, u32[]{:S(2)}) async-start(bf16[64,24,1024]{2,1,0:T(8,128)(2,1)} %bitcast.37), calls=%async_computation.3 | async-start | bytes 6291456 | tf_op jit(solution)/shard_map/all_to_all | solution.py:560
  195.3 56.3 %collective-permute-start.9 = (bf16[384,1024]{1,0:T(8,128)(2,1)}, bf16[384,1024]{1,0:T(8,128)(2,1)}, u32[]{:S(2)}, u32[]{:S(2)}) collective-permute-start(bf16[384,1024]{1,0:T(8,128)(2,1)} %copy-done.21), channel_id=1, source_target_pairs={{0,64},{64,0},{1,65},{65,1},{2,66},{66,2},{3,67},{67,3},{4,68},{68... | collective-permute-start | bytes 2359304 | tf_op jit(solution)/shard_map/ppermute | solution.py:546
  243.5 12.2 %copy-start.4 = (bf16[4,384,1024]{2,1,0:T(8,128)(2,1)}, bf16[4,384,1024]{2,1,0:T(8,128)(2,1)S(1)}, u32[]{:S(2)}) copy-start(bf16[4,384,1024]{2,1,0:T(8,128)(2,1)S(1)} %get-tuple-element.61.x_ref) | copy-start | bytes 9437188
  243.5 12.2 %copy-start.1 = (bf16[1,512,4096]{2,1,0:T(8,128)(2,1)S(1)}, bf16[1,512,4096]{2,1,0:T(8,128)(2,1)}, u32[]{:S(2)}) copy-start(bf16[1,512,4096]{2,1,0:T(8,128)(2,1)} %param.24) | copy-start | bytes 12582916
  243.5 12.2 %collective-permute-start.10 = (bf16[384,256]{1,0:T(8,128)(2,1)S(1)}, bf16[384,256]{1,0:T(8,128)(2,1)S(1)}, u32[]{:S(2)}, u32[]{:S(2)}) collective-permute-start(bf16[384,256]{1,0:T(8,128)(2,1)S(1)} %get-tuple-element.58), channel_id=1, source_target_pairs={{0,64},{64,0},{1,65},{65,1},{2,66},{66,2},{3,67},{67,3},{4,68},{68... | collective-permute-start | bytes 589832 | tf_op jit(solution)/shard_map/ppermute | solution.py:565
  248.3 77.8 %collective-permute-start.11 = (bf16[4096,256]{1,0:T(8,128)(2,1)}, bf16[4096,256]{1,0:T(8,128)(2,1)}, u32[]{:S(2)}, u32[]{:S(2)}) collective-permute-start(bf16[4096,256]{1,0:T(8,128)(2,1)} %up_half.3), channel_id=1, source_target_pairs={{0,64},{64,0},{1,65},{65,1},{2,66},{66,2},{3,67},{67,3},{4,68},{68... | collective-permute-start | bytes 6291464 | tf_op jit(solution)/shard_map/ppermute | solution.py:569
  255.7 5.3 %copy-start.27 = (bf16[384,256]{1,0:T(8,128)(2,1)}, bf16[384,256]{1,0:T(8,128)(2,1)S(1)}, u32[]{:S(2)}) copy-start(bf16[384,256]{1,0:T(8,128)(2,1)S(1)} %collective-permute-done.10.hf_ref) | copy-start | bytes 589828
  262.6 69.0 %all-to-all-start.4 = ((bf16[64,24,1024]{2,1,0:T(8,128)(2,1)}), bf16[64,24,1024]{2,1,0:T(8,128)(2,1)S(1)}, u32[]{:S(2)}, u32[]{:S(2)}) async-start(bf16[64,24,1024]{2,1,0:T(8,128)(2,1)} %bitcast.33), calls=%async_computation.4 | async-start | bytes 6291456 | tf_op jit(solution)/shard_map/all_to_all | solution.py:567
  274.6 2.3 copy-start.24
  274.6 2.3 copy-start.28
  (21 other events, 31.0 us)

commit v7 on v5

--- a/solution.py
+++ b/solution.py
@@ -523,13 +523,13 @@
         place, arrived, up_weight[0], back
     )
     hid_far = lax.ppermute(hid_other, "dp", swap)
-    hidden, far_2 = lax.optimization_barrier((hidden, far_2))
-    returned = exchange(expert_out(hidden, down_weight[0]), ALL)
+    products = expert_out(hidden, down_weight[0])
+    products, far_2, hid_far = lax.optimization_barrier((products, far_2, hid_far))
+    returned = exchange(products, ALL)
     up_other = up_half(own_rows, pre_other)
     up_far = lax.ppermute(up_other, "dp", swap)
     block_out = combine(returned, stream, gate, target, weight_col)
     up_own = up_half(own_rows, pre_own)
-    block_out, hid_far = lax.optimization_barrier((block_out, hid_far))
     down_total = down_sum(hid_own, grads, hid_far, (far_0, far_1, far_2))
     up_total = plus(up_own, up_far)
     return (block_out.reshape(2, TOK // 2, D), up_total[None], down_total[None])

time: 338 us -> 336 us (level)
    ppermute x3, waiting for transfers between devices: 27.4 us -> 24 us  [body(): far_0, far_1, far_2 = [lax.ppermute(g, 'dp', swap) for g in grads]]
    unnamed x72 -> x74, local copies, waits for them, and re-layouts: 28.7 us -> 29.7 us
  transfers between devices with their start and end apart: 17 -> 17, of which waited for: 12 -> 11; matrix products, arithmetic and copies ran while one was open for 1% -> 1% of each run, Pallas kernels for 16% -> 17%
where the time goes in v7:
time: 336 us; the launch traced here: 334 us
  waiting for transfers between devices  176 us (52%)
  Pallas kernels  66 us (20%)
  starting transfers between devices  56.7 us (17%)
  local copies, waits for them, and re-layouts  30.3 us (9%)
  other arithmetic  4.08 us (1%)
    ppermute x1, waiting for transfers between devices, body(): up_far = lax.ppermute(up_other, 'dp', swap)  50.3 us
    all_to_all x1, waiting for transfers between devices, body(): arrived = exchange(chunks, ALL)  37.9 us
    all_to_all x1, waiting for transfers between devices, body(): rows = exchange(pack(queries, keys, values), SEQ)  37.6 us
    unnamed x74, local copies, waits for them, and re-layouts  29.7 us
    ppermute x3, waiting for transfers between devices, body(): far_0, far_1, far_2 = [lax.ppermute(g, 'dp', swap) for g in grads]  24 us
    pallas_call x1, Pallas kernels, attend(): pl.pallas_call(kernel, grid=(8,), in_specs=[pl.BlockSpec((1, 1, 512, HEAD...  23.4 us
    all_to_all x1, waiting for transfers between devices, body(): grad_arrived = exchange(grad_chunks, ALL)  13.7 us
    pallas_call x2, Pallas kernels, project(): pl.pallas_call(kernel, in_specs=[scalars()] + resident(3), out_specs=resi...  12.6 us
  transfers between devices with their start and end apart: 17, of which 11 were waited for; matrix products, arithmetic and copies ran while one was open for 1% of the time, Pallas kernels for 17%

profile of v7, /device:TPU:1, one launch (start us, length us, event | category | flops | bytes accessed | tf_op | source)
XLA Modules:
  0.0 333.7 jit_solution(545573944426817961)
XLA Ops:
  0.6 4.4 %pack_heads.1 = bf16[8,3,512,128]{3,2,1,0:T(8,128)(2,1)} custom-call(bf16[2,512,512]{2,1,0:T(8,128)(2,1)} %q_ref.1, bf16[2,512,512]{2,1,0:T(8,128)(2,1)} %k_ref.1, bf16[2,512,512]{2,1,0:T(8,128)(2,1)} %v_ref.1), custom_call_target="tpu_custom_call" | custom-call | tf_op jit(solution)/shard_map/pack_heads/pallas_call | solution.py:82
  5.0 6.0 %all-to-all-start = ((bf16[8,3,512,128]{3,2,1,0:T(8,128)(2,1)}), bf16[8,3,512,128]{3,2,1,0:T(8,128)(2,1)S(1)}, u32[]{:S(2)}, u32[]{:S(2)}) async-start(bf16[8,3,512,128]{3,2,1,0:T(8,128)(2,1)} %pack_heads.1), calls=%async_computation | async-start | bytes 6291456 | tf_op jit(solution)/shard_map/all_to_all | solution.py:494
  18.2 37.6 %all-to-all-done.q_ref.qn_ref.k_ref.v_ref = bf16[8,3,512,128]{3,2,1,0:T(8,128)(2,1)S(1)} async-done(((bf16[8,3,512,128]{3,2,1,0:T(8,128)(2,1)}), bf16[8,3,512,128]{3,2,1,0:T(8,128)(2,1)S(1)}, u32[]{:S(2)}, u32[]{:S(2)}) %all-to-all-start) | async-done | bytes 3145760 | tf_op jit(solution)/shard_map/all_to_all | solution.py:494
  57.6 8.1 %all-to-all-start.1 = ((bf16[64,24,1024]{2,1,0:T(8,128)(2,1)}), bf16[64,24,1024]{2,1,0:T(8,128)(2,1)S(1)}, u32[]{:S(2)}, u32[]{:S(2)}) async-start(bf16[64,24,1024]{2,1,0:T(8,128)(2,1)} %bitcast.35), calls=%async_computation.1 | async-start | bytes 6291456 | tf_op jit(solution)/shard_map/all_to_all | solution.py:499
  67.6 23.4 %attend.1 = bf16[8,2,4,64,128]{4,3,2,1,0:T(8,128)(2,1)S(1)} custom-call(bf16[8,3,512,128]{3,2,1,0:T(8,128)(2,1)S(1)} %copy-done.9, bf16[8,3,512,128]{3,2,1,0:T(8,128)(2,1)S(1)} %copy-done.9, bf16[8,3,512,128]{3,2,1,0:T(8,128)(2,1)S(1)} %copy-done.9, bf16[8,3,512,128]{3,2,1,0:T(8,128)(2,1)S(1)} %copy-done.9), custom_call_target="tpu_custom_call" | custom-call | flops 17179869184 | bytes 4194304 | tf_op jit(solution)/shard_map/attend/pallas_call | solution.py:144
  92.0 13.7 %all-to-all-done.1 = bf16[64,24,1024]{2,1,0:T(8,128)(2,1)S(1)} async-done(((bf16[64,24,1024]{2,1,0:T(8,128)(2,1)}), bf16[64,24,1024]{2,1,0:T(8,128)(2,1)S(1)}, u32[]{:S(2)}, u32[]{:S(2)}) %all-to-all-start.1) | async-done | bytes 3145760 | tf_op jit(solution)/shard_map/all_to_all | solution.py:499
  105.7 4.3 %all-to-all-start.2 = ((bf16[16,256,128]{2,1,0:T(8,128)(2,1)}), bf16[16,256,128]{2,1,0:T(8,128)(2,1)}, u32[]{:S(2)}, u32[]{:S(2)}) async-start(bf16[16,256,128]{2,1,0:T(8,128)(2,1)} %bitcast.39), calls=%async_computation.2 | async-start | bytes 2097152 | tf_op jit(solution)/shard_map/all_to_all | solution.py:503
  110.0 2.2 copy-done
  112.2 2.6 grads_in.1
  117.7 2.6 collective-permute-start
  120.4 5.4 %all-to-all-done.2 = bf16[16,256,128]{2,1,0:T(8,128)(2,1)} async-done(((bf16[16,256,128]{2,1,0:T(8,128)(2,1)}), bf16[16,256,128]{2,1,0:T(8,128)(2,1)}, u32[]{:S(2)}, u32[]{:S(2)}) %all-to-all-start.2) | async-done | bytes 1048608 | tf_op jit(solution)/shard_map/all_to_all | solution.py:503
  125.9 2.2 copy-done.6
  128.1 5.3 %project.3 = (bf16[128,2048]{1,0:T(8,128)(2,1)S(1)}, bf16[128,2048]{1,0:T(8,128)(2,1)S(1)}) custom-call(s32[3]{0:T(128)S(1)} %pad_add_fusion.place_ref, bf16[2,4,2,4,64,128]{5,4,3,2,1,0:T(8,128)(2,1)} %bitcast.12.a_ref, bf16[512,4096]{1,0:T(8,128)(2,1)S(1)} %copy-done.6, bf16[512,4096]{1,0:T(8,128)(2,1)} %collective-permute-done.1.ws_ref), custom_call_target="tpu_custom_call" | custom-call | flops 1073741824 | bytes 1048576 | tf_op jit(solution)/shard_map/project/pallas_call | solution.py:202
  134.6 2.6 collective-permute-start.4
  137.2 6.1 %collective-permute-done.refs_3_ = bf16[384,1024]{1,0:T(8,128)(2,1)S(1)} collective-permute-done((bf16[384,1024]{1,0:T(8,128)(2,1)}, bf16[384,1024]{1,0:T(8,128)(2,1)S(1)}, u32[]{:S(2)}, u32[]{:S(2)}) %collective-permute-start) | collective-permute-done | bytes 786464 | tf_op jit(solution)/shard_map/ppermute | solution.py:506
  145.2 7.3 %project.2 = (bf16[128,2048]{1,0:T(8,128)(2,1)S(1)}, bf16[128,2048]{1,0:T(8,128)(2,1)S(1)}, bf16[128,2048]{1,0:T(8,128)(2,1)S(1)}, bf16[128,2048]{1,0:T(8,128)(2,1)S(1)}, bf16[128,4096]{1,0:T(8,128)(2,1)S(1)}) custom-call(s32[3]{0:T(128)S(1)} %pad_add_fusion.place_ref, bf16[2,4,2,4,64,128]{5,4,3,2,1,0:T(8,128)(2,1)} %bitcast.12.a_ref, ...), custom_call_target="tpu_custom_call" | custom-call | flops 3221225472 | bytes 1048576 | tf_op jit(solution)/shard_map/project/pallas_call | solution.py:202
  152.6 2.7 collective-permute-start.6
  155.7 3.3 collective-permute-start.8
  159.0 18.0 %collective-permute-done.4.refs_4_ = bf16[384,2048]{1,0:T(8,128)(2,1)S(1)} collective-permute-done((bf16[384,2048]{1,0:T(8,128)(2,1)S(1)}, bf16[384,2048]{1,0:T(8,128)(2,1)S(1)}, u32[]{:S(2)}, u32[]{:S(2)}) %collective-permute-start.4) | collective-permute-done | bytes 1572896 | tf_op jit(solution)/shard_map/ppermute | solution.py:506
  178.4 2.6 norm_send.1
  183.9 8.6 %all-to-all-start.3 = ((bf16[64,24,1024]{2,1,0:T(8,128)(2,1)}), bf16[64,24,1024]{2,1,0:T(8,128)(2,1)S(1)}, u32[]{:S(2)}, u32[]{:S(2)}) async-start(bf16[64,24,1024]{2,1,0:T(8,128)(2,1)} %bitcast.37), calls=%async_computation.3 | async-start | bytes 6291456 | tf_op jit(solution)/shard_map/all_to_all | solution.py:520
  194.7 37.9 %all-to-all-done.3 = bf16[64,24,1024]{2,1,0:T(8,128)(2,1)S(1)} async-done(((bf16[64,24,1024]{2,1,0:T(8,128)(2,1)}), bf16[64,24,1024]{2,1,0:T(8,128)(2,1)S(1)}, u32[]{:S(2)}, u32[]{:S(2)}) %all-to-all-start.3) | async-done | bytes 3145760 | tf_op jit(solution)/shard_map/all_to_all | solution.py:520
  232.6 2.2 copy-done.7
  235.9 3.5 %hidden_units.1 = (bf16[4,384,1024]{2,1,0:T(8,128)(2,1)S(1)}, bf16[384,512]{1,0:T(8,128)(2,1)S(1)}, bf16[384,256]{1,0:T(8,128)(2,1)S(1)}, bf16[384,256]{1,0:T(8,...) custom-call(s32[3]{0:T(128)S(1)} %pad_add_fusion.place_ref, bf16[1536,1024]{1,0:T(8,128)(2,1)S(1)} %bitcast.34, ...), custom_call_target="tpu_custom_call" | custom-call | tf_op jit(solution)/shard_map/hidden_units/pallas_call | solution.py:357
  242.1 2.7 up_half.3
  245.7 2.6 expert_out.1
  249.9 3.0 collective-permute-done.10.hf_ref
  253.7 9.1 %all-to-all-start.4 = ((bf16[64,24,1024]{2,1,0:T(8,128)(2,1)}), bf16[64,24,1024]{2,1,0:T(8,128)(2,1)S(1)}, u32[]{:S(2)}, u32[]{:S(2)}) async-start(bf16[64,24,1024]{2,1,0:T(8,128)(2,1)} %bitcast.33), calls=%async_computation.4 | async-start | bytes 6291456 | tf_op jit(solution)/shard_map/all_to_all | solution.py:528
  268.0 5.0 %down_sum.1 = bf16[256,4096]{1,0:T(8,128)(2,1)} custom-call(bf16[384,256]{1,0:T(8,128)(2,1)S(1)} %get-tuple-element.64.h_ref, bf16[384,256]{1,0:T(8,128)(2,1)S(1)} %copy-done.28, bf16[384,1024]{1,0:T(8,128)(2,1)} %get-tuple-element.42.refs_0_, bf16[384,2048]{1,0:T(8,128)(2,1)S(1)} %copy-done.15, bf16[384,1024]{1,0:T(8,128)(2,1)S(1)} %copy-done.22, ...), custom_call_target="tpu_custom_call" | custom-call | flops 1610612736 | bytes 9437184 | tf_op jit(solution)/shard_map/down_sum/pallas_call | solution.py:426
  273.0 50.3 %collective-permute-done.11 = bf16[4096,256]{1,0:T(8,128)(2,1)} collective-permute-done((bf16[4096,256]{1,0:T(8,128)(2,1)}, bf16[4096,256]{1,0:T(8,128)(2,1)}, u32[]{:S(2)}, u32[]{:S(2)}) %collective-permute-start.11) | collective-permute-done | bytes 2097184 | tf_op jit(solution)/shard_map/ppermute | solution.py:530
  323.3 3.4 %fusion = bf16[1,4096,256]{2,1,0:T(8,128)(2,1)} fusion(bf16[4096,256]{1,0:T(8,128)(2,1)} %collective-permute-done.11, bf16[4096,256]{1,0:T(8,128)(2,1)S(1)} %up_half.2), kind=kLoop, calls=%fused_computation.1 | loop fusion | flops 4194304 | bytes 6291456 | tf_op jit(solution)/shard_map/broadcast_in_dim | solution.py:535
  330.5 3.1 combine.1
  (109 shorter events, 40.8 us)
Async XLA Ops:
  5.0 7.0 %copy-start.33 = (s32[2,64,2]{1,2,0:T(2,128)S(1)}, s32[2,64,2]{1,2,0:T(2,128)}, u32[]{:S(2)}) copy-start(s32[2,64,2]{1,2,0:T(2,128)} %param.19) | copy-start | bytes 3076
  5.0 7.3 %copy-start.34 = (f32[2,64,2]{1,2,0:T(2,128)S(1)}, f32[2,64,2]{1,2,0:T(2,128)}, u32[]{:S(2)}) copy-start(f32[2,64,2]{1,2,0:T(2,128)} %param.20) | copy-start | bytes 3076
  5.0 8.0 %copy-start.35 = (s32[2]{0:T(128)S(1)}, s32[2]{0:T(128)}, u32[]{:S(2)}) copy-start(s32[2]{0:T(128)} %param.21) | copy-start | bytes 28
  5.0 8.1 %copy-start.32 = (f32[2,4096]{1,0:T(2,128)S(1)}, f32[2,4096]{1,0:T(2,128)}, u32[]{:S(2)}) copy-start(f32[2,4096]{1,0:T(2,128)} %param.22) | copy-start | bytes 98308
  5.0 50.8 %all-to-all-start = ((bf16[8,3,512,128]{3,2,1,0:T(8,128)(2,1)}), bf16[8,3,512,128]{3,2,1,0:T(8,128)(2,1)S(1)}, u32[]{:S(2)}, u32[]{:S(2)}) async-start(bf16[8,3,512,128]{3,2,1,0:T(8,128)(2,1)} %pack_heads.1), calls=%async_computation | async-start | bytes 6291456 | tf_op jit(solution)/shard_map/all_to_all | solution.py:494
  11.0 114.9 %collective-permute-start.1 = (bf16[512,4096]{1,0:T(8,128)(2,1)}, bf16[512,4096]{1,0:T(8,128)(2,1)}, u32[]{:S(2)}, u32[]{:S(2)}) collective-permute-start(bf16[512,4096]{1,0:T(8,128)(2,1)} %wo_ref.3), channel_id=1, source_target_pairs={{0,1},{1,0},{2,3},{3,2},{4,5},{5,4},{6,7},{7,6},{8,9},{9,8},{10,11... | collective-permute-start | bytes 12582920 | tf_op jit(solution)/shard_map/ppermute | solution.py:495
  57.6 48.1 %all-to-all-start.1 = ((bf16[64,24,1024]{2,1,0:T(8,128)(2,1)}), bf16[64,24,1024]{2,1,0:T(8,128)(2,1)S(1)}, u32[]{:S(2)}, u32[]{:S(2)}) async-start(bf16[64,24,1024]{2,1,0:T(8,128)(2,1)} %bitcast.35), calls=%async_computation.1 | async-start | bytes 6291456 | tf_op jit(solution)/shard_map/all_to_all | solution.py:499
  105.7 20.2 %all-to-all-start.2 = ((bf16[16,256,128]{2,1,0:T(8,128)(2,1)}), bf16[16,256,128]{2,1,0:T(8,128)(2,1)}, u32[]{:S(2)}, u32[]{:S(2)}) async-start(bf16[16,256,128]{2,1,0:T(8,128)(2,1)} %bitcast.39), calls=%async_computation.2 | async-start | bytes 2097152 | tf_op jit(solution)/shard_map/all_to_all | solution.py:503
  117.7 25.5 %collective-permute-start = (bf16[384,1024]{1,0:T(8,128)(2,1)}, bf16[384,1024]{1,0:T(8,128)(2,1)S(1)}, u32[]{:S(2)}, u32[]{:S(2)}) collective-permute-start(bf16[384,1024]{1,0:T(8,128)(2,1)} %get-tuple-element.42.refs_0_), channel_id=1, source_target_pairs={{0,64},{64,0},{1,65},{65,1},{2,66},{66,2},{3,67},{67,3},{4,68},{68... | collective-permute-start | bytes 2359304 | tf_op jit(solution)/shard_map/ppermute | solution.py:506
  125.9 2.2 copy-start.6
  128.1 6.5 %copy-start.14 = (bf16[384,2048]{1,0:T(8,128)(2,1)S(1)}, bf16[384,2048]{1,0:T(8,128)(2,1)}, u32[]{:S(2)}) copy-start(bf16[384,2048]{1,0:T(8,128)(2,1)} %copy-done.13) | copy-start | bytes 4718596
  133.4 21.9 %collective-permute-start.2 = (bf16[128,2048]{1,0:T(8,128)(2,1)S(1)}, bf16[128,2048]{1,0:T(8,128)(2,1)S(1)}, u32[]{:S(2)}, u32[]{:S(2)}) collective-permute-start(bf16[128,2048]{1,0:T(8,128)(2,1)S(1)} %get-tuple-element.46), channel_id=1, source_target_pairs={{0,2},{2,4},{4,6},{6,0},{1,3},{3,5},{5,7},{7,1},{8,10},{10,12},{12... | collective-permute-start | bytes 1572872 | tf_op jit(solution)/shard_map/ppermute | solution.py:508
  134.6 42.4 %collective-permute-start.4 = (bf16[384,2048]{1,0:T(8,128)(2,1)S(1)}, bf16[384,2048]{1,0:T(8,128)(2,1)S(1)}, u32[]{:S(2)}, u32[]{:S(2)}) collective-permute-start(bf16[384,2048]{1,0:T(8,128)(2,1)S(1)} %copy-done.14), channel_id=1, source_target_pairs={{0,64},{64,0},{1,65},{65,1},{2,66},{66,2},{3,67},{67,3},{4,68},{68... | collective-permute-start | bytes 4718600 | tf_op jit(solution)/shard_map/ppermute | solution.py:506
  143.2 9.3 %copy-start.23 = (bf16[384,1024]{1,0:T(8,128)(2,1)}, bf16[384,1024]{1,0:T(8,128)(2,1)S(1)}, u32[]{:S(2)}) copy-start(bf16[384,1024]{1,0:T(8,128)(2,1)S(1)} %collective-permute-done.refs_3_) | copy-start | bytes 2359300
  143.2 12.3 %collective-permute-start.7 = (bf16[128,2048]{1,0:T(8,128)(2,1)S(1)}, bf16[128,2048]{1,0:T(8,128)(2,1)S(1)}, u32[]{:S(2)}, u32[]{:S(2)}) collective-permute-start(bf16[128,2048]{1,0:T(8,128)(2,1)S(1)} %get-tuple-element.53), channel_id=1, source_target_pairs={{0,6},{2,0},{4,2},{6,4},{1,7},{3,1},{5,3},{7,5},{8,14},{10,8},{12,... | collective-permute-start | bytes 1572872 | tf_op jit(solution)/shard_map/ppermute | solution.py:509
  152.5 25.8 %copy-start.18 = (bf16[2,64,4096]{2,1,0:T(8,128)(2,1)S(1)}, bf16[2,64,4096]{2,1,0:T(8,128)(2,1)}, u32[]{:S(2)}) copy-start(bf16[2,64,4096]{2,1,0:T(8,128)(2,1)} %param.16) | copy-start | bytes 3145732
  152.6 25.8 %copy-start.31 = (f32[4096]{0:T(1024)S(1)}, f32[4096]{0:T(1024)}, u32[]{:S(2)}) copy-start(f32[4096]{0:T(1024)} %param.18) | copy-start | bytes 49156
  152.6 24.6 %collective-permute-start.5 = (bf16[128,2048]{1,0:T(8,128)(2,1)S(1)}, bf16[128,2048]{1,0:T(8,128)(2,1)S(1)}, u32[]{:S(2)}, u32[]{:S(2)}) collective-permute-start(bf16[128,2048]{1,0:T(8,128)(2,1)S(1)} %get-tuple-element.50), channel_id=1, source_target_pairs={{0,2},{2,4},{4,6},{6,0},{1,3},{3,5},{5,7},{7,1},{8,10},{10,12},{12... | collective-permute-start | bytes 1572872 | tf_op jit(solution)/shard_map/ppermute | solution.py:512
  152.6 24.6 %collective-permute-start.6 = (bf16[128,2048]{1,0:T(8,128)(2,1)S(1)}, bf16[128,2048]{1,0:T(8,128)(2,1)S(1)}, u32[]{:S(2)}, u32[]{:S(2)}) collective-permute-start(bf16[128,2048]{1,0:T(8,128)(2,1)S(1)} %get-tuple-element.51), channel_id=1, source_target_pairs={{0,6},{2,0},{4,2},{6,4},{1,7},{3,1},{5,3},{7,5},{8,14},{10,8},{12,... | collective-permute-start | bytes 1572872 | tf_op jit(solution)/shard_map/ppermute | solution.py:513
  155.4 21.7 %collective-permute-start.3 = (bf16[128,2048]{1,0:T(8,128)(2,1)S(1)}, bf16[128,2048]{1,0:T(8,128)(2,1)S(1)}, u32[]{:S(2)}, u32[]{:S(2)}) collective-permute-start(bf16[128,2048]{1,0:T(8,128)(2,1)S(1)} %add_convert_fusion.2), channel_id=1, source_target_pairs={{0,2},{2,4},{4,6},{6,0},{1,3},{3,5},{5,7},{7,1},{8,10},{10,12},{12... | collective-permute-start | bytes 1572872 | tf_op jit(solution)/shard_map/ppermute | solution.py:514
  155.7 22.6 %collective-permute-start.8 = (bf16[128,2048]{1,0:T(8,128)(2,1)S(1)}, bf16[128,2048]{1,0:T(8,128)(2,1)S(1)}, u32[]{:S(2)}, u32[]{:S(2)}) collective-permute-start(bf16[128,2048]{1,0:T(8,128)(2,1)S(1)} %add_convert_fusion.1), channel_id=1, source_target_pairs={{0,6},{2,0},{4,2},{6,4},{1,7},{3,1},{5,3},{7,5},{8,14},{10,8},{12,... | collective-permute-start | bytes 1572872 | tf_op jit(solution)/shard_map/ppermute | solution.py:515
  176.9 4.0 %copy-start.16 = (bf16[384,2048]{1,0:T(8,128)(2,1)}, bf16[384,2048]{1,0:T(8,128)(2,1)S(1)}, u32[]{:S(2)}) copy-start(bf16[384,2048]{1,0:T(8,128)(2,1)S(1)} %collective-permute-done.4.refs_4_) | copy-start | bytes 4718596
  183.9 48.7 %all-to-all-start.3 = ((bf16[64,24,1024]{2,1,0:T(8,128)(2,1)}), bf16[64,24,1024]{2,1,0:T(8,128)(2,1)S(1)}, u32[]{:S(2)}, u32[]{:S(2)}) async-start(bf16[64,24,1024]{2,1,0:T(8,128)(2,1)} %bitcast.37), calls=%async_computation.3 | async-start | bytes 6291456 | tf_op jit(solution)/shard_map/all_to_all | solution.py:520
  192.6 57.4 %collective-permute-start.9 = (bf16[384,1024]{1,0:T(8,128)(2,1)}, bf16[384,1024]{1,0:T(8,128)(2,1)}, u32[]{:S(2)}, u32[]{:S(2)}) collective-permute-start(bf16[384,1024]{1,0:T(8,128)(2,1)} %copy-done.21), channel_id=1, source_target_pairs={{0,64},{64,0},{1,65},{65,1},{2,66},{66,2},{3,67},{67,3},{4,68},{68... | collective-permute-start | bytes 2359304 | tf_op jit(solution)/shard_map/ppermute | solution.py:506
  232.6 2.2 copy-start.7
  240.1 5.6 %copy-start.4 = (bf16[4,384,1024]{2,1,0:T(8,128)(2,1)}, bf16[4,384,1024]{2,1,0:T(8,128)(2,1)S(1)}, u32[]{:S(2)}) copy-start(bf16[4,384,1024]{2,1,0:T(8,128)(2,1)S(1)} %get-tuple-element.61.x_ref) | copy-start | bytes 9437188
  240.1 5.6 %copy-start.1 = (bf16[1,512,4096]{2,1,0:T(8,128)(2,1)S(1)}, bf16[1,512,4096]{2,1,0:T(8,128)(2,1)}, u32[]{:S(2)}) copy-start(bf16[1,512,4096]{2,1,0:T(8,128)(2,1)} %param.24) | copy-start | bytes 12582916
  240.1 12.9 %collective-permute-start.10 = (bf16[384,256]{1,0:T(8,128)(2,1)S(1)}, bf16[384,256]{1,0:T(8,128)(2,1)S(1)}, u32[]{:S(2)}, u32[]{:S(2)}) collective-permute-start(bf16[384,256]{1,0:T(8,128)(2,1)S(1)} %get-tuple-element.58), channel_id=1, source_target_pairs={{0,64},{64,0},{1,65},{65,1},{2,66},{66,2},{3,67},{67,3},{4,68},{68... | collective-permute-start | bytes 589832 | tf_op jit(solution)/shard_map/ppermute | solution.py:525
  244.8 78.5 %collective-permute-start.11 = (bf16[4096,256]{1,0:T(8,128)(2,1)}, bf16[4096,256]{1,0:T(8,128)(2,1)}, u32[]{:S(2)}, u32[]{:S(2)}) collective-permute-start(bf16[4096,256]{1,0:T(8,128)(2,1)} %up_half.3), channel_id=1, source_target_pairs={{0,64},{64,0},{1,65},{65,1},{2,66},{66,2},{3,67},{67,3},{4,68},{68... | collective-permute-start | bytes 6291464 | tf_op jit(solution)/shard_map/ppermute | solution.py:530
  253.7 75.3 %all-to-all-start.4 = ((bf16[64,24,1024]{2,1,0:T(8,128)(2,1)}), bf16[64,24,1024]{2,1,0:T(8,128)(2,1)S(1)}, u32[]{:S(2)}, u32[]{:S(2)}) async-start(bf16[64,24,1024]{2,1,0:T(8,128)(2,1)} %bitcast.33), calls=%async_computation.4 | async-start | bytes 6291456 | tf_op jit(solution)/shard_map/all_to_all | solution.py:528
  265.7 2.3 copy-start.24
  265.7 2.3 copy-start.28
  (21 other events, 29.5 us)

commit v8 on v7

--- a/solution.py
+++ b/solution.py
@@ -507,10 +507,10 @@
     fa, fb = project(place, (2,), (2,), heads, out_weight, weight_other)
     fa = lax.ppermute(fa, "z", above)
     fb = lax.ppermute(fb, "z", below)
-    heads, far_0 = lax.optimization_barrier((heads, far_0))
     ua, ub, da, db, own = project(place, (1, 3, 0), (2, 2, 1), heads, out_weight, weight_other)
     ub = lax.ppermute(ub, "z", above)
     da = lax.ppermute(da, "z", below)
+    fa, far_0 = lax.optimization_barrier((fa, far_0))
     ua = lax.ppermute(plus(ua, fa), "z", above)
     db = lax.ppermute(plus(db, fb), "z", below)
     own, ua, far_1 = lax.optimization_barrier((own, ua, far_1))

time: 336 us -> 333 us (level)
  transfers between devices with their start and end apart: 17 -> 17, of which waited for: 11 -> 9; matrix products, arithmetic and copies ran while one was open for 1% -> 1% of each run, Pallas kernels for 17% -> 17%
where the time goes in v8:
time: 333 us; the launch traced here: 331 us
  waiting for transfers between devices  175 us (53%)
  Pallas kernels  66 us (20%)
  starting transfers between devices  53.9 us (16%)
  local copies, waits for them, and re-layouts  30.3 us (9%)
  other arithmetic  4.08 us (1%)
    ppermute x1, waiting for transfers between devices, body(): up_far = lax.ppermute(up_other, 'dp', swap)  50.3 us
    all_to_all x1, waiting for transfers between devices, body(): arrived = exchange(chunks, ALL)  38.1 us
    all_to_all x1, waiting for transfers between devices, body(): rows = exchange(pack(queries, keys, values), SEQ)  37.6 us
    unnamed x74, local copies, waits for them, and re-layouts  29.7 us
    ppermute x3, waiting for transfers between devices, body(): far_0, far_1, far_2 = [lax.ppermute(g, 'dp', swap) for g in grads]  24.8 us
    pallas_call x1, Pallas kernels, attend(): pl.pallas_call(kernel, grid=(8,), in_specs=[pl.BlockSpec((1, 1, 512, HEAD...  23.4 us
    all_to_all x1, waiting for transfers between devices, body(): grad_arrived = exchange(grad_chunks, ALL)  13.7 us
    pallas_call x2, Pallas kernels, project(): pl.pallas_call(kernel, in_specs=[scalars()] + resident(3), out_specs=resi...  12.6 us
  transfers between devices with their start and end apart: 17, of which 9 were waited for; matrix products, arithmetic and copies ran while one was open for 1% of the time, Pallas kernels for 17%

profile of v8, /device:TPU:1, one launch (start us, length us, event | category | flops | bytes accessed | tf_op | source)
XLA Modules:
  0.0 330.6 jit_solution(750992420310369348)
XLA Ops:
  0.6 4.4 %pack_heads.1 = bf16[8,3,512,128]{3,2,1,0:T(8,128)(2,1)} custom-call(bf16[2,512,512]{2,1,0:T(8,128)(2,1)} %q_ref.1, bf16[2,512,512]{2,1,0:T(8,128)(2,1)} %k_ref.1, bf16[2,512,512]{2,1,0:T(8,128)(2,1)} %v_ref.1), custom_call_target="tpu_custom_call" | custom-call | tf_op jit(solution)/shard_map/pack_heads/pallas_call | solution.py:82
  5.0 6.0 %all-to-all-start = ((bf16[8,3,512,128]{3,2,1,0:T(8,128)(2,1)}), bf16[8,3,512,128]{3,2,1,0:T(8,128)(2,1)S(1)}, u32[]{:S(2)}, u32[]{:S(2)}) async-start(bf16[8,3,512,128]{3,2,1,0:T(8,128)(2,1)} %pack_heads.1), calls=%async_computation | async-start | bytes 6291456 | tf_op jit(solution)/shard_map/all_to_all | solution.py:494
  18.2 37.6 %all-to-all-done.q_ref.qn_ref.k_ref.v_ref = bf16[8,3,512,128]{3,2,1,0:T(8,128)(2,1)S(1)} async-done(((bf16[8,3,512,128]{3,2,1,0:T(8,128)(2,1)}), bf16[8,3,512,128]{3,2,1,0:T(8,128)(2,1)S(1)}, u32[]{:S(2)}, u32[]{:S(2)}) %all-to-all-start) | async-done | bytes 3145760 | tf_op jit(solution)/shard_map/all_to_all | solution.py:494
  57.6 8.1 %all-to-all-start.1 = ((bf16[64,24,1024]{2,1,0:T(8,128)(2,1)}), bf16[64,24,1024]{2,1,0:T(8,128)(2,1)S(1)}, u32[]{:S(2)}, u32[]{:S(2)}) async-start(bf16[64,24,1024]{2,1,0:T(8,128)(2,1)} %bitcast.35), calls=%async_computation.1 | async-start | bytes 6291456 | tf_op jit(solution)/shard_map/all_to_all | solution.py:499
  67.6 23.4 %attend.1 = bf16[8,2,4,64,128]{4,3,2,1,0:T(8,128)(2,1)S(1)} custom-call(bf16[8,3,512,128]{3,2,1,0:T(8,128)(2,1)S(1)} %copy-done.9, bf16[8,3,512,128]{3,2,1,0:T(8,128)(2,1)S(1)} %copy-done.9, bf16[8,3,512,128]{3,2,1,0:T(8,128)(2,1)S(1)} %copy-done.9, bf16[8,3,512,128]{3,2,1,0:T(8,128)(2,1)S(1)} %copy-done.9), custom_call_target="tpu_custom_call" | custom-call | flops 17179869184 | bytes 4194304 | tf_op jit(solution)/shard_map/attend/pallas_call | solution.py:144
  92.0 13.7 %all-to-all-done.1 = bf16[64,24,1024]{2,1,0:T(8,128)(2,1)S(1)} async-done(((bf16[64,24,1024]{2,1,0:T(8,128)(2,1)}), bf16[64,24,1024]{2,1,0:T(8,128)(2,1)S(1)}, u32[]{:S(2)}, u32[]{:S(2)}) %all-to-all-start.1) | async-done | bytes 3145760 | tf_op jit(solution)/shard_map/all_to_all | solution.py:499
  105.7 4.3 %all-to-all-start.2 = ((bf16[16,256,128]{2,1,0:T(8,128)(2,1)}), bf16[16,256,128]{2,1,0:T(8,128)(2,1)}, u32[]{:S(2)}, u32[]{:S(2)}) async-start(bf16[16,256,128]{2,1,0:T(8,128)(2,1)} %bitcast.39), calls=%async_computation.2 | async-start | bytes 2097152 | tf_op jit(solution)/shard_map/all_to_all | solution.py:503
  110.0 2.2 copy-done
  112.2 2.6 grads_in.1
  117.7 2.6 collective-permute-start.2
  120.4 5.4 %all-to-all-done.2 = bf16[16,256,128]{2,1,0:T(8,128)(2,1)} async-done(((bf16[16,256,128]{2,1,0:T(8,128)(2,1)}), bf16[16,256,128]{2,1,0:T(8,128)(2,1)}, u32[]{:S(2)}, u32[]{:S(2)}) %all-to-all-start.2) | async-done | bytes 1048608 | tf_op jit(solution)/shard_map/all_to_all | solution.py:503
  125.9 2.2 copy-done.6
  128.1 5.3 %project.3 = (bf16[128,2048]{1,0:T(8,128)(2,1)S(1)}, bf16[128,2048]{1,0:T(8,128)(2,1)S(1)}) custom-call(s32[3]{0:T(128)S(1)} %pad_add_fusion.place_ref, bf16[2,4,2,4,64,128]{5,4,3,2,1,0:T(8,128)(2,1)} %bitcast.12.a_ref, bf16[512,4096]{1,0:T(8,128)(2,1)S(1)} %copy-done.6, bf16[512,4096]{1,0:T(8,128)(2,1)} %collective-permute-done.ws_ref), custom_call_target="tpu_custom_call" | custom-call | flops 1073741824 | bytes 1048576 | tf_op jit(solution)/shard_map/project/pallas_call | solution.py:202
  134.6 2.6 collective-permute-start.4
  138.8 7.3 %project.2 = (bf16[128,2048]{1,0:T(8,128)(2,1)S(1)}, bf16[128,2048]{1,0:T(8,128)(2,1)S(1)}, bf16[128,2048]{1,0:T(8,128)(2,1)S(1)}, bf16[128,2048]{1,0:T(8,128)(2,1)S(1)}, bf16[128,4096]{1,0:T(8,128)(2,1)S(1)}) custom-call(s32[3]{0:T(128)S(1)} %pad_add_fusion.place_ref, bf16[2,4,2,4,64,128]{5,4,3,2,1,0:T(8,128)(2,1)} %bitcast.12.a_ref, ...), custom_call_target="tpu_custom_call" | custom-call | flops 3221225472 | bytes 1048576 | tf_op jit(solution)/shard_map/project/pallas_call | solution.py:202
  146.2 2.6 collective-permute-start.6
  149.3 2.9 collective-permute-start.8
  152.1 24.8 %collective-permute-done.4.refs_4_ = bf16[384,2048]{1,0:T(8,128)(2,1)S(1)} collective-permute-done((bf16[384,2048]{1,0:T(8,128)(2,1)S(1)}, bf16[384,2048]{1,0:T(8,128)(2,1)S(1)}, u32[]{:S(2)}, u32[]{:S(2)}) %collective-permute-start.4) | collective-permute-done | bytes 1572896 | tf_op jit(solution)/shard_map/ppermute | solution.py:506
  177.0 2.6 norm_send.1
  182.6 6.9 %all-to-all-start.3 = ((bf16[64,24,1024]{2,1,0:T(8,128)(2,1)}), bf16[64,24,1024]{2,1,0:T(8,128)(2,1)S(1)}, u32[]{:S(2)}, u32[]{:S(2)}) async-start(bf16[64,24,1024]{2,1,0:T(8,128)(2,1)} %bitcast.37), calls=%async_computation.3 | async-start | bytes 6291456 | tf_op jit(solution)/shard_map/all_to_all | solution.py:520
  191.4 38.1 %all-to-all-done.3 = bf16[64,24,1024]{2,1,0:T(8,128)(2,1)S(1)} async-done(((bf16[64,24,1024]{2,1,0:T(8,128)(2,1)}), bf16[64,24,1024]{2,1,0:T(8,128)(2,1)S(1)}, u32[]{:S(2)}, u32[]{:S(2)}) %all-to-all-start.3) | async-done | bytes 3145760 | tf_op jit(solution)/shard_map/all_to_all | solution.py:520
  229.5 2.2 copy-done.7
  232.8 3.5 %hidden_units.1 = (bf16[4,384,1024]{2,1,0:T(8,128)(2,1)S(1)}, bf16[384,512]{1,0:T(8,128)(2,1)S(1)}, bf16[384,256]{1,0:T(8,128)(2,1)S(1)}, bf16[384,256]{1,0:T(8,...) custom-call(s32[3]{0:T(128)S(1)} %pad_add_fusion.place_ref, bf16[1536,1024]{1,0:T(8,128)(2,1)S(1)} %bitcast.34, ...), custom_call_target="tpu_custom_call" | custom-call | tf_op jit(solution)/shard_map/hidden_units/pallas_call | solution.py:357
  238.8 2.7 up_half.3
  242.6 2.6 expert_out.1
  246.9 2.8 collective-permute-done.10.hf_ref
  250.4 9.1 %all-to-all-start.4 = ((bf16[64,24,1024]{2,1,0:T(8,128)(2,1)}), bf16[64,24,1024]{2,1,0:T(8,128)(2,1)S(1)}, u32[]{:S(2)}, u32[]{:S(2)}) async-start(bf16[64,24,1024]{2,1,0:T(8,128)(2,1)} %bitcast.33), calls=%async_computation.4 | async-start | bytes 6291456 | tf_op jit(solution)/shard_map/all_to_all | solution.py:528
  264.7 5.0 %down_sum.1 = bf16[256,4096]{1,0:T(8,128)(2,1)} custom-call(bf16[384,256]{1,0:T(8,128)(2,1)S(1)} %get-tuple-element.64.h_ref, bf16[384,256]{1,0:T(8,128)(2,1)S(1)} %copy-done.28, bf16[384,1024]{1,0:T(8,128)(2,1)} %get-tuple-element.45.refs_0_, bf16[384,2048]{1,0:T(8,128)(2,1)S(1)} %copy-done.15, bf16[384,1024]{1,0:T(8,128)(2,1)S(1)} %copy-done.22, ...), custom_call_target="tpu_custom_call" | custom-call | flops 1610612736 | bytes 9437184 | tf_op jit(solution)/shard_map/down_sum/pallas_call | solution.py:426
  269.7 50.3 %collective-permute-done.11 = bf16[4096,256]{1,0:T(8,128)(2,1)} collective-permute-done((bf16[4096,256]{1,0:T(8,128)(2,1)}, bf16[4096,256]{1,0:T(8,128)(2,1)}, u32[]{:S(2)}, u32[]{:S(2)}) %collective-permute-start.11) | collective-permute-done | bytes 2097184 | tf_op jit(solution)/shard_map/ppermute | solution.py:530
  320.0 3.4 %fusion = bf16[1,4096,256]{2,1,0:T(8,128)(2,1)} fusion(bf16[4096,256]{1,0:T(8,128)(2,1)} %collective-permute-done.11, bf16[4096,256]{1,0:T(8,128)(2,1)S(1)} %up_half.2), kind=kLoop, calls=%fused_computation.1 | loop fusion | flops 4194304 | bytes 6291456 | tf_op jit(solution)/shard_map/broadcast_in_dim | solution.py:535
  323.4 2.4 all-to-all-done.4
  327.4 3.1 combine.1
  (109 shorter events, 36.6 us)
Async XLA Ops:
  5.0 7.0 %copy-start.33 = (s32[2,64,2]{1,2,0:T(2,128)S(1)}, s32[2,64,2]{1,2,0:T(2,128)}, u32[]{:S(2)}) copy-start(s32[2,64,2]{1,2,0:T(2,128)} %param.19) | copy-start | bytes 3076
  5.0 7.3 %copy-start.34 = (f32[2,64,2]{1,2,0:T(2,128)S(1)}, f32[2,64,2]{1,2,0:T(2,128)}, u32[]{:S(2)}) copy-start(f32[2,64,2]{1,2,0:T(2,128)} %param.20) | copy-start | bytes 3076
  5.0 8.0 %copy-start.35 = (s32[2]{0:T(128)S(1)}, s32[2]{0:T(128)}, u32[]{:S(2)}) copy-start(s32[2]{0:T(128)} %param.21) | copy-start | bytes 28
  5.0 8.1 %copy-start.32 = (f32[2,4096]{1,0:T(2,128)S(1)}, f32[2,4096]{1,0:T(2,128)}, u32[]{:S(2)}) copy-start(f32[2,4096]{1,0:T(2,128)} %param.22) | copy-start | bytes 98308
  5.0 50.8 %all-to-all-start = ((bf16[8,3,512,128]{3,2,1,0:T(8,128)(2,1)}), bf16[8,3,512,128]{3,2,1,0:T(8,128)(2,1)S(1)}, u32[]{:S(2)}, u32[]{:S(2)}) async-start(bf16[8,3,512,128]{3,2,1,0:T(8,128)(2,1)} %pack_heads.1), calls=%async_computation | async-start | bytes 6291456 | tf_op jit(solution)/shard_map/all_to_all | solution.py:494
  11.0 114.9 %collective-permute-start = (bf16[512,4096]{1,0:T(8,128)(2,1)}, bf16[512,4096]{1,0:T(8,128)(2,1)}, u32[]{:S(2)}, u32[]{:S(2)}) collective-permute-start(bf16[512,4096]{1,0:T(8,128)(2,1)} %wo_ref.3), channel_id=1, source_target_pairs={{0,1},{1,0},{2,3},{3,2},{4,5},{5,4},{6,7},{7,6},{8,9},{9,8},{10,11... | collective-permute-start | bytes 12582920 | tf_op jit(solution)/shard_map/ppermute | solution.py:495
  57.6 48.1 %all-to-all-start.1 = ((bf16[64,24,1024]{2,1,0:T(8,128)(2,1)}), bf16[64,24,1024]{2,1,0:T(8,128)(2,1)S(1)}, u32[]{:S(2)}, u32[]{:S(2)}) async-start(bf16[64,24,1024]{2,1,0:T(8,128)(2,1)} %bitcast.35), calls=%async_computation.1 | async-start | bytes 6291456 | tf_op jit(solution)/shard_map/all_to_all | solution.py:499
  105.7 20.2 %all-to-all-start.2 = ((bf16[16,256,128]{2,1,0:T(8,128)(2,1)}), bf16[16,256,128]{2,1,0:T(8,128)(2,1)}, u32[]{:S(2)}, u32[]{:S(2)}) async-start(bf16[16,256,128]{2,1,0:T(8,128)(2,1)} %bitcast.39), calls=%async_computation.2 | async-start | bytes 2097152 | tf_op jit(solution)/shard_map/all_to_all | solution.py:503
  117.7 28.5 %collective-permute-start.2 = (bf16[384,1024]{1,0:T(8,128)(2,1)}, bf16[384,1024]{1,0:T(8,128)(2,1)S(1)}, u32[]{:S(2)}, u32[]{:S(2)}) collective-permute-start(bf16[384,1024]{1,0:T(8,128)(2,1)} %get-tuple-element.45.refs_0_), channel_id=1, source_target_pairs={{0,64},{64,0},{1,65},{65,1},{2,66},{66,2},{3,67},{67,3},{4,68},{68... | collective-permute-start | bytes 2359304 | tf_op jit(solution)/shard_map/ppermute | solution.py:506
  125.9 2.2 copy-start.6
  128.1 6.5 %copy-start.14 = (bf16[384,2048]{1,0:T(8,128)(2,1)S(1)}, bf16[384,2048]{1,0:T(8,128)(2,1)}, u32[]{:S(2)}) copy-start(bf16[384,2048]{1,0:T(8,128)(2,1)} %copy-done.13) | copy-start | bytes 4718596
  133.4 15.5 %collective-permute-start.1 = (bf16[128,2048]{1,0:T(8,128)(2,1)S(1)}, bf16[128,2048]{1,0:T(8,128)(2,1)S(1)}, u32[]{:S(2)}, u32[]{:S(2)}) collective-permute-start(bf16[128,2048]{1,0:T(8,128)(2,1)S(1)} %get-tuple-element.44), channel_id=1, source_target_pairs={{0,2},{2,4},{4,6},{6,0},{1,3},{3,5},{5,7},{7,1},{8,10},{10,12},{12... | collective-permute-start | bytes 1572872 | tf_op jit(solution)/shard_map/ppermute | solution.py:508
  134.6 42.4 %collective-permute-start.4 = (bf16[384,2048]{1,0:T(8,128)(2,1)S(1)}, bf16[384,2048]{1,0:T(8,128)(2,1)S(1)}, u32[]{:S(2)}, u32[]{:S(2)}) collective-permute-start(bf16[384,2048]{1,0:T(8,128)(2,1)S(1)} %copy-done.14), channel_id=1, source_target_pairs={{0,64},{64,0},{1,65},{65,1},{2,66},{66,2},{3,67},{67,3},{4,68},{68... | collective-permute-start | bytes 4718600 | tf_op jit(solution)/shard_map/ppermute | solution.py:506
  137.2 12.0 %collective-permute-start.7 = (bf16[128,2048]{1,0:T(8,128)(2,1)S(1)}, bf16[128,2048]{1,0:T(8,128)(2,1)S(1)}, u32[]{:S(2)}, u32[]{:S(2)}) collective-permute-start(bf16[128,2048]{1,0:T(8,128)(2,1)S(1)} %get-tuple-element.53), channel_id=1, source_target_pairs={{0,6},{2,0},{4,2},{6,4},{1,7},{3,1},{5,3},{7,5},{8,14},{10,8},{12,... | collective-permute-start | bytes 1572872 | tf_op jit(solution)/shard_map/ppermute | solution.py:509
  146.1 30.9 %copy-start.18 = (bf16[2,64,4096]{2,1,0:T(8,128)(2,1)S(1)}, bf16[2,64,4096]{2,1,0:T(8,128)(2,1)}, u32[]{:S(2)}) copy-start(bf16[2,64,4096]{2,1,0:T(8,128)(2,1)} %param.16) | copy-start | bytes 3145732
  146.1 30.9 %copy-start.31 = (f32[4096]{0:T(1024)S(1)}, f32[4096]{0:T(1024)}, u32[]{:S(2)}) copy-start(f32[4096]{0:T(1024)} %param.18) | copy-start | bytes 49156
  146.1 30.8 %collective-permute-start.5 = (bf16[128,2048]{1,0:T(8,128)(2,1)S(1)}, bf16[128,2048]{1,0:T(8,128)(2,1)S(1)}, u32[]{:S(2)}, u32[]{:S(2)}) collective-permute-start(bf16[128,2048]{1,0:T(8,128)(2,1)S(1)} %get-tuple-element.50), channel_id=1, source_target_pairs={{0,2},{2,4},{4,6},{6,0},{1,3},{3,5},{5,7},{7,1},{8,10},{10,12},{12... | collective-permute-start | bytes 1572872 | tf_op jit(solution)/shard_map/ppermute | solution.py:511
  146.2 33.3 %copy-start.23 = (bf16[384,1024]{1,0:T(8,128)(2,1)}, bf16[384,1024]{1,0:T(8,128)(2,1)S(1)}, u32[]{:S(2)}) copy-start(bf16[384,1024]{1,0:T(8,128)(2,1)S(1)} %collective-permute-done.2.refs_3_) | copy-start | bytes 2359300
  146.2 30.7 %collective-permute-start.6 = (bf16[128,2048]{1,0:T(8,128)(2,1)S(1)}, bf16[128,2048]{1,0:T(8,128)(2,1)S(1)}, u32[]{:S(2)}, u32[]{:S(2)}) collective-permute-start(bf16[128,2048]{1,0:T(8,128)(2,1)S(1)} %get-tuple-element.51), channel_id=1, source_target_pairs={{0,6},{2,0},{4,2},{6,4},{1,7},{3,1},{5,3},{7,5},{8,14},{10,8},{12,... | collective-permute-start | bytes 1572872 | tf_op jit(solution)/shard_map/ppermute | solution.py:512
  149.0 27.9 %collective-permute-start.3 = (bf16[128,2048]{1,0:T(8,128)(2,1)S(1)}, bf16[128,2048]{1,0:T(8,128)(2,1)S(1)}, u32[]{:S(2)}, u32[]{:S(2)}) collective-permute-start(bf16[128,2048]{1,0:T(8,128)(2,1)S(1)} %add_convert_fusion.2), channel_id=1, source_target_pairs={{0,2},{2,4},{4,6},{6,0},{1,3},{3,5},{5,7},{7,1},{8,10},{10,12},{12... | collective-permute-start | bytes 1572872 | tf_op jit(solution)/shard_map/ppermute | solution.py:514
  149.3 27.7 %collective-permute-start.8 = (bf16[128,2048]{1,0:T(8,128)(2,1)S(1)}, bf16[128,2048]{1,0:T(8,128)(2,1)S(1)}, u32[]{:S(2)}, u32[]{:S(2)}) collective-permute-start(bf16[128,2048]{1,0:T(8,128)(2,1)S(1)} %add_convert_fusion.1), channel_id=1, source_target_pairs={{0,6},{2,0},{4,2},{6,4},{1,7},{3,1},{5,3},{7,5},{8,14},{10,8},{12,... | collective-permute-start | bytes 1572872 | tf_op jit(solution)/shard_map/ppermute | solution.py:515
  176.9 2.6 copy-start.16
  182.6 46.9 %all-to-all-start.3 = ((bf16[64,24,1024]{2,1,0:T(8,128)(2,1)}), bf16[64,24,1024]{2,1,0:T(8,128)(2,1)S(1)}, u32[]{:S(2)}, u32[]{:S(2)}) async-start(bf16[64,24,1024]{2,1,0:T(8,128)(2,1)} %bitcast.37), calls=%async_computation.3 | async-start | bytes 6291456 | tf_op jit(solution)/shard_map/all_to_all | solution.py:520
  189.5 57.4 %collective-permute-start.9 = (bf16[384,1024]{1,0:T(8,128)(2,1)}, bf16[384,1024]{1,0:T(8,128)(2,1)}, u32[]{:S(2)}, u32[]{:S(2)}) collective-permute-start(bf16[384,1024]{1,0:T(8,128)(2,1)} %copy-done.21), channel_id=1, source_target_pairs={{0,64},{64,0},{1,65},{65,1},{2,66},{66,2},{3,67},{67,3},{4,68},{68... | collective-permute-start | bytes 2359304 | tf_op jit(solution)/shard_map/ppermute | solution.py:506
  229.5 2.2 copy-start.7
  237.0 5.6 %copy-start.4 = (bf16[4,384,1024]{2,1,0:T(8,128)(2,1)}, bf16[4,384,1024]{2,1,0:T(8,128)(2,1)S(1)}, u32[]{:S(2)}) copy-start(bf16[4,384,1024]{2,1,0:T(8,128)(2,1)S(1)} %get-tuple-element.61.x_ref) | copy-start | bytes 9437188
  237.0 5.6 %copy-start.1 = (bf16[1,512,4096]{2,1,0:T(8,128)(2,1)S(1)}, bf16[1,512,4096]{2,1,0:T(8,128)(2,1)}, u32[]{:S(2)}) copy-start(bf16[1,512,4096]{2,1,0:T(8,128)(2,1)} %param.24) | copy-start | bytes 12582916
  237.0 12.7 %collective-permute-start.10 = (bf16[384,256]{1,0:T(8,128)(2,1)S(1)}, bf16[384,256]{1,0:T(8,128)(2,1)S(1)}, u32[]{:S(2)}, u32[]{:S(2)}) collective-permute-start(bf16[384,256]{1,0:T(8,128)(2,1)S(1)} %get-tuple-element.58), channel_id=1, source_target_pairs={{0,64},{64,0},{1,65},{65,1},{2,66},{66,2},{3,67},{67,3},{4,68},{68... | collective-permute-start | bytes 589832 | tf_op jit(solution)/shard_map/ppermute | solution.py:525
  241.5 78.5 %collective-permute-start.11 = (bf16[4096,256]{1,0:T(8,128)(2,1)}, bf16[4096,256]{1,0:T(8,128)(2,1)}, u32[]{:S(2)}, u32[]{:S(2)}) collective-permute-start(bf16[4096,256]{1,0:T(8,128)(2,1)} %up_half.3), channel_id=1, source_target_pairs={{0,64},{64,0},{1,65},{65,1},{2,66},{66,2},{3,67},{67,3},{4,68},{68... | collective-permute-start | bytes 6291464 | tf_op jit(solution)/shard_map/ppermute | solution.py:530
  250.4 75.5 %all-to-all-start.4 = ((bf16[64,24,1024]{2,1,0:T(8,128)(2,1)}), bf16[64,24,1024]{2,1,0:T(8,128)(2,1)S(1)}, u32[]{:S(2)}, u32[]{:S(2)}) async-start(bf16[64,24,1024]{2,1,0:T(8,128)(2,1)} %bitcast.33), calls=%async_computation.4 | async-start | bytes 6291456 | tf_op jit(solution)/shard_map/all_to_all | solution.py:528
  262.3 2.3 copy-start.24
  262.3 2.3 copy-start.28
  (21 other events, 29.5 us)
